TPU v7x, 128 devices: a whole 4x4x4 slice. The times are simulated.
128 devices in a mesh: dp: 4 (over y), ctx: 32 (over x, z, core).
Axes of the slice: x: 4, y: 4, z: 4, core: 2. Of those that a mesh axis runs over, the one named last changes fastest.
Arguments:
- queries: bfloat16 [4, 6144, 8192], P('dp', 'ctx'), may hold values from -7 to 7
- keys: bfloat16 [4, 6144, 512], P('dp', 'ctx'), may hold values from -7 to 7
- values: bfloat16 [4, 6144, 512], P('dp', 'ctx'), may hold values from -6 to 6
- targets: bfloat16 [4, 6144, 8192], P('dp', 'ctx'), may hold values from -6 to 6
- segments: int32 [4, 6144], P('dp', 'ctx'), may hold values from 0 to 3, never falling along the last dimension, each value on 1 to 3072 neighbouring positions
- window: int32 [4], replicated, may hold values from 32 to 64, as said below
- query_feature_projection: bfloat16 [64, 128, 128], replicated, may hold values from -0.35 to 0.35
- key_map: bfloat16 [4, 128, 128], replicated, may hold values from -0.35 to 0.35
Outputs:
- grad_query_map: float32 [64, 128, 128], P('ctx')
- grad_key_map: float32 [4, 128, 128], replicated
Inputs may be any that keep to these rules, and one draw needn't show every extreme that they name: `segments`: document numbers never fall along a sequence; each document has 1 to 3072 positions, and some document exactly 3072. Some head has a window of exactly 64.
All inputs are finite; a program needn't handle non-finite values.
Results may differ from a plain program's by a relative error of at most 0.0006.
Values may be sent and summed in bfloat16 or wider, within the bound.
No kernel may reach another device: no remote copies, remote signals or barrier semaphores. Data moves between devices by JAX's collectives and lax.ppermute only.
A program may use at most 192 MiB of HBM per device.

v0:
```python
import jax
import jax.numpy as jnp
from jax import lax
from jax.sharding import PartitionSpec as P

WINDOW_LIMIT = 64


def from_behind(block, axis, distance):
    devices = range(lax.axis_size(axis))
    route = [(i - distance, i) for i in devices if i - distance in devices]
    return lax.ppermute(block, axis, route)


def entering(value, axis, join, neutral, backward):
    count, mine = (lax.axis_size(axis), lax.axis_index(axis))
    pieces = jax.tree.map(lambda part: lax.all_gather(part, axis), value)
    if backward:
        pieces = jax.tree.map(lambda part: part[::-1], pieces)
        mine = count - 1 - mine
    subtotal = jax.tree.map(
        lambda part, zero: jnp.full_like(part, 0) + jnp.asarray(zero, part.dtype), value, neutral
    )

    def step(position, subtotal):
        longer = join(subtotal, jax.tree.map(lambda part: part[position], pieces))
        return jax.tree.map(lambda new, old: jnp.where(position < mine, new, old), longer, subtotal)

    return lax.fori_loop(0, count - 1, step, subtotal)


def feature_map(logits):
    return jnp.concatenate(
        [jax.nn.softmax(logits, axis=-1), jax.nn.softmax(-logits, axis=-1)], axis=-1
    )


def feature_grad(logits, upstream):
    feature_width = logits.shape[-1]
    upper_probs = jax.nn.softmax(logits, axis=-1)
    lower_probs = jax.nn.softmax(-logits, axis=-1)
    grad_upper = upstream[..., :feature_width]
    grad_lower = upstream[..., feature_width:]
    upper_part = upper_probs * (
        grad_upper - jnp.sum(upper_probs * grad_upper, axis=-1, keepdims=True)
    )
    lower_part = lower_probs * (
        grad_lower - jnp.sum(lower_probs * grad_lower, axis=-1, keepdims=True)
    )
    return upper_part - lower_part


def combine_states(former, latter):
    keep_factor = 1.0 - latter[2]
    return (
        latter[0] + keep_factor * former[0],
        latter[1] + keep_factor * former[1],
        jnp.maximum(former[2], latter[2]),
    )


def on_device(queries, keys, values, targets, segments, window, query_feature_projection, key_map):
    highest = lax.Precision.HIGHEST
    head_count = query_feature_projection.shape[0]
    kv_heads = key_map.shape[0]
    head_dim = query_feature_projection.shape[1]
    map_width = query_feature_projection.shape[2]
    query_group_size = head_count // kv_heads
    tok_rows = queries.shape[1]
    near_rows = tok_rows + WINDOW_LIMIT
    ctx_index = lax.axis_index("ctx")
    offset = ctx_index * tok_rows
    positions = offset + jnp.arange(tok_rows, dtype=jnp.int32)
    near_positions = offset - WINDOW_LIMIT + jnp.arange(near_rows, dtype=jnp.int32)
    row_keys = keys[0]
    row_values = values[0]
    segment_ids = segments[0]
    rim_rows = (
        row_keys[tok_rows - WINDOW_LIMIT :],
        row_values[tok_rows - WINDOW_LIMIT :],
        segment_ids[tok_rows - WINDOW_LIMIT :].astype(jnp.bfloat16),
    )
    rim_keys, rim_values, rim_segments = from_behind(
        (rim_rows[0], rim_rows[1], rim_rows[2]), "ctx", 1
    )
    near_keys = jnp.concatenate([rim_keys, row_keys], 0).reshape(near_rows, kv_heads, head_dim)
    near_values = jnp.concatenate([rim_values, row_values], 0).reshape(
        near_rows, kv_heads, head_dim
    )
    near_segments = jnp.where(
        near_positions >= 0, jnp.concatenate([rim_segments.astype(jnp.int32), segment_ids], 0), -1
    )
    prev_last = near_segments[WINDOW_LIMIT - 1]
    seg_last = segment_ids[tok_rows - 1]
    reset_flag = (prev_last != seg_last).astype(jnp.float32)
    key_logits = jnp.einsum("ngd,gdf->gnf", near_keys, key_map, preferred_element_type=jnp.float32)
    key_features = feature_map(key_logits)
    own_values = near_values[WINDOW_LIMIT:]
    tail_mask = (segment_ids == seg_last).astype(jnp.float32)
    own_features = key_features[:, WINDOW_LIMIT:] * tail_mask[None, :, None]
    block_state = jnp.einsum(
        "gjf,jgd->gfd", own_features, own_values.astype(jnp.float32), precision=highest
    )
    block_norm = jnp.sum(own_features, axis=1)
    identity = (jnp.zeros_like(block_state), jnp.zeros_like(block_norm), jnp.zeros((), jnp.float32))
    prefix_state, prefix_norm, prefix_flag = entering(
        (block_state, block_norm, reset_flag), "ctx", combine_states, identity, False
    )
    head_queries = queries[0].reshape(tok_rows, kv_heads, query_group_size, head_dim)
    query_weight_matrix = query_feature_projection.reshape(
        kv_heads, query_group_size, head_dim, map_width
    )
    query_logits = jnp.einsum(
        "ighd,ghdf->ighf", head_queries, query_weight_matrix, preferred_element_type=jnp.float32
    )
    query_features = feature_map(query_logits)
    scores = jnp.einsum(
        "ighd,jgd->ighj", head_queries, near_keys, preferred_element_type=jnp.float32
    ) * head_dim ** (-0.5)
    same_doc = segment_ids[:, None] == near_segments[None, :]
    distance = positions[:, None] - near_positions[None, :]
    window_reach = window[None, :, None]
    in_window = (
        same_doc[:, None, :] & (distance[:, None, :] >= 0) & (distance[:, None, :] < window_reach)
    )
    own_far = (
        same_doc[:, None, :]
        & (near_positions >= offset)[None, None, :]
        & (distance[:, None, :] >= window_reach)
    )
    rim_near = (
        same_doc[:, None, :]
        & (near_positions < offset)[None, None, :]
        & (distance[:, None, :] < window_reach)
    )
    signed_mask = (own_far.astype(jnp.float32) - rim_near.astype(jnp.float32))[:, :, None, :]
    window_mask = in_window[:, :, None, :]
    window_max = jnp.max(jnp.where(window_mask, scores, -jnp.inf), axis=-1, keepdims=True)
    window_weights = jnp.where(
        window_mask, jnp.exp(jnp.where(window_mask, scores - window_max, 0.0)), 0.0
    )
    linear_weights = (
        jnp.einsum("ighf,gjf->ighj", query_features, key_features, precision=highest) * signed_mask
    )
    carried = (segment_ids == prev_last).astype(jnp.float32)[:, None, None]
    all_weights = window_weights + linear_weights
    near_values_wide = near_values.astype(jnp.float32)
    numerator = jnp.einsum("ighj,jgd->ighd", all_weights, near_values_wide, precision=highest)
    numerator = numerator + carried[..., None] * jnp.einsum(
        "ighf,gfd->ighd", query_features, prefix_state, precision=highest
    )
    denominator = jnp.sum(all_weights, axis=-1) + carried * jnp.einsum(
        "ighf,gf->igh", query_features, prefix_norm, precision=highest
    )
    outputs = numerator / denominator[..., None]
    residual_out = outputs - targets[0].reshape(
        tok_rows, kv_heads, query_group_size, head_dim
    ).astype(jnp.float32)
    grad_numerator = residual_out / denominator[..., None]
    grad_denominator = -jnp.sum(residual_out * outputs, axis=-1) / denominator
    grad_linear = signed_mask * (
        jnp.einsum("ighd,jgd->ighj", grad_numerator, near_values_wide, precision=highest)
        + grad_denominator[..., None]
    )
    grad_query_features = jnp.einsum("ighj,gjf->ighf", grad_linear, key_features, precision=highest)
    carried_terms = (
        jnp.einsum("ighd,gfd->ighf", grad_numerator, prefix_state, precision=highest)
        + grad_denominator[..., None] * prefix_norm[None, :, None, :]
    )
    grad_query_features = grad_query_features + carried[..., None] * carried_terms
    grad_key_features = jnp.einsum("ighj,ighf->gjf", grad_linear, query_features, precision=highest)
    carried_features = query_features * carried[..., None]
    grad_state = jnp.einsum("ighf,ighd->gfd", carried_features, grad_numerator, precision=highest)
    grad_norm = jnp.einsum("ighf,igh->gf", carried_features, grad_denominator, precision=highest)
    later_state, later_norm, later_flag = entering(
        (grad_state, grad_norm, reset_flag), "ctx", combine_states, identity, True
    )
    state_terms = (
        jnp.einsum("gfd,jgd->gjf", later_state, near_values_wide[WINDOW_LIMIT:], precision=highest)
        + later_norm[:, None, :]
    )
    state_terms = state_terms * tail_mask[None, :, None]
    grad_key_features = grad_key_features + jnp.concatenate(
        [jnp.zeros((kv_heads, WINDOW_LIMIT, 2 * map_width), jnp.float32), state_terms], axis=1
    )
    grad_key_logits = feature_grad(key_logits, grad_key_features)
    grad_query_logits = feature_grad(query_logits, grad_query_features)
    key_grad = jnp.einsum(
        "ngd,gnf->gdf", near_keys.astype(jnp.float32), grad_key_logits, precision=highest
    )
    query_grad = jnp.einsum(
        "ighd,ighf->ghdf", head_queries.astype(jnp.float32), grad_query_logits, precision=highest
    )
    query_grad = query_grad.reshape(head_count, head_dim, map_width)
    full_query, full_key = lax.psum((query_grad, key_grad), ("dp", "ctx"))
    head_share = head_count // lax.axis_size("ctx")
    own_query = lax.dynamic_slice_in_dim(full_query, ctx_index * head_share, head_share, 0)
    return (own_query, full_key)


def solution(mesh):
    return jax.shard_map(
        on_device,
        mesh=mesh,
        in_specs=(
            P("dp", "ctx", None),
            P("dp", "ctx", None),
            P("dp", "ctx", None),
            P("dp", "ctx", None),
            P("dp", "ctx"),
            P(),
            P(),
            P(),
        ),
        out_specs=(P("ctx", None, None), P()),
        check_vma=False,
    )
```

profile of v0, /device:TPU:0, one launch (start us, length us, event | category | flops | bytes accessed | tf_op | source)
XLA Modules:
  0.0 811.5 jit_solution(4638825012145083334)
XLA Ops:
  10.2 4.6 collective-permute-start.1
  17.1 1.7 concatenate.38
  20.1 1.9 compare_convert_fusion.1
  22.1 2.0 fusion.118
  27.4 2.5 fusion.95
  31.4 2.5 collective-permute-start.2
  33.9 1.6 copy.44
  35.6 2.9 copy.79
  39.2 3.9 copy.80
  43.8 3.1 fusion.54
  46.9 13.4 %fusion.116 = (f32[192,4,16]{0,2,1:T(8,128)S(1)}, f32[192,4,16,128]{3,0,2,1:T(8,128)S(1)}) fusion(f32[4,16,128,192]{2,3,1,0:T(8,128)S(1)} %fusion.54), kind=kOutput, calls=%fused_computation.158 | output fusion | flops 6291583 | bytes 12632064 | tf_op jit(solution)/shard_map/sub | solution.py:34
  60.3 13.3 %fusion.117 = (f32[192,4,16]{0,2,1:T(8,128)S(1)}, f32[192,4,16,128]{3,0,2,1:T(8,128)S(1)}) fusion(f32[4,16,128,192]{2,3,1,0:T(8,128)S(1)} %fusion.54), kind=kOutput, calls=%fused_computation.159 | output fusion | flops 3145855 | bytes 12632064 | tf_op jit(solution)/shard_map/sub | solution.py:40
  73.7 7.2 broadcast_divide_fusion
  82.9 64.5 %all-reduce.1 = f32[32]{0:T(128)S(1)} all-reduce(f32[32]{0:T(128)S(1)} %dynamic-update-slice), channel_id=1, replica_groups=mesh['dp'=4,'ctx'=32] {'ctx'}, use_global_device_ids=true, to_apply=%add.1 | all-reduce | flops 32 | bytes 256
  148.7 21.2 %all-gather.4 = f32[32,4,256]{2,1,0:T(4,128)S(1)} all-gather(f32[1,4,256]{2,1,0:T(4,128)S(1)} %bitcast.204), channel_id=3, replica_groups=mesh['dp'=4,'ctx'=32] {'ctx'}, dimensions={0}, use_global_device_ids=true | all-gather | bytes 135168 | tf_op jit(solution)/shard_map/all_gather | solution.py:17
  170.7 16.7 %fusion.57 = f32[4,256,192,16]{1,2,3,0:T(8,128)} fusion(f32[192,4,16,128]{3,0,2,1:T(8,128)} %get-tuple-element.359, f32[192,4,16,128]{3,0,2,1:T(8,128)} %get-tuple-element.360, f32[4,256,128]{1,2,0:T(8,128)S(1)} %get-tuple-element.361, f32[4,256,128]{1,2,0:T(8,128)S(1)} %copy-done.7), kind=kOutput, calls=%fused_computation.75 | convolution fusion | flops 9667084288 | bytes 26214400 | tf_op jit(solution)/shard_map/ighf,gjf->ighj/dot_general | solution.py:143
  187.4 8.3 %fusion.52 = f32[4,256,192,16]{1,2,3,0:T(8,128)} fusion(bf16[192,4,16,128]{3,2,1,0:T(8,128)(2,1)S(1)} %bitcast.195, bf16[256,4,128]{2,0,1:T(8,128)(2,1)S(1)} %copy_dynamic-update-slice_fusion), kind=kOutput, calls=%fused_computation.70 | convolution fusion | flops 805306368 | bytes 15990784 | tf_op jit(solution)/shard_map/ighd,jgd->ighj/dot_general | solution.py:117
  195.7 22.1 %fusion.120 = (f32[192,4,16]{0,2,1:T(8,128)S(1)}, f32[192,4,16,256]{3,0,2,1:T(8,128)}) fusion(f32[192,4,256]{2,0,1:T(8,128)S(1)} %convert_subtract_fusion, f32[4,256,192,16]{1,2,3,0:T(8,128)} %fusion.57, f32[4,256,192,16]{1,2,3,0:T(8,128)} %fusion.52, pred[192,4,256]{2,0,1:T(8,128)(4,1)S(1)} %compare_and_fusion), kind=kOutput, calls=%fused_computation.162 | output fusion | flops 28311808 | bytes 38780928 | tf_op jit(solution)/shard_map/sub | solution.py:140
  217.8 10.2 %fusion.93 = f32[4,128,192,16]{1,2,3,0:T(8,128)} fusion(f32[192,4,16,256]{3,0,2,1:T(8,128)} %get-tuple-element.354, bf16[192,4,128]{2,0,1:T(8,128)(2,1)S(1)} %copy-done.11, bf16[64,4,128]{2,0,1:T(8,128)(2,1)S(1)} %copy_bitcast_fusion), kind=kOutput, calls=%fused_computation.120 | convolution fusion | flops 4832362496 | bytes 19136512 | tf_op jit(solution)/shard_map/ighj,jgd->ighd/dot_general | solution.py:148
  228.0 85.5 %while.32 = (s32[]{:T(128)}, f32[4,256,128]{2,1,0:T(8,128)S(1)}, f32[4,256]{1,0:T(4,128)S(1)}, s32[]{:T(128)}, f32[32,4,256,128]{3,2,1,0:T(8,128)}, /*index=5*/f...) while((s32[]{:T(128)}, f32[4,256,128]{2,1,0:T(8,128)S(1)}, ...), condition=%wide.region_11.12_spmd.clone, body=%wide.region_10.11_spmd.clone.sunk | while | flops 528389 | bytes 1585315 | solution.py:29
  313.5 15.2 %fusion.56 = f32[4,1,192,16]{1,2,3,0:T(8,128)} fusion(f32[192,4,16,128]{3,0,2,1:T(8,128)} %get-tuple-element.359, f32[192,4,16,128]{3,0,2,1:T(8,128)} %get-tuple-element.360, f32[4,256,1,1]{1,0,2,3:T(4,128)S(1)} %bitcast.203), kind=kOutput, calls=%fused_computation.74 | convolution fusion | flops 40894464 | bytes 12636160 | tf_op jit(solution)/shard_map/ighf,gf->igh/dot_general | solution.py:152
  328.7 4.8 copy.64
  333.5 21.5 %multiply_reduce_fusion.2 = (f32[192,4,16]{0,2,1:T(8,128)}, f32[192,4,16,128]{3,0,2,1:T(8,128)S(1)}) fusion(f32[192,4,16,128]{3,2,1,0:T(8,128)} %bitcast.199, f32[192,4,16]{0,2,1:T(8,128)S(1)} %bitcast_add_fusion.6, f32[4,128,192,16]{1,2,3,0:T(8,128)} %fusion.93, f32[192,4,16,128]{3,0,2,1:T(8,128)} %get-tuple-element.359, ...), kind=kOutput, calls=%fused_computation.54 | convolution fusion | flops 4845981696 | bytes 32080640 | tf_op jit(solution)/shard_map/ighf,gfd->ighd/dot_general | solution.py:149
  355.0 2.7 copy-done.5
  357.7 23.9 %fusion.70 = f32[4,256,128]{2,1,0:T(8,128)} fusion(f32[192,4,16,128]{3,0,2,1:T(8,128)S(1)} %get-tuple-element.339, f32[192]{0:T(256)S(1)} %get-tuple-element.343, f32[192,4,16,128]{3,0,2,1:T(8,128)} %get-tuple-element.359, f32[192,4,16,128]{3,0,2,1:T(8,128)} %get-tuple-element.360), kind=kOutput, calls=%fused_computation.88 | convolution fusion | flops 4838129664 | bytes 19399424 | tf_op jit(solution)/shard_map/ighf,ighd->gfd/dot_general | solution.py:173
  383.2 10.6 %fusion.17 = f32[4,1,256,1]{2,1,3,0:T(1,128)S(1)} fusion(f32[192]{0:T(256)S(1)} %get-tuple-element.343, f32[192,4,16,128]{3,0,2,1:T(8,128)} %get-tuple-element.359, f32[192,4,16,128]{3,0,2,1:T(8,128)} %get-tuple-element.360, f32[192,4,16,1]{0,2,1,3:T(8,128)S(1)} %bitcast.201), kind=kOutput, calls=%fused_computation.27 | convolution fusion | flops 44040192 | bytes 12636928 | tf_op jit(solution)/shard_map/ighf,igh->gf/dot_general | solution.py:174
  393.8 27.4 %all-gather.5 = f32[32,4,256]{2,1,0:T(4,128)} all-gather(f32[1,4,256]{2,1,0:T(4,128)S(1)} %bitcast.205), channel_id=5, replica_groups=mesh['dp'=4,'ctx'=32] {'ctx'}, dimensions={0}, use_global_device_ids=true | all-gather | bytes 135168 | tf_op jit(solution)/shard_map/all_gather | solution.py:17
  421.2 1.6 reverse
  422.8 10.0 %fusion.92 = f32[4,256,192,16]{1,2,3,0:T(8,128)} fusion(f32[192,4,16,128]{3,0,2,1:T(8,128)} %copy-done.5, bf16[192,4,128]{2,0,1:T(8,128)(2,1)S(1)} %copy-done.11, bf16[64,4,128]{2,0,1:T(8,128)(2,1)S(1)} %copy_bitcast_fusion), kind=kOutput, calls=%fused_computation.119 | convolution fusion | flops 4832362496 | bytes 19136512 | tf_op jit(solution)/shard_map/ighd,jgd->ighj/dot_general | solution.py:162
  432.8 17.6 %fusion.23 = f32[4,256,192,16]{1,2,3,0:T(8,128)} fusion(f32[4,256,192,16]{1,2,3,0:T(8,128)} %fusion.92, f32[192,4,16]{0,2,1:T(8,128)S(1)} %negate_divide_fusion, f32[192,4,256]{2,0,1:T(8,128)S(1)} %convert_subtract_fusion, f32[4,256,128]{1,2,0:T(8,128)S(1)} %get-tuple-element.361, f32[4,256,128]{1,2,0:T(8,128)S(1)} %copy-done.7), kind=kOutput, calls=%fused_computation.32 | convolution fusion | flops 9670230016 | bytes 27049984 | tf_op jit(solution)/shard_map/ighj,gjf->ighf/dot_general | solution.py:165
  450.4 18.8 %fusion.10 = f32[192,4,16,256]{3,0,2,1:T(8,128)} fusion(f32[4,256,192,16]{1,2,3,0:T(8,128)} %fusion.23, f32[4,256]{1,0:T(4,128)S(1)} %get-tuple-element.253, f32[192]{0:T(256)S(1)} %get-tuple-element.343, f32[192,4,16]{0,2,1:T(8,128)S(1)} %negate_divide_fusion, f32[192,4,16,128]{3,0,2,1:T(8,128)} %copy-done.5, f32[4,256,128]{2,1,0:T(8,128)S(1)} %get-tuple-element.252), kind=kOutput, calls=%fused_computation.16 | convolution fusion | flops 4844421120 | bytes 32035584 | tf_op jit(solution)/shard_map/ighd,gfd->ighf/dot_general | solution.py:167
  469.2 8.8 %multiply_reduce_fusion.1 = (f32[192,4,16]{0,2,1:T(8,128)S(1)}, f32[192,4,16]{0,2,1:T(8,128)S(1)}) fusion(f32[192,4,16,128]{3,0,2,1:T(8,128)} %get-tuple-element.360, f32[192,4,16,256]{3,0,2,1:T(8,128)} %fusion.10, f32[192,4,16,128]{3,0,2,1:T(8,128)S(1)} %bitcast.193), kind=kLoop, calls=%fused_computation.49 | loop fusion | flops 6266880 | bytes 25264128 | tf_op jit(solution)/shard_map/reduce_sum | solution.py:45
  478.1 19.4 %fusion.28 = f32[4,16,128,128]{3,2,1,0:T(8,128)} fusion(f32[192,4,16,128]{3,0,2,1:T(8,128)S(1)} %bitcast.193, f32[192,4,16,128]{3,0,2,1:T(8,128)} %get-tuple-element.360, f32[192,4,16,256]{3,0,2,1:T(8,128)} %fusion.10, f32[192,4,16]{0,2,1:T(8,128)S(1)} %get-tuple-element.305, f32[192,4,16]{0,2,1:T(8,128)S(1)} %get-tuple-element.304, ...), kind=kOutput, calls=%fused_computation.42 | convolution fusion | flops 2423783424 | bytes 32604160 | tf_op jit(solution)/shard_map/ighd,ighf->ghdf/dot_general | solution.py:191
  497.5 5.6 copy.52
  503.0 11.5 %rev.9 = f32[32,4,256,128]{3,2,1,0:T(8,128)} reverse(f32[32,4,256,128]{3,2,1,0:T(8,128)} %bitcast.198), dimensions={0} | reverse | bytes 33554432 | tf_op jit(solution)/shard_map/rev | solution.py:19
  514.6 103.4 %while.33 = (s32[]{:T(128)}, f32[4,256,128]{2,1,0:T(8,128)S(1)}, f32[4,256]{1,0:T(4,128)S(1)}, s32[]{:T(128)}, f32[32,4,256,128]{3,2,1,0:T(8,128)}, /*index=5*/f...) while((s32[]{:T(128)}, f32[4,256,128]{2,1,0:T(8,128)S(1)}, ...), condition=%wide.region_18.19_spmd.clone, body=%wide.region_17.18_spmd.clone.sunk | while | flops 528389 | bytes 1585315 | solution.py:29
  515.7 1.5 fusion.144
  519.1 1.5 fusion.144
  529.1 1.5 fusion.144
  532.4 1.5 fusion.144
  535.8 1.5 fusion.144
  539.1 1.5 fusion.144
  542.4 1.5 fusion.144
  545.8 1.5 fusion.144
  618.7 27.2 %fusion.63 = f32[4,256,256]{1,2,0:T(8,128)S(1)} fusion(f32[192,4,16,128]{3,0,2,1:T(8,128)} %get-tuple-element.359, f32[192,4,16,128]{3,0,2,1:T(8,128)} %get-tuple-element.360, f32[4,256,192,16]{1,2,3,0:T(8,128)} %fusion.92, f32[192,4,16]{0,2,1:T(8,128)S(1)} %negate_divide_fusion, f32[192,4,256]{2,0,1:T(8,128)} %copy-done.9, f32[4,192,256]{1,2,0:T(8,128)S(1)} %fusion.62), kind=kOutput, calls=%fused_computation.80 | convolution fusion | flops 9673375744 | bytes 27836416 | tf_op jit(solution)/shard_map/ighj,ighf->gjf/dot_general | solution.py:171
  647.4 154.1 %all-reduce.5.cloned.1.call-done = (f32[64,128,128]{2,1,0:T(8,128)}, f32[4,128,128]{2,1,0:T(8,128)}) async-done(((f32[64,128,128]{2,1,0:T(8,128)}, f32[4,128,128]{2,1,0:T(8,128)}), (f32[64,128,128]{2,1,0:T(8,128)}, f32[4,128,128]{2,1,0:T(8,128)})) %all-reduce.5.cloned.1.call-update) | async-done | bytes 4456464 | tf_op jit(solution)/shard_map/psum | solution.py:195
  801.5 1.6 constant_dynamic-slice_fusion
  803.1 1.7 copy.127
  (271 shorter events, 157.7 us)
Async XLA Ops:
  7.2 36.6 %copy-start = (bf16[64,128,128]{2,1,0:T(8,128)(2,1)S(1)}, bf16[64,128,128]{2,1,0:T(8,128)(2,1)}, u32[]{:S(2)}) copy-start(bf16[64,128,128]{2,1,0:T(8,128)(2,1)} %param.18) | copy-start | bytes 6291460
  7.2 220.8 %all-gather.9.cloned.1.call-start = ((), (), s32[]{:S(2)}) async-start(), calls=%async_computation | async-start | bytes 17301504 | tf_op jit(solution)/shard_map/all_gather | solution.py:17
  8.2 13.8 %collective-permute-start = (bf16[64,512]{1,0:T(8,128)(2,1)S(1)}, bf16[64,512]{1,0:T(8,128)(2,1)S(1)}, u32[]{:S(2)}, u32[]{:S(2)}) collective-permute-start(bf16[64,512]{1,0:T(8,128)(2,1)S(1)} %slice_bitcast_fusion.1), channel_id=1, source_target_pairs={{0,1},{1,2},{2,3},{3,4},{4,5},{5,6},{6,7},{7,8},{8,9},{9,10},{10,1... | collective-permute-start | bytes 196616 | tf_op jit(solution)/shard_map/ppermute | solution.py:12
  10.2 8.6 %collective-permute-start.1 = (bf16[64]{0:T(256)(128)(2,1)S(1)}, bf16[64]{0:T(256)(128)(2,1)S(1)}, u32[]{:S(2)}, u32[]{:S(2)}) collective-permute-start(bf16[64]{0:T(256)(128)(2,1)S(1)} %fusion.110), channel_id=1, source_target_pairs={{0,1},{1,2},{2,3},{3,4},{4,5},{5,6},{6,7},{7,8},{8,9},{9,10},{10,1... | collective-permute-start | bytes 392 | tf_op jit(solution)/shard_map/ppermute | solution.py:12
  19.5 14.4 %copy-start.14 = (s32[256]{0:T(256)}, s32[256]{0:T(256)S(1)}, u32[]{:S(2)}) copy-start(s32[256]{0:T(256)S(1)} %get-tuple-element.357) | copy-start | bytes 3076
  26.5 0.8 copy-start.6
  29.9 473.2 %all-gather.11.cloned.1.call-start = ((), (), s32[]{:S(2)}) async-start(), calls=%async_computation.1 | async-start | bytes 17301504 | tf_op jit(solution)/shard_map/all_gather | solution.py:17
  31.4 138.5 %collective-permute-start.2 = (bf16[64,512]{1,0:T(8,128)(2,1)}, bf16[64,512]{1,0:T(8,128)(2,1)}, u32[]{:S(2)}, u32[]{:S(2)}) collective-permute-start(bf16[64,512]{1,0:T(8,128)(2,1)} %slice_bitcast_fusion), channel_id=1, source_target_pairs={{0,1},{1,2},{2,3},{3,4},{4,5},{5,6},{6,7},{7,8},{8,9},{9,10},{10,1... | collective-permute-start | bytes 196616 | tf_op jit(solution)/shard_map/ppermute | solution.py:12
  35.6 2.9 copy-start.10
  38.5 5.3 copy-start.2
  39.2 3.9 copy-start.19
  73.6 73.7 %copy-start.13 = (s32[1,192]{1,0:T(1,128)S(1)}, s32[1,192]{1,0:T(1,128)}, u32[]{:S(2)}) copy-start(s32[1,192]{1,0:T(1,128)} %param.16) | copy-start | bytes 2308
  73.6 73.7 %copy-start.15 = (s32[256]{0:T(256)S(1)}, s32[256]{0:T(256)}, u32[]{:S(2)}) copy-start(s32[256]{0:T(256)} %copy-done.14) | copy-start | bytes 3076
  73.7 74.0 %copy-start.16 = (s32[4]{0:T(128)S(1)}, s32[4]{0:T(128)}, u32[]{:S(2)}) copy-start(s32[4]{0:T(128)} %param.17) | copy-start | bytes 52
  73.7 74.5 %copy-start.7 = (f32[4,256,128]{1,2,0:T(8,128)S(1)}, f32[4,256,128]{1,2,0:T(8,128)}, u32[]{:S(2)}) copy-start(f32[4,256,128]{1,2,0:T(8,128)} %copy-done.6) | copy-start | bytes 1572868
  148.2 284.6 %copy-start.9 = (f32[192,4,256]{2,0,1:T(8,128)}, f32[192,4,256]{2,0,1:T(8,128)S(1)}, u32[]{:S(2)}) copy-start(f32[192,4,256]{2,0,1:T(8,128)S(1)} %convert_subtract_fusion) | copy-start | bytes 2359300
  170.7 16.7 %copy-start.3 = (bf16[24,8,64,128]{3,2,1,0:T(8,128)(2,1)S(1)}, bf16[24,8,64,128]{3,2,1,0:T(8,128)(2,1)}, u32[]{:S(2)}) copy-start(bf16[24,8,64,128]{3,2,1,0:T(8,128)(2,1)} %copy-done.2) | copy-start | bytes 9437188
  195.7 22.1 %copy-start.11 = (bf16[192,4,128]{2,0,1:T(8,128)(2,1)S(1)}, bf16[192,4,128]{2,0,1:T(8,128)(2,1)}, u32[]{:S(2)}) copy-start(bf16[192,4,128]{2,0,1:T(8,128)(2,1)} %copy.44) | copy-start | bytes 589828
  313.5 15.2 %copy-start.17 = (f32[32]{0:T(128)}, f32[32]{0:T(128)S(1)}, u32[]{:S(2)}) copy-start(f32[32]{0:T(128)S(1)} %get-tuple-element.533) | copy-start | bytes 388
  355.0 2.7 copy-start.5
  357.7 24.0 %copy-start.18 = (f32[32]{0:T(128)S(1)}, f32[32]{0:T(128)}, u32[]{:S(2)}) copy-start(f32[32]{0:T(128)} %copy-done.17) | copy-start | bytes 388
  381.7 419.8 %all-reduce.5.cloned.1.call-start = ((), (), s32[]{:S(2)}) async-start(), calls=%async_computation.2 | async-start | bytes 8912896 | tf_op jit(solution)/shard_map/psum | solution.py:195
  422.8 46.5 %slice-start = ((s8[6291456]{0:T(1024)(128)(4,1)}), s8[4194304]{0:T(1024)(128)(4,1)S(1)}, s32[]{:S(2)}) async-start(s8[6291456]{0:T(1024)(128)(4,1)} %bitcast.192), calls=%async_computation.3 | async-start | bytes 8388608
  432.8 36.4 %slice-start.1 = ((s8[6291456]{0:T(1024)(128)(4,1)}), s8[2097152]{0:T(1024)(128)(4,1)S(1)}, s32[]{:S(2)}) async-start(s8[6291456]{0:T(1024)(128)(4,1)} %bitcast.192), calls=%async_computation.4 | async-start | bytes 4194304
  469.2 8.9 %copy-start.4 = (bf16[24,8,64,128]{3,2,1,0:T(8,128)(2,1)S(1)}, bf16[24,8,64,128]{3,2,1,0:T(8,128)(2,1)}, u32[]{:S(2)}) copy-start(bf16[24,8,64,128]{3,2,1,0:T(8,128)(2,1)} %copy-done.2) | copy-start | bytes 9437188
  503.0 11.5 %copy-start.20 = (f32[32]{0:T(128)S(1)}, f32[32]{0:T(128)}, u32[]{:S(2)}) copy-start(f32[32]{0:T(128)} %rev.10) | copy-start | bytes 388
  514.6 103.4 %copy-start.12 = (bf16[192,4,128]{2,1,0:T(4,128)(2,1)S(1)}, bf16[192,4,128]{2,1,0:T(4,128)(2,1)}, u32[]{:S(2)}) copy-start(bf16[192,4,128]{2,1,0:T(4,128)(2,1)} %concatenate.38) | copy-start | bytes 589828
  618.7 27.2 %copy-start.8 = (f32[4,256,128]{1,2,0:T(8,128)S(1)}, f32[4,256,128]{1,2,0:T(8,128)}, u32[]{:S(2)}) copy-start(f32[4,256,128]{1,2,0:T(8,128)} %copy-done.6) | copy-start | bytes 1572868
  618.7 186.1 %copy-start.1 = (bf16[64,128,128]{2,1,0:T(8,128)(2,1)S(1)}, bf16[64,128,128]{2,1,0:T(8,128)(2,1)}, u32[]{:S(2)}) copy-start(bf16[64,128,128]{2,1,0:T(8,128)(2,1)} %param.18) | copy-start | bytes 6291460
Sparse Core Ops, SparseCore 0:
  30.0 74.7 all-gather.8
  381.8 73.2 all-gather.10
  647.5 153.9 all-reduce.4
where the time goes:
time: 824 us; the launch traced here: 812 us
  matrix products  210 us (25%)
  other arithmetic  186 us (23%)
  waiting for transfers between devices  154 us (19%)
  blocking collectives  113 us (14%)
  local copies, waits for them, and re-layouts  84.8 us (10%)
  loops' own time  38.9 us (5%)
  between operations  15.6 us (2%)
  starting transfers between devices  8.55 us (1%)
    psum x1, waiting for transfers between devices, on_device(): full_query, full_key = lax.psum((query_grad, key_grad), ('dp', 'ctx'))  154 us
    select_n x124, other arithmetic, step(): jnp.where(position < mine, new, old)  114 us
    unnamed x1, blocking collectives  64.5 us
    all_gather x2, blocking collectives, entering(): pieces = jax.tree.map(lambda part: lax.all_gather(part, axis), value)  48.5 us
    another operation x2, loops' own time, entering(): return lax.fori_loop(0, count - 1, step, subtotal)  38.9 us
    dynamic_slice x62, local copies, waits for them, and re-layouts, step(): longer = join(subtotal, jax.tree.map(lambda part: part[position], pieces))  36.1 us
    dot_general x1, matrix products, on_device(): jnp.einsum('ighj,ighf->gjf', grad_linear, query_features, precision=highest)  27.2 us
    dot_general x1, matrix products, on_device(): jnp.einsum('ighf,ighd->gfd', carried_features, grad_numerator, precision=...  23.9 us
  transfers between devices with their start and end apart: 6, of which 1 were waited for; matrix products, arithmetic and copies ran while one was open for 26% of the time, Pallas kernels for 0%

commit v1 on v0

v1 whole, which is shorter than its diff:
```python
import functools
import jax
import jax.numpy as jnp
from jax import lax
from jax.experimental import pallas as pl
from jax.experimental.pallas import tpu as pltpu
from jax.sharding import PartitionSpec as P

CHUNK = 64
QUAD = 4
LANES = QUAD * CHUNK
NEAR = 2 * CHUNK
MASKED = -1e30
F32 = jnp.float32
BF16 = jnp.bfloat16
VMEM_LIMIT = 60 * 1024 * 1024


def halves(x):
    high = x.astype(BF16)
    return high, (x - high.astype(F32)).astype(BF16)


def mm(a, b):
    return jnp.dot(a, b, preferred_element_type=F32)


def mm_nt(a, b):
    return lax.dot_general(a, b, (((1,), (1,)), ((), ())), preferred_element_type=F32)


def softmaxes(logits, axis):
    upper = jnp.exp(logits - jnp.max(logits, axis=axis, keepdims=True))
    lower = jnp.exp(jnp.min(logits, axis=axis, keepdims=True) - logits)
    return (
        upper * (1.0 / jnp.sum(upper, axis=axis, keepdims=True)),
        lower * (1.0 / jnp.sum(lower, axis=axis, keepdims=True)),
    )


def softmax_grads(upper, lower, grad_upper, grad_lower, axis):
    return upper * (
        grad_upper - jnp.sum(upper * grad_upper, axis=axis, keepdims=True)
    ) - lower * (grad_lower - jnp.sum(lower * grad_lower, axis=axis, keepdims=True))


def keep(seg_ref, chunk):
    same = seg_ref[CHUNK * (chunk + 1) - 1] == seg_ref[CHUNK * (chunk + 2) - 1]
    return jnp.where(same, 1.0, 0.0).astype(F32)


def side(first, count, piece):
    return piece[:, first : first + count].reshape(-1, piece.shape[2])


def block_kernel(
    chunks, seg_ref, key_ref, value_ref, map_ref, seg_row_ref, state_ref, piece_ref
):
    upper, lower = softmaxes(mm(key_ref[...], map_ref[0]), 1)
    high, low = halves(jnp.concatenate([upper, lower], 1))
    values = value_ref[...].astype(F32)
    total = None
    for c in range(chunks):
        own = slice(CHUNK * c, CHUNK * (c + 1))
        tail = seg_row_ref[c, :, :CHUNK] == seg_ref[CHUNK * (c + 1) - 1]
        turned = jnp.concatenate([values[own].T, jnp.ones((16, CHUNK), F32)], 0)
        turned = jnp.where(tail, turned, 0.0).astype(BF16)
        state = mm(
            jnp.concatenate([turned, turned], 1), jnp.concatenate([high[own], low[own]], 0)
        )[: state_ref.shape[2]]
        state_ref[0, c] = state
        total = state if c == 0 else state + keep(seg_ref, c - 1) * total
    cut_up(total, seg_ref, piece_ref)


def key_kernel(
    chunks, window_ref, key_ref, value_ref, map_ref, seg_col_ref, seg_row_ref,
    feat_high_ref, feat_low_ref, feat_t_ref, value_t_ref, value_pair_ref, bias_ref, sign_ref,
):
    reach = window_ref[pl.program_id(0)]
    upper, lower = softmaxes(mm(key_ref[...], map_ref[0]), 1)
    features = jnp.concatenate([upper, lower], 1)
    high, low = halves(features)
    feat_high_ref[0] = high
    feat_low_ref[0] = low
    values = value_ref[...]
    value_pair_ref[0] = jnp.concatenate([values, values], 1)
    wide_values = values.astype(F32)
    for c in range(chunks):
        rows = slice(CHUNK * c, CHUNK * c + NEAR)
        turned_high, turned_low = halves(features[rows].T)
        feat_t_ref[0, c] = jnp.concatenate([turned_high, turned_low], 1)
        value_t = wide_values[rows].T.astype(BF16)
        value_t_ref[0, c] = jnp.concatenate([value_t, value_t], 1)
        near_row = lax.broadcasted_iota(jnp.int32, (NEAR, LANES), 0)
        token = lax.broadcasted_iota(jnp.int32, (NEAR, LANES), 1) % CHUNK
        distance = CHUNK + token - near_row
        same_doc = seg_col_ref[rows] == seg_row_ref[c]
        inside = distance < reach
        in_window = same_doc & (distance >= 0) & inside
        bias_ref[0, c] = jnp.where(in_window, 0.0, MASKED).astype(F32)
        far = same_doc & (near_row >= CHUNK) & (distance >= reach)
        rim = same_doc & (near_row < CHUNK) & inside
        sign_ref[0, c] = jnp.where(far, 1.0, jnp.where(rim, -1.0, 0.0)).astype(F32)


def cut_up(total, seg_ref, piece_ref):
    share = piece_ref.shape[1] - 8
    width = total.shape[1]
    end = seg_ref[seg_ref.shape[0] - 1].astype(F32)
    extra = jnp.where(
        lax.broadcasted_iota(jnp.int32, (8, width), 0) == 0, total[128:136], end
    )
    for i in range(piece_ref.shape[0]):
        piece_ref[i, :share] = total[share * i : share * (i + 1)]
        piece_ref[i, share:] = extra


def whole_state(piece):
    share = piece.shape[1] - 8
    state = side(0, share, piece)
    norm = jnp.broadcast_to(piece[0, share : share + 1], (8, piece.shape[2]))
    return jnp.concatenate([state, norm], 0)


def scan_kernel(count, backward, piece_ref, out_ref):
    mark = piece_ref.shape[1] - 7
    total = jnp.zeros(piece_ref.shape[1:], F32)
    for position in range(count - 1, -1, -1) if backward else range(count):
        out_ref[position] = total
        piece = piece_ref[position]
        former = piece_ref[max(position - 1, 0), mark : mark + 1]
        total = piece + jnp.where(piece[mark : mark + 1] == former, total, 0.0)


def place_diagonal(blocks, diag_ref):
    for i, block in enumerate(blocks):
        diag_ref[i * CHUNK : (i + 1) * CHUNK, i * 128 : (i + 1) * 128] = block


def local_kernel(
    chunks, q0_ref, q1_ref, q2_ref, q3_ref, m0_ref, m1_ref, m2_ref, m3_ref, key_ref, high_ref,
    low_ref, value_t_ref, bias_ref, sign_ref, *refs,
):
    numer_ref, denom_ref, qf_high_ref, qf_low_ref, diag_ref = refs[-5:]

    @pl.when(pl.program_id(0) + pl.program_id(1) == 0)
    def _():
        diag_ref[...] = jnp.zeros_like(diag_ref)

    q_refs = (q0_ref, q1_ref, q2_ref, q3_ref)
    maps = jnp.concatenate([ref[0] for ref in (m0_ref, m1_ref, m2_ref, m3_ref)], 0)
    maps = maps.astype(F32).T.astype(BF16)
    every = range(chunks)
    near = [slice(CHUNK * c, CHUNK * c + NEAR) for c in every]
    blocks = [[ref[CHUNK * c : CHUNK * (c + 1)] for ref in q_refs] for c in every]
    for c in every:
        place_diagonal(blocks[c], diag_ref.at[c])
    logits = [mm_nt(maps, diag_ref[c]) for c in every]
    scores = [mm_nt(key_ref[near[c]], jnp.concatenate(blocks[c], 0)) for c in every]
    for c in every:
        upper, lower = softmaxes(logits[c], 0)
        high, low = halves(jnp.concatenate([upper, lower], 0))
        qf_high_ref[0, c] = high
        qf_low_ref[0, c] = low
        score = scores[c] * 128 ** (-0.5) + bias_ref[0, c]
        weights = jnp.exp(score - jnp.max(score, axis=0, keepdims=True))
        key_high = high_ref[0, near[c]]
        both = mm(jnp.concatenate([key_high, low_ref[0, near[c]]], 0), high)
        linear = both[:NEAR] + both[NEAR:] + mm(key_high, low)
        weights = weights + linear * sign_ref[0, c]
        denom_ref[0, c] = jnp.sum(weights, axis=0, keepdims=True)
        numer_ref[0, c] = mm(value_t_ref[0, c], jnp.concatenate(halves(weights), 0))


def enter_states(chunks, seg_ref, first_ref, state_ref, feat_t_ref, rows_ref, columns_ref, norm_ref):
    state = whole_state(first_ref)
    for c in range(chunks):
        if c > 0:
            state = state_ref[0, c - 1] + keep(seg_ref, c - 1) * state
        high, low = halves(jnp.concatenate([state, state[128:]], 0))
        rows_ref[c] = jnp.concatenate([high, low], 0)
        turned_high, turned_low = halves(state[:128].T)
        feat_high, feat_low = feat_t_ref[0, c, :, :NEAR], feat_t_ref[0, c, :, NEAR:]
        columns_ref[0, c] = jnp.concatenate(
            [feat_high, feat_high, turned_high, turned_high, feat_low, turned_low], 1
        )
        norm_ref[0, c] = jnp.broadcast_to(state[128:129], (128, state.shape[1])).T


def output_kernel(
    chunks, seg_ref, t0_ref, t1_ref, t2_ref, t3_ref, numer_ref, denom_ref, qf_high_ref, qf_low_ref,
    first_ref, state_ref, feat_t_ref, value_pair_ref, sign_ref, seg_row_ref, right_ref,
    grad_denom_ref, key_grad_ref, state_grad_ref, piece_ref, columns_ref, norm_ref, rows_ref,
):
    begins = pl.program_id(1) + pl.program_id(2) == 0
    ends = (pl.program_id(1) == 1) & (pl.program_id(2) == pl.num_programs(2) - 1)

    @pl.when(begins)
    def _():
        enter_states(
            chunks, seg_ref, first_ref, state_ref, feat_t_ref, rows_ref, columns_ref, norm_ref
        )

    t_refs = (t0_ref, t1_ref, t2_ref, t3_ref)
    padded = rows_ref.shape[1] // 2
    results = []
    for c in range(chunks):
        carried = jnp.where(seg_row_ref[c] == seg_ref[c * CHUNK + CHUNK - 1], 1.0, 0.0).astype(F32)
        high, low = qf_high_ref[0, c], qf_low_ref[0, c]
        both = mm(rows_ref[c], high)
        carry = both[:padded] + both[padded:] + mm(rows_ref[c, :padded], low)
        carry = carry * carried
        inverse = 1.0 / (denom_ref[0, c] + carry[128:129])
        outputs = (numer_ref[0, c] + carry[:128]) * inverse
        targets = jnp.concatenate([ref[CHUNK * c : CHUNK * (c + 1)] for ref in t_refs], 0)
        residual = outputs - targets.astype(F32).T
        grad = residual * inverse
        grad_denom = -jnp.sum(residual * outputs, axis=0, keepdims=True) * inverse
        grad_denom_ref[0, c] = grad_denom * carried
        grad_high, grad_low = halves(grad)
        near = slice(CHUNK * c, CHUNK * c + NEAR)
        linear = mm(value_pair_ref[0, near], jnp.concatenate([grad_high, grad_low], 0))
        linear_high, linear_low = halves((linear + grad_denom) * sign_ref[0, c])
        mask = carried.astype(BF16)
        grad_high, grad_low = grad_high * mask, grad_low * mask
        right_ref[0, c] = jnp.concatenate([linear_high, linear_low, grad_high, grad_low], 0)
        denom_high, denom_low = halves(jnp.broadcast_to(grad_denom * carried, (16, LANES)))
        left_high = jnp.concatenate([linear_high, grad_high, denom_high], 0)
        left_low = jnp.concatenate([linear_low, grad_low, denom_low], 0)
        both = mm_nt(jnp.concatenate([left_high, left_low], 0), high)
        rows = left_high.shape[0]
        results.append(both[:rows] + both[rows:] + mm_nt(left_high, low))

    @pl.when(begins)
    def _():
        for c in range(chunks):
            key_grad_ref[0, c] = results[c][:NEAR]
            state_grad_ref[0, c] = results[c][NEAR : NEAR + 136]

    @pl.when(jnp.logical_not(begins))
    def _():
        for c in range(chunks):
            key_grad_ref[0, c] += results[c][:NEAR]
            state_grad_ref[0, c] += results[c][NEAR : NEAR + 136]

    @pl.when(ends)
    def _():
        total = state_grad_ref[0, chunks - 1]
        for c in range(chunks - 2, -1, -1):
            total = state_grad_ref[0, c] + keep(seg_ref, c) * total
        cut_up(total, seg_ref, piece_ref)


def query_kernel(
    chunks, core_ref, q0_ref, q1_ref, q2_ref, q3_ref, right_ref, grad_denom_ref, qf_high_ref,
    qf_low_ref, columns_ref, norm_ref, mine_ref, theirs_ref, diag_ref,
):
    @pl.when(pl.program_id(0) + pl.program_id(1) == 0)
    def _():
        diag_ref[...] = jnp.zeros_like(diag_ref)

    q_refs = (q0_ref, q1_ref, q2_ref, q3_ref)
    for c in range(chunks):
        place_diagonal([ref[CHUNK * c : CHUNK * (c + 1)] for ref in q_refs], diag_ref.at[c])
    total = None
    for c in range(chunks):
        stack = right_ref[0, c]
        right = jnp.concatenate([stack, stack[:NEAR], stack[2 * NEAR : 2 * NEAR + 128]], 0)
        norm = jnp.concatenate([norm_ref[0, c]] * (LANES // 128), 1)
        feature_grad = mm(columns_ref[0, c], right) + norm * grad_denom_ref[0, c]
        high, low = qf_high_ref[0, c], qf_low_ref[0, c]
        upper = high[:128].astype(F32) + low[:128].astype(F32)
        lower = high[128:].astype(F32) + low[128:].astype(F32)
        logit_grad = softmax_grads(upper, lower, feature_grad[:128], feature_grad[128:], 0)
        both = mm(jnp.concatenate(halves(logit_grad), 0), diag_ref[c])
        query_grad = both[:128] + both[128:]
        total = query_grad if total is None else total + query_grad

    share = mine_ref.shape[2]
    for core, own in enumerate(((mine_ref, theirs_ref), (theirs_ref, mine_ref))):

        @pl.when(core_ref[0] == core)
        def _(own=own):
            for k in range(mine_ref.shape[0]):
                for i in range(QUAD):
                    own[i % 2][k, i // 2] = total[
                        share * k : share * (k + 1), i * 128 : (i + 1) * 128
                    ]


def tail_kernel(
    chunks, seg_ref, key_ref, value_ref, map_ref, seg_col_ref, later_ref, state_grad_ref,
    key_grad_ref, out_ref,
):
    logits = mm(key_ref[...], map_ref[0])
    upper, lower = softmaxes(logits, 1)
    values = value_ref[...]
    pieces = [key_grad_ref[0, 0, :CHUNK]]
    leaving = whole_state(later_ref)
    states = []
    for c in range(chunks - 1, -1, -1):
        states.append(leaving)
        leaving = state_grad_ref[0, c] + keep(seg_ref, c) * leaving
    states = states[::-1]
    for c in range(chunks):
        own = slice(CHUNK * (c + 1), CHUNK * (c + 2))
        grads = key_grad_ref[0, c, CHUNK:]
        if c + 1 < chunks:
            grads = grads + key_grad_ref[0, c + 1, :CHUNK]
        tail = jnp.where(seg_col_ref[own] == seg_ref[CHUNK * (c + 2) - 1], 1.0, 0.0).astype(F32)
        entry_high, entry_low = halves(states[c][:128])
        through = mm(
            jnp.concatenate([values[own], values[own]], 1),
            jnp.concatenate([entry_high, entry_low], 0),
        )
        pieces.append(grads + tail * (through + states[c][128:129]))
    grads = jnp.concatenate(pieces, 0)
    logit_grad = softmax_grads(upper, lower, grads[:, :128], grads[:, 128:], 1)
    turned = key_ref[...].astype(F32).T.astype(BF16)
    out_ref[0] = mm(
        jnp.concatenate([turned, turned], 1), jnp.concatenate(halves(logit_grad), 0)
    )


def call(
    kernel, name, microseconds, grid, in_specs, out_specs, out_shape, args, scalars=0, scratch=(),
    aliases=None,
):
    return pl.pallas_call(
        kernel,
        grid_spec=pltpu.PrefetchScalarGridSpec(
            num_scalar_prefetch=scalars,
            grid=grid,
            in_specs=in_specs,
            out_specs=out_specs,
            scratch_shapes=scratch,
        ),
        out_shape=out_shape,
        compiler_params=pltpu.CompilerParams(vmem_limit_bytes=VMEM_LIMIT),
        cost_estimate=pl.CostEstimate(
            flops=int(microseconds * 1e9), bytes_accessed=int(microseconds * 3e6), transcendentals=0
        ),
        input_output_aliases=aliases or {},
        name=name,
    )(*args)


def exchange(pieces, axis):
    return lax.all_to_all(pieces, axis, 0, 0, tiled=True)


def on_device(queries, keys, values, targets, segments, window, query_feature_projection, key_map):
    head_count, head_dim, map_width = query_feature_projection.shape
    groups = key_map.shape[0]
    tok_rows = queries.shape[1]
    near_rows = tok_rows + CHUNK
    chunks = tok_rows // CHUNK
    features = 2 * map_width
    quads = head_count // groups // QUAD // 2
    ctx, dp = lax.axis_size("ctx"), lax.axis_size("dp")
    me = lax.axis_index("ctx")
    state_rows = head_dim + 8
    sds = jax.ShapeDtypeStruct

    seg_row = segments[0]
    seg_rows = jnp.tile(seg_row.reshape(chunks, 1, CHUNK), (1, 1, QUAD))
    query_rows, target_rows = queries[0], targets[0]
    group_spec = lambda *shape: pl.BlockSpec((1,) + shape, lambda g, *_: (g,) + (0,) * len(shape))
    whole = lambda shape: pl.BlockSpec(shape, lambda *_: (0,) * len(shape))
    column = lambda rows: pl.BlockSpec((rows, head_dim), lambda g, *_: (0, g))
    per_group = ctx // groups
    piece_shape = (ctx, head_dim // per_group + 8, features)
    piece_spec = pl.BlockSpec((per_group,) + piece_shape[1:], lambda g, *_: (g, 0, 0))

    chunk_state, block_pieces = call(
        functools.partial(block_kernel, chunks), "block", 4, (groups,),
        [
            column(tok_rows), column(tok_rows), group_spec(head_dim, map_width),
            whole((chunks, 1, LANES)),
        ],
        [group_spec(chunks, state_rows, features), piece_spec],
        [sds((groups, chunks, state_rows, features), F32), sds(piece_shape, F32)],
        (seg_row, keys[0], values[0], key_map, seg_rows),
        scalars=1,
    )

    def across(pieces, backward, beside=lambda: ()):
        received, aside = exchange(pieces, "ctx"), beside()
        received, aside = lax.optimization_barrier((received, aside))
        summed = call(
            functools.partial(scan_kernel, ctx, backward), "scan", 2, (1,), [whole(piece_shape)],
            whole(piece_shape), sds(piece_shape, F32), (received,),
        )
        return exchange(summed, "ctx"), aside

    rim = jnp.concatenate([keys[0, -CHUNK:], values[0, -CHUNK:]], 1)
    rim_seg = jnp.broadcast_to(seg_row[-CHUNK:].astype(BF16)[:, None], (CHUNK, 128))
    rim = lax.ppermute(
        jnp.concatenate([rim, rim_seg], 1), "ctx", [(i, i + 1) for i in range(ctx - 1)]
    )
    width = keys.shape[2]
    near_keys = jnp.concatenate([rim[:, :width], keys[0]], 0)
    near_values = jnp.concatenate([rim[:, width : 2 * width], values[0]], 0)
    rim_segments = jnp.where(me > 0, rim[:, 2 * width].astype(jnp.int32), -1)
    near_segments = jnp.concatenate([rim_segments, seg_row], 0)
    seg_col = near_segments[:, None]
    feat_high, feat_low, feat_t, value_t, value_pair, bias, sign = call(
        functools.partial(key_kernel, chunks), "keys", 5, (groups,),
        [
            column(near_rows), column(near_rows), group_spec(head_dim, map_width),
            whole((near_rows, 1)), whole((chunks, 1, LANES)),
        ],
        [
            group_spec(near_rows, features), group_spec(near_rows, features),
            group_spec(chunks, features, 2 * NEAR), group_spec(chunks, head_dim, 2 * NEAR),
            group_spec(near_rows, 2 * head_dim), group_spec(chunks, NEAR, LANES),
            group_spec(chunks, NEAR, LANES),
        ],
        [
            sds((groups, near_rows, features), BF16), sds((groups, near_rows, features), BF16),
            sds((groups, chunks, features, 2 * NEAR), BF16),
            sds((groups, chunks, head_dim, 2 * NEAR), BF16),
            sds((groups, near_rows, 2 * head_dim), BF16),
            sds((groups, chunks, NEAR, LANES), F32), sds((groups, chunks, NEAR, LANES), F32),
        ],
        (window, near_keys, near_values, key_map, seg_col, seg_rows),
        scalars=1,
    )

    half_steps = groups * quads
    steps = 2 * half_steps
    grid = (groups, quads)
    spot = lambda g, q: g * quads + q

    def step_spec(half, *shape):
        return pl.BlockSpec(
            (1,) + shape, lambda g, q, *_: (half * half_steps + spot(g, q),) + (0,) * len(shape)
        )

    def head_specs(half):
        return [
            pl.BlockSpec(
                (tok_rows, head_dim), lambda g, q, *_, i=i: (0, (spot(g, q) * QUAD + i) * 2 + half)
            )
            for i in range(QUAD)
        ]

    def local(half, so_far):
        map_specs = [
            pl.BlockSpec(
                (1, head_dim, map_width),
                lambda g, q, *_, i=i: ((spot(g, q) * QUAD + i) * 2 + half, 0, 0),
            )
            for i in range(QUAD)
        ]
        step = functools.partial(step_spec, half)
        return call(
            functools.partial(local_kernel, chunks), "local", 15, grid,
            head_specs(half) + map_specs
            + [
                column(near_rows), group_spec(near_rows, features),
                group_spec(near_rows, features), group_spec(chunks, head_dim, 2 * NEAR),
                group_spec(chunks, NEAR, LANES), group_spec(chunks, NEAR, LANES),
            ]
            + [pl.BlockSpec(memory_space=pl.ANY)] * len(so_far),
            [
                step(chunks, head_dim, LANES), step(chunks, 1, LANES),
                step(chunks, features, LANES), step(chunks, features, LANES),
            ],
            [
                sds((steps, chunks, head_dim, LANES), F32), sds((steps, chunks, 1, LANES), F32),
                sds((steps, chunks, features, LANES), BF16),
                sds((steps, chunks, features, LANES), BF16),
            ],
            (
                *([query_rows] * QUAD), *([query_feature_projection] * QUAD), near_keys, feat_high,
                feat_low, value_t, bias, sign, *so_far,
            ),
            scratch=[pltpu.VMEM((chunks, LANES, QUAD * head_dim), BF16)],
            aliases={14 + i: i for i in range(len(so_far))},
        )

    entering, forward = across(block_pieces, False, lambda: local(0, ()))
    entering, forward = lax.optimization_barrier((entering, local(1, forward)))

    every_step = lambda *shape: pl.BlockSpec(
        (1,) + shape, lambda g, h, q, *_: (h * half_steps + spot(g, q),) + (0,) * len(shape)
    )
    right, grad_denom, key_grad, state_grad, grad_pieces, columns, norms = call(
        functools.partial(output_kernel, chunks), "outputs", 45, (groups, 2, quads),
        [
            pl.BlockSpec(
                (tok_rows, head_dim),
                lambda g, h, q, *_, i=i: (0, (spot(g, q) * QUAD + i) * 2 + h),
            )
            for i in range(QUAD)
        ]
        + [
            every_step(chunks, head_dim, LANES), every_step(chunks, 1, LANES),
            every_step(chunks, features, LANES), every_step(chunks, features, LANES),
            piece_spec, group_spec(chunks, state_rows, features),
            group_spec(chunks, features, 2 * NEAR), group_spec(near_rows, 2 * head_dim),
            group_spec(chunks, NEAR, LANES), whole((chunks, 1, LANES)),
        ],
        [
            every_step(chunks, 4 * NEAR, LANES), every_step(chunks, 1, LANES),
            group_spec(chunks, NEAR, features), group_spec(chunks, state_rows, features),
            piece_spec, group_spec(chunks, features, 6 * 128), group_spec(chunks, features, 128),
        ],
        [
            sds((steps, chunks, 4 * NEAR, LANES), BF16), sds((steps, chunks, 1, LANES), F32),
            sds((groups, chunks, NEAR, features), F32),
            sds((groups, chunks, state_rows, features), F32), sds(piece_shape, F32),
            sds((groups, chunks, features, 6 * 128), BF16),
            sds((groups, chunks, features, 128), F32),
        ],
        (
            near_segments, *([target_rows] * QUAD), *forward, entering, chunk_state, feat_t,
            value_pair, sign, seg_rows,
        ),
        scalars=1,
        scratch=[pltpu.VMEM((chunks, 2 * (state_rows + 8), features), BF16)],
    )

    core = lax.rem(me, 2)
    partner = [(i, i ^ 1) for i in range(ctx)]

    def query(half):
        share = map_width // dp
        step = functools.partial(step_spec, half)
        shape = (dp, head_count // 4, share, head_dim)
        part = pl.BlockSpec((dp, QUAD // 2, share, head_dim), lambda g, q, *_: (0, spot(g, q), 0, 0))
        mine, theirs = call(
            functools.partial(query_kernel, chunks), "queries", 15, grid,
            head_specs(half)
            + [
                step(chunks, 4 * NEAR, LANES), step(chunks, 1, LANES),
                step(chunks, features, LANES), step(chunks, features, LANES),
                group_spec(chunks, features, 6 * 128), group_spec(chunks, features, 128),
            ],
            [part, part], [sds(shape, F32), sds(shape, F32)],
            (core[None], *([query_rows] * QUAD), right, grad_denom, *forward[2:], columns, norms),
            scalars=1,
            scratch=[pltpu.VMEM((chunks, LANES, QUAD * head_dim), BF16)],
        )
        return (mine + lax.ppermute(theirs, "ctx", partner)).reshape(-1, share, head_dim)

    later, first = across(grad_pieces, True, lambda: query(0))
    later, second = lax.optimization_barrier((later, query(1)))

    key_grad = call(
        functools.partial(tail_kernel, chunks), "tail", 5, (groups,),
        [
            column(near_rows), column(near_rows), group_spec(head_dim, map_width),
            whole((near_rows, 1)), piece_spec, group_spec(chunks, state_rows, features),
            group_spec(chunks, NEAR, features),
        ],
        group_spec(head_dim, map_width), sds((groups, head_dim, map_width), F32),
        (
            near_segments, near_keys, near_values, key_map, seg_col, later, state_grad, key_grad,
        ),
        scalars=1,
    )

    everyone = ("dp", "ctx")
    devices = dp * ctx
    same_core = [[i for i in range(devices) if i % 2 == k] for k in range(2)]

    def summed(pieces):
        received = lax.all_to_all(
            pieces, everyone, 0, 0, tiled=True, axis_index_groups=same_core
        )
        return jnp.sum(received, axis=0)

    first = summed(first)
    key_halves = key_grad.reshape(2, -1, map_width)
    key_mine = lax.dynamic_index_in_dim(key_halves, core, 0, False)
    key_theirs = lax.dynamic_index_in_dim(key_halves, 1 - core, 0, False)
    key_mine = key_mine + lax.ppermute(key_theirs, "ctx", partner)
    rows = second.shape[1]
    second = summed(
        jnp.concatenate([second, key_mine.reshape(devices // 2, -1, map_width)], 1)
    )
    key_share = second[rows:]
    full_key = exchange(jnp.broadcast_to(key_share, (devices,) + key_share.shape), everyone)
    full_key = full_key.reshape(devices // 2, 2, -1, map_width).transpose(1, 0, 2, 3)
    full_key = full_key.reshape(groups, head_dim, map_width)
    own = jnp.stack([first, second[:rows]], 0)
    full_query = lax.all_gather(own, "dp", axis=1, tiled=True)
    return (full_query.transpose(0, 2, 1), full_key)


def solution(mesh):
    return jax.shard_map(
        on_device,
        mesh=mesh,
        in_specs=(
            P("dp", "ctx", None),
            P("dp", "ctx", None),
            P("dp", "ctx", None),
            P("dp", "ctx", None),
            P("dp", "ctx"),
            P(),
            P(),
            P(),
        ),
        out_specs=(P("ctx", None, None), P()),
        check_vma=False,
    )
```

time: 824 us -> 242 us (0.29); the launches traced: 812 us -> 240 us
  matrix products: 210 us -> 0 us
  other arithmetic: 186 us -> 7.36 us
  Pallas kernels: 0 us -> 116 us
  waiting for transfers between devices: 154 us -> 43.6 us
  blocking collectives: 113 us -> 12.4 us
  local copies, waits for them, and re-layouts: 84.8 us -> 8.22 us
  starting transfers between devices: 8.55 us -> 51.5 us
  loops' own time: 38.9 us -> 0 us
  between operations: 15.6 us -> 0.89 us
    dot_general x16 -> x0, matrix products: 207 us -> none  [the longest x1 27.2 us: on_device(): jnp.einsum('ighj,ighf->gjf', grad_linear, query_features, precision=highest)]
    psum x1 -> x0, waiting for transfers between devices: 154 us -> none  [on_device(): full_query, full_key = lax.psum((query_grad, key_grad), ('dp', 'ctx'))]
    pallas_call x0 -> x10, Pallas kernels: none -> 116 us  [call(): pl.pallas_call(kernel, grid_spec=pltpu.PrefetchScalarGridSpec(num_scalar_...]
    select_n x125 -> x1, other arithmetic: 115 us -> 0.11 us  [on_device(): rim_segments = jnp.where(me > 0, rim[:, 2 * width].astype(jnp.int32), -1)]
    unnamed x1 -> x0, blocking collectives: 64.5 us -> none
    all_to_all x0 -> x7, starting transfers between devices: none -> 49.3 us  [the longest x5 37 us: exchange(): return lax.all_to_all(pieces, axis, 0, 0, tiled=True)]
    sub x5 -> x0, other arithmetic: 49.2 us -> none  [the longest x1 22.1 us: on_device(): scores - window_max]
    all_to_all x0 -> x7, waiting for transfers between devices: none -> 42.2 us  [the longest x2 28.6 us: summed(): lax.all_to_all(pieces, everyone, 0, 0, tiled=True, axis_index_groups=same...]
  transfers between devices with their start and end apart: 6 -> 11, of which waited for: 1 -> 4; matrix products, arithmetic and copies ran while one was open for 26% -> 4% of each run, Pallas kernels for 0% -> 27%
where the time goes in v1:
time: 242 us; the launch traced here: 240 us
  Pallas kernels  116 us (48%)
  starting transfers between devices  51.5 us (21%)
  waiting for transfers between devices  43.6 us (18%)
  blocking collectives  12.4 us (5%)
  local copies, waits for them, and re-layouts  8.22 us (3%)
  other arithmetic  7.36 us (3%)
    pallas_call x10, Pallas kernels, call(): pl.pallas_call(kernel, grid_spec=pltpu.PrefetchScalarGridSpec(num_scalar_...  116 us
    all_to_all x5, starting transfers between devices, exchange(): return lax.all_to_all(pieces, axis, 0, 0, tiled=True)  37 us
    all_to_all x2, waiting for transfers between devices, summed(): lax.all_to_all(pieces, everyone, 0, 0, tiled=True, axis_index_groups=same...  28.6 us
    all_to_all x5, waiting for transfers between devices, exchange(): return lax.all_to_all(pieces, axis, 0, 0, tiled=True)  13.6 us
    all_gather x1, blocking collectives, on_device(): full_query = lax.all_gather(own, 'dp', axis=1, tiled=True)  12.4 us
    all_to_all x2, starting transfers between devices, summed(): lax.all_to_all(pieces, everyone, 0, 0, tiled=True, axis_index_groups=same...  12.3 us
  transfers between devices with their start and end apart: 11, of which 4 were waited for; matrix products, arithmetic and copies ran while one was open for 4% of the time, Pallas kernels for 27%

profile of v1, /device:TPU:0, one launch (start us, length us, event | category | flops | bytes accessed | tf_op | source)
XLA Modules:
  0.0 239.6 jit_solution(9326815836734522730)
XLA Ops:
  0.6 0.7 fusion
  1.3 0.9 slice_bitcast_fusion
  2.3 1.3 collective-permute-start
  3.6 0.5 broadcast.12
  4.1 1.3 reduce.5
  5.4 0.1 tile.10
  5.5 0.7 tile.12.seg_row_ref
  6.2 5.4 %block.1 = (f32[4,3,136,256]{3,2,1,0:T(8,128)}, f32[32,24,256]{2,1,0:T(8,128)}) custom-call(s32[192]{0:T(256)} %bitcast.42, bf16[192,512]{1,0:T(8,128)(2,1)} %bitcast.33, bf16[192,512]{1,0:T(8,128)(2,1)} %bitcast.35, bf16[4,128,128]{2,1,0:T(8,128)(2,1)} %map_ref.5, s32[3,1,256]{2,1,0:T(1,128)} %tile.12.seg_row_ref), custom_call_target="tpu_custom_call" | custom-call | flops 4000000000 | bytes 12000000 | tf_op jit(solution)/shard_map/block/pallas_call | solution.py:330
  11.6 10.2 %all-to-all-start = ((f32[32,24,256]{2,1,0:T(8,128)}), f32[32,24,256]{2,1,0:T(8,128)S(1)}, u32[]{:S(2)}, u32[]{:S(2)}) async-start(f32[32,24,256]{2,1,0:T(8,128)} %get-tuple-element.44), calls=%async_computation | async-start | bytes 1572864 | tf_op jit(solution)/shard_map/all_to_all | solution.py:350
  21.8 0.1 select_reduce_fusion
  22.0 0.8 copy.22.seg_col_ref
  22.8 0.7 pad_maximum_fusion.1.key_ref
  23.5 0.7 pad_maximum_fusion.2.value_ref
  24.2 6.0 %keys.1 = (bf16[4,256,256]{2,1,0:T(8,128)(2,1)}, bf16[4,256,256]{2,1,0:T(8,128)(2,1)}, bf16[4,3,256,256]{3,2,1,0:T(8,128)(2,1)}, bf16[4,3,128,256]{3,2,1,0:T(8,1...) custom-call(s32[4]{0:T(128)} %window_ref.1, ...), custom_call_target="tpu_custom_call" | custom-call | flops 5000000000 | bytes 15000000 | tf_op jit(solution)/shard_map/keys/pallas_call | solution.py:330
  30.2 14.9 %local.2 = (f32[16,3,128,256]{3,2,1,0:T(8,128)}, f32[16,3,1,256]{3,2,1,0:T(1,128)}, bf16[16,3,256,256]{3,2,1,0:T(8,128)(2,1)}, bf16[16,3,256,256]{3,2,1,0:T(8,128)(2,1)}) custom-call(bf16[192,8192]{1,0:T(8,128)(2,1)} %bitcast.48, bf16[192,8192]{1,0:T(8,128)(2,1)} %bitcast.49, bf16[192,8192]{1,0:T(8,128)(2,1)} %bitcast.50, bf16[192,8192]{1,0:T(8,128)(2,1)} %bitcast.51, ...), custom_call_target="tpu_custom_call" | custom-call | flops 15000000512 | bytes 45000000 | tf_op jit(solution)/shard_map/local/pallas_call | solution.py:330
  45.1 0.9 copy-done.2
  46.0 2.1 scan.2
  48.2 7.4 %all-to-all-start.1 = ((f32[32,24,256]{2,1,0:T(8,128)}), f32[32,24,256]{2,1,0:T(8,128)S(1)}, u32[]{:S(2)}, u32[]{:S(2)}) async-start(f32[32,24,256]{2,1,0:T(8,128)} %scan.2), calls=%async_computation.1 | async-start | bytes 1572864 | tf_op jit(solution)/shard_map/all_to_all | solution.py:350
  55.5 15.0 %local.3 = (f32[16,3,128,256]{3,2,1,0:T(8,128)}, f32[16,3,1,256]{3,2,1,0:T(1,128)}, bf16[16,3,256,256]{3,2,1,0:T(8,128)(2,1)}, bf16[16,3,256,256]{3,2,1,0:T(8,128)(2,1)}) custom-call(bf16[192,8192]{1,0:T(8,128)(2,1)} %bitcast.52, bf16[192,8192]{1,0:T(8,128)(2,1)} %bitcast.53, ...), custom_call_target="tpu_custom_call", output_to_operand_aliasing={{0}: (14, {}), {1}: (15, {}), {2}: (16, {}), {3}: (17, {})} | custom-call | flops 15000000512 | bytes 45000000 | tf_op jit(solution)/shard_map/local/pallas_call | solution.py:330
  70.5 0.9 copy-done.3
  71.4 34.3 %outputs.1 = (bf16[16,3,512,256]{3,2,1,0:T(8,128)(2,1)}, f32[16,3,1,256]{3,2,1,0:T(1,128)}, f32[4,3,128,256]{3,2,1,0:T(8,128)}, f32[4,3,136,256]{3,2,1,0:T(8,128...) custom-call(s32[256]{0:T(256)} %copy-done.6, bf16[192,8192]{1,0:T(8,128)(2,1)} %bitcast.44, ...), custom_call_target="tpu_custom_call" | custom-call | flops 44999999488 | bytes 135000000 | tf_op jit(solution)/shard_map/outputs/pallas_call | solution.py:330
  105.8 14.9 %queries.2 = (f32[4,16,32,128]{3,2,1,0:T(8,128)}, f32[4,16,32,128]{3,2,1,0:T(8,128)}) custom-call(s32[1]{0:T(128)} %bitcast.9.core_ref, bf16[192,8192]{1,0:T(8,128)(2,1)} %bitcast.56, bf16[192,8192]{1,0:T(8,128)(2,1)} %bitcast.57, bf16[192,8192]{1,0:T(8,128)(2,1)} %bitcast.58, bf16[192,8192]{1,0:T(8,128)(2,1)} %bitcast.59, ...), custom_call_target="tpu_custom_call" | custom-call | flops 15000000512 | bytes 45000000 | tf_op jit(solution)/shard_map/queries/pallas_call | solution.py:330
  120.7 0.4 collective-permute-start.1
  121.1 7.4 %all-to-all-start.2 = ((f32[32,24,256]{2,1,0:T(8,128)}), f32[32,24,256]{2,1,0:T(8,128)}, u32[]{:S(2)}, u32[]{:S(2)}) async-start(f32[32,24,256]{2,1,0:T(8,128)} %get-tuple-element.71), calls=%async_computation.2 | async-start | bytes 1572864 | tf_op jit(solution)/shard_map/all_to_all | solution.py:350
  128.4 15.0 %queries.3 = (f32[4,16,32,128]{3,2,1,0:T(8,128)}, f32[4,16,32,128]{3,2,1,0:T(8,128)}) custom-call(s32[1]{0:T(128)} %bitcast.9.core_ref, bf16[192,8192]{1,0:T(8,128)(2,1)} %bitcast.60, bf16[192,8192]{1,0:T(8,128)(2,1)} %bitcast.61, bf16[192,8192]{1,0:T(8,128)(2,1)} %bitcast.62, bf16[192,8192]{1,0:T(8,128)(2,1)} %bitcast.63, ...), custom_call_target="tpu_custom_call" | custom-call | flops 15000000512 | bytes 45000000 | tf_op jit(solution)/shard_map/queries/pallas_call | solution.py:330
  143.4 0.3 collective-permute-start.2
  143.8 1.2 add.17
  145.0 2.1 scan.3
  147.1 7.5 %all-to-all-start.4 = ((f32[32,24,256]{2,1,0:T(8,128)}), f32[32,24,256]{2,1,0:T(8,128)}, u32[]{:S(2)}, u32[]{:S(2)}) async-start(f32[32,24,256]{2,1,0:T(8,128)} %scan.3), calls=%async_computation.4 | async-start | bytes 1572864 | tf_op jit(solution)/shard_map/all_to_all | solution.py:350
  154.6 0.2 add.18
  154.8 13.6 %all-to-all-done.4.later_ref = f32[32,24,256]{2,1,0:T(8,128)} async-done(((f32[32,24,256]{2,1,0:T(8,128)}), f32[32,24,256]{2,1,0:T(8,128)}, u32[]{:S(2)}, u32[]{:S(2)}) %all-to-all-start.4) | async-done | bytes 786464 | tf_op jit(solution)/shard_map/all_to_all | solution.py:350
  168.4 7.6 %all-to-all-start.3 = ((f32[64,32,128]{2,1,0:T(8,128)}), f32[64,32,128]{2,1,0:T(8,128)S(1)}, u32[]{:S(2)}, u32[]{:S(2)}) async-start(f32[64,32,128]{2,1,0:T(8,128)} %bitcast.10), calls=%async_computation.3 | async-start | bytes 2097152 | tf_op jit(solution)/shard_map/all_to_all | solution.py:571
  176.1 6.1 %tail.1 = f32[4,128,128]{2,1,0:T(8,128)} custom-call(s32[256]{0:T(256)} %copy-done.6, bf16[256,512]{1,0:T(8,128)(2,1)} %pad_maximum_fusion.1.key_ref, bf16[256,512]{1,0:T(8,128)(2,1)} %pad_maximum_fusion.2.value_ref, bf16[4,128,128]{2,1,0:T(8,128)(2,1)} %map_ref.5, s32[256,1]{1,0:T(8,128)} %copy.22.seg_col_ref, f32[32,24,256]{2,1,0:T(8,128)} %all-to-all-done.4.later_ref, ...), custom_call_target="tpu_custom_call" | custom-call | flops 5000000000 | bytes 15000000 | tf_op jit(solution)/shard_map/tail/pallas_call | solution.py:330
  182.2 0.9 dynamic-slice_bitcast_fusion
  183.1 0.1 collective-permute-start.3
  183.2 1.3 collective-permute-done.3
  184.5 0.9 bitcast_add_fusion
  185.4 1.2 pad_maximum_fusion
  186.6 8.3 %all-to-all-done.3 = f32[64,32,128]{2,1,0:T(8,128)S(1)} async-done(((f32[64,32,128]{2,1,0:T(8,128)}), f32[64,32,128]{2,1,0:T(8,128)S(1)}, u32[]{:S(2)}, u32[]{:S(2)}) %all-to-all-start.3) | async-done | bytes 1048608 | tf_op jit(solution)/shard_map/all_to_all | solution.py:571
  194.9 4.7 %all-to-all-start.5 = ((f32[64,36,128]{2,1,0:T(8,128)}), f32[64,36,128]{2,1,0:T(8,128)S(1)}, u32[]{:S(2)}, u32[]{:S(2)}) async-start(f32[64,36,128]{2,1,0:T(8,128)} %pad_maximum_fusion), calls=%async_computation.5 | async-start | bytes 2621440 | tf_op jit(solution)/shard_map/all_to_all | solution.py:571
  199.6 0.1 reduce_sum.18
  199.7 20.3 %all-to-all-done.5 = f32[64,36,128]{2,1,0:T(8,128)S(1)} async-done(((f32[64,36,128]{2,1,0:T(8,128)}), f32[64,36,128]{2,1,0:T(8,128)S(1)}, u32[]{:S(2)}, u32[]{:S(2)}) %all-to-all-start.5) | async-done | bytes 1179680 | tf_op jit(solution)/shard_map/all_to_all | solution.py:571
  220.0 0.1 reduce_sum.19
  220.2 0.7 broadcast_in_dim.24
  220.9 4.6 %all-to-all-start.6 = ((f32[128,4,128]{2,1,0:T(4,128)}), f32[128,4,128]{2,1,0:T(4,128)S(1)}, u32[]{:S(2)}, u32[]{:S(2)}) async-start(f32[128,4,128]{2,1,0:T(4,128)} %broadcast_in_dim.24), calls=%async_computation.6 | async-start | bytes 524288 | tf_op jit(solution)/shard_map/all_to_all | solution.py:350
  225.6 12.4 %all_gather.3 = f32[2,128,128]{2,0,1:T(2,128)S(1)} all-gather(f32[2,32,128]{2,0,1:T(2,128)S(1)} %copy.24), channel_id=1, replica_groups=mesh['dp'=4,'ctx'=32] {'dp'}, dimensions={1}, use_global_device_ids=true | all-gather | bytes 163840 | tf_op jit(solution)/shard_map/all_gather | solution.py:590
  237.9 0.8 copy.27
  238.7 0.9 copy.26
  (31 shorter events, 0.3 us)
Async XLA Ops:
  2.3 19.5 %collective-permute-start = (bf16[64,1152]{1,0:T(8,128)(2,1)S(1)}, bf16[64,1152]{1,0:T(8,128)(2,1)S(1)}, u32[]{:S(2)}, u32[]{:S(2)}) collective-permute-start(bf16[64,1152]{1,0:T(8,128)(2,1)S(1)} %pad_maximum_fusion.3), channel_id=1, source_target_pairs={{0,1},{1,2},{2,3},{3,4},{4,5},{5,6},{6,7},{7,8},{8,9},{9,10},{10,1... | collective-permute-start | bytes 442376 | tf_op jit(solution)/shard_map/ppermute | solution.py:399
  6.2 15.7 %copy-start.7 = (s32[1,192]{1,0:T(1,128)S(1)}, s32[1,192]{1,0:T(1,128)}, u32[]{:S(2)}) copy-start(s32[1,192]{1,0:T(1,128)} %param.12) | copy-start | bytes 2308
  11.6 11.2 %copy-start.4 = (bf16[1,192,512]{2,1,0:T(8,128)(2,1)S(1)}, bf16[1,192,512]{2,1,0:T(8,128)(2,1)}, u32[]{:S(2)}) copy-start(bf16[1,192,512]{2,1,0:T(8,128)(2,1)} %param.9) | copy-start | bytes 589828
  11.6 12.0 %copy-start.5 = (bf16[1,192,512]{2,1,0:T(8,128)(2,1)S(1)}, bf16[1,192,512]{2,1,0:T(8,128)(2,1)}, u32[]{:S(2)}) copy-start(bf16[1,192,512]{2,1,0:T(8,128)(2,1)} %param.10) | copy-start | bytes 589828
  11.6 33.6 %all-to-all-start = ((f32[32,24,256]{2,1,0:T(8,128)}), f32[32,24,256]{2,1,0:T(8,128)S(1)}, u32[]{:S(2)}, u32[]{:S(2)}) async-start(f32[32,24,256]{2,1,0:T(8,128)} %get-tuple-element.44), calls=%async_computation | async-start | bytes 1572864 | tf_op jit(solution)/shard_map/all_to_all | solution.py:350
  22.0 8.2 %copy-start.6 = (s32[256]{0:T(256)}, s32[256]{0:T(256)S(1)}, u32[]{:S(2)}) copy-start(s32[256]{0:T(256)S(1)} %pad_add_fusion.seg_ref) | copy-start | bytes 3076
  45.1 0.9 copy-start.2
  48.2 22.3 %all-to-all-start.1 = ((f32[32,24,256]{2,1,0:T(8,128)}), f32[32,24,256]{2,1,0:T(8,128)S(1)}, u32[]{:S(2)}, u32[]{:S(2)}) async-start(f32[32,24,256]{2,1,0:T(8,128)} %scan.2), calls=%async_computation.1 | async-start | bytes 1572864 | tf_op jit(solution)/shard_map/all_to_all | solution.py:350
  70.5 0.9 copy-start.3
  120.7 23.1 %collective-permute-start.1 = (f32[4,16,32,128]{3,2,1,0:T(8,128)}, f32[4,16,32,128]{3,2,1,0:T(8,128)S(1)}, u32[]{:S(2)}, u32[]{:S(2)}) collective-permute-start(f32[4,16,32,128]{3,2,1,0:T(8,128)} %get-tuple-element.77), channel_id=1, source_target_pairs={{0,1},{1,0},{2,3},{3,2},{4,5},{5,4},{6,7},{7,6},{8,9},{9,8},{10,11... | collective-permute-start | bytes 3145736 | tf_op jit(solution)/shard_map/ppermute | solution.py:547
  121.1 23.9 %all-to-all-start.2 = ((f32[32,24,256]{2,1,0:T(8,128)}), f32[32,24,256]{2,1,0:T(8,128)}, u32[]{:S(2)}, u32[]{:S(2)}) async-start(f32[32,24,256]{2,1,0:T(8,128)} %get-tuple-element.71), calls=%async_computation.2 | async-start | bytes 1572864 | tf_op jit(solution)/shard_map/all_to_all | solution.py:350
  128.4 15.3 %copy-start.1 = (f32[4,16,32,128]{3,2,1,0:T(8,128)S(1)}, f32[4,16,32,128]{3,2,1,0:T(8,128)}, u32[]{:S(2)}) copy-start(f32[4,16,32,128]{3,2,1,0:T(8,128)} %get-tuple-element.76) | copy-start | bytes 3145732
  143.4 11.2 %collective-permute-start.2 = (f32[4,16,32,128]{3,2,1,0:T(8,128)}, f32[4,16,32,128]{3,2,1,0:T(8,128)S(1)}, u32[]{:S(2)}, u32[]{:S(2)}) collective-permute-start(f32[4,16,32,128]{3,2,1,0:T(8,128)} %get-tuple-element.81), channel_id=1, source_target_pairs={{0,1},{1,0},{2,3},{3,2},{4,5},{5,4},{6,7},{7,6},{8,9},{9,8},{10,11... | collective-permute-start | bytes 3145736 | tf_op jit(solution)/shard_map/ppermute | solution.py:547
  147.1 7.5 %copy-start = (f32[4,16,32,128]{3,2,1,0:T(8,128)S(1)}, f32[4,16,32,128]{3,2,1,0:T(8,128)}, u32[]{:S(2)}) copy-start(f32[4,16,32,128]{3,2,1,0:T(8,128)} %get-tuple-element.80) | copy-start | bytes 3145732
  147.1 21.3 %all-to-all-start.4 = ((f32[32,24,256]{2,1,0:T(8,128)}), f32[32,24,256]{2,1,0:T(8,128)}, u32[]{:S(2)}, u32[]{:S(2)}) async-start(f32[32,24,256]{2,1,0:T(8,128)} %scan.3), calls=%async_computation.4 | async-start | bytes 1572864 | tf_op jit(solution)/shard_map/all_to_all | solution.py:350
  168.4 26.5 %all-to-all-start.3 = ((f32[64,32,128]{2,1,0:T(8,128)}), f32[64,32,128]{2,1,0:T(8,128)S(1)}, u32[]{:S(2)}, u32[]{:S(2)}) async-start(f32[64,32,128]{2,1,0:T(8,128)} %bitcast.10), calls=%async_computation.3 | async-start | bytes 2097152 | tf_op jit(solution)/shard_map/all_to_all | solution.py:571
  183.1 1.4 collective-permute-start.3
  194.9 25.1 %all-to-all-start.5 = ((f32[64,36,128]{2,1,0:T(8,128)}), f32[64,36,128]{2,1,0:T(8,128)S(1)}, u32[]{:S(2)}, u32[]{:S(2)}) async-start(f32[64,36,128]{2,1,0:T(8,128)} %pad_maximum_fusion), calls=%async_computation.5 | async-start | bytes 2621440 | tf_op jit(solution)/shard_map/all_to_all | solution.py:571
  220.9 17.8 %all-to-all-start.6 = ((f32[128,4,128]{2,1,0:T(4,128)}), f32[128,4,128]{2,1,0:T(4,128)S(1)}, u32[]{:S(2)}, u32[]{:S(2)}) async-start(f32[128,4,128]{2,1,0:T(4,128)} %broadcast_in_dim.24), calls=%async_computation.6 | async-start | bytes 524288 | tf_op jit(solution)/shard_map/all_to_all | solution.py:350

commit v2 on v1

--- a/solution.py
+++ b/solution.py
@@ -11,8 +11,10 @@
 LANES = QUAD * CHUNK
 NEAR = 2 * CHUNK
 MASKED = -1e30
+OWN_FAR, OWN_NEAR, RIM_NEAR = 1.0, 2.0, 3.0
 F32 = jnp.float32
 BF16 = jnp.bfloat16
+RING = 4
 VMEM_LIMIT = 60 * 1024 * 1024
 
 
@@ -75,7 +77,7 @@
 
 def key_kernel(
     chunks, window_ref, key_ref, value_ref, map_ref, seg_col_ref, seg_row_ref,
-    feat_high_ref, feat_low_ref, feat_t_ref, value_t_ref, value_pair_ref, bias_ref, sign_ref,
+    feat_high_ref, feat_low_ref, feat_t_ref, value_t_ref, value_pair_ref, kind_ref,
 ):
     reach = window_ref[pl.program_id(0)]
     upper, lower = softmaxes(mm(key_ref[...], map_ref[0]), 1)
@@ -92,16 +94,23 @@
         feat_t_ref[0, c] = jnp.concatenate([turned_high, turned_low], 1)
         value_t = wide_values[rows].T.astype(BF16)
         value_t_ref[0, c] = jnp.concatenate([value_t, value_t], 1)
-        near_row = lax.broadcasted_iota(jnp.int32, (NEAR, LANES), 0)
-        token = lax.broadcasted_iota(jnp.int32, (NEAR, LANES), 1) % CHUNK
+        near_row = lax.broadcasted_iota(jnp.int32, (NEAR, 128), 0)
+        token = lax.broadcasted_iota(jnp.int32, (NEAR, 128), 1) % CHUNK
         distance = CHUNK + token - near_row
-        same_doc = seg_col_ref[rows] == seg_row_ref[c]
+        same_doc = seg_col_ref[rows] == seg_row_ref[c, :, :128]
         inside = distance < reach
-        in_window = same_doc & (distance >= 0) & inside
-        bias_ref[0, c] = jnp.where(in_window, 0.0, MASKED).astype(F32)
-        far = same_doc & (near_row >= CHUNK) & (distance >= reach)
-        rim = same_doc & (near_row < CHUNK) & inside
-        sign_ref[0, c] = jnp.where(far, 1.0, jnp.where(rim, -1.0, 0.0)).astype(F32)
+        own = near_row >= CHUNK
+        kind = jnp.where(inside, jnp.where(own, OWN_NEAR, RIM_NEAR), jnp.where(own, OWN_FAR, 0.0))
+        kind_ref[0, c] = jnp.where(same_doc & (distance >= 0), kind, 0.0).astype(BF16)
+
+
+def kinds(kind_ref, c):
+    kind = kind_ref[0, c].astype(F32)
+    return jnp.concatenate([kind] * (LANES // 128), 1)
+
+
+def signed(kind, linear):
+    return jnp.where(kind == OWN_FAR, linear, jnp.where(kind == RIM_NEAR, -linear, 0.0))
 
 
 def cut_up(total, seg_ref, piece_ref):
@@ -140,7 +149,7 @@
 
 def local_kernel(
     chunks, q0_ref, q1_ref, q2_ref, q3_ref, m0_ref, m1_ref, m2_ref, m3_ref, key_ref, high_ref,
-    low_ref, value_t_ref, bias_ref, sign_ref, *refs,
+    low_ref, value_t_ref, kind_ref, *refs,
 ):
     numer_ref, denom_ref, qf_high_ref, qf_low_ref, diag_ref = refs[-5:]
 
@@ -158,39 +167,37 @@
         place_diagonal(blocks[c], diag_ref.at[c])
     logits = [mm_nt(maps, diag_ref[c]) for c in every]
     scores = [mm_nt(key_ref[near[c]], jnp.concatenate(blocks[c], 0)) for c in every]
+    cuts = [halves(jnp.concatenate(softmaxes(logits[c], 0), 0)) for c in every]
+    both = [
+        mm(jnp.concatenate([high_ref[0, near[c]], low_ref[0, near[c]]], 0), cuts[c][0])
+        for c in every
+    ]
+    third = [mm(high_ref[0, near[c]], cuts[c][1]) for c in every]
     for c in every:
-        upper, lower = softmaxes(logits[c], 0)
-        high, low = halves(jnp.concatenate([upper, lower], 0))
-        qf_high_ref[0, c] = high
-        qf_low_ref[0, c] = low
-        score = scores[c] * 128 ** (-0.5) + bias_ref[0, c]
+        qf_high_ref[0, c], qf_low_ref[0, c] = cuts[c]
+        kind = kinds(kind_ref, c)
+        score = jnp.where(kind >= OWN_NEAR, scores[c] * 128 ** (-0.5), MASKED)
         weights = jnp.exp(score - jnp.max(score, axis=0, keepdims=True))
-        key_high = high_ref[0, near[c]]
-        both = mm(jnp.concatenate([key_high, low_ref[0, near[c]]], 0), high)
-        linear = both[:NEAR] + both[NEAR:] + mm(key_high, low)
-        weights = weights + linear * sign_ref[0, c]
+        linear = both[c][:NEAR] + both[c][NEAR:] + third[c]
+        weights = weights + signed(kind, linear)
         denom_ref[0, c] = jnp.sum(weights, axis=0, keepdims=True)
         numer_ref[0, c] = mm(value_t_ref[0, c], jnp.concatenate(halves(weights), 0))
 
 
-def enter_states(chunks, seg_ref, first_ref, state_ref, feat_t_ref, rows_ref, columns_ref, norm_ref):
+def enter_states(chunks, seg_ref, first_ref, state_ref, rows_ref, columns_ref, norm_ref):
     state = whole_state(first_ref)
     for c in range(chunks):
         if c > 0:
             state = state_ref[0, c - 1] + keep(seg_ref, c - 1) * state
         high, low = halves(jnp.concatenate([state, state[128:]], 0))
         rows_ref[c] = jnp.concatenate([high, low], 0)
-        turned_high, turned_low = halves(state[:128].T)
-        feat_high, feat_low = feat_t_ref[0, c, :, :NEAR], feat_t_ref[0, c, :, NEAR:]
-        columns_ref[0, c] = jnp.concatenate(
-            [feat_high, feat_high, turned_high, turned_high, feat_low, turned_low], 1
-        )
-        norm_ref[0, c] = jnp.broadcast_to(state[128:129], (128, state.shape[1])).T
+        columns_ref[0, c] = jnp.concatenate(halves(state[:128].T), 1)
+        norm_ref[0, c] = state[128:]
 
 
 def output_kernel(
     chunks, seg_ref, t0_ref, t1_ref, t2_ref, t3_ref, numer_ref, denom_ref, qf_high_ref, qf_low_ref,
-    first_ref, state_ref, feat_t_ref, value_pair_ref, sign_ref, seg_row_ref, right_ref,
+    first_ref, state_ref, value_pair_ref, kind_ref, seg_row_ref, right_ref,
     grad_denom_ref, key_grad_ref, state_grad_ref, piece_ref, columns_ref, norm_ref, rows_ref,
 ):
     begins = pl.program_id(1) + pl.program_id(2) == 0
@@ -198,39 +205,51 @@
 
     @pl.when(begins)
     def _():
-        enter_states(
-            chunks, seg_ref, first_ref, state_ref, feat_t_ref, rows_ref, columns_ref, norm_ref
-        )
+        enter_states(chunks, seg_ref, first_ref, state_ref, rows_ref, columns_ref, norm_ref)
 
     t_refs = (t0_ref, t1_ref, t2_ref, t3_ref)
     padded = rows_ref.shape[1] // 2
-    results = []
-    for c in range(chunks):
-        carried = jnp.where(seg_row_ref[c] == seg_ref[c * CHUNK + CHUNK - 1], 1.0, 0.0).astype(F32)
-        high, low = qf_high_ref[0, c], qf_low_ref[0, c]
-        both = mm(rows_ref[c], high)
-        carry = both[:padded] + both[padded:] + mm(rows_ref[c, :padded], low)
-        carry = carry * carried
+    every = range(chunks)
+    carried = [
+        jnp.where(seg_row_ref[c] == seg_ref[c * CHUNK + CHUNK - 1], 1.0, 0.0).astype(F32)
+        for c in every
+    ]
+    both = [mm(rows_ref[c], qf_high_ref[0, c]) for c in every]
+    third = [mm(rows_ref[c, :padded], qf_low_ref[0, c]) for c in every]
+    cuts, grad_denoms = [], []
+    for c in every:
+        carry = (both[c][:padded] + both[c][padded:] + third[c]) * carried[c]
         inverse = 1.0 / (denom_ref[0, c] + carry[128:129])
         outputs = (numer_ref[0, c] + carry[:128]) * inverse
         targets = jnp.concatenate([ref[CHUNK * c : CHUNK * (c + 1)] for ref in t_refs], 0)
         residual = outputs - targets.astype(F32).T
-        grad = residual * inverse
         grad_denom = -jnp.sum(residual * outputs, axis=0, keepdims=True) * inverse
-        grad_denom_ref[0, c] = grad_denom * carried
-        grad_high, grad_low = halves(grad)
-        near = slice(CHUNK * c, CHUNK * c + NEAR)
-        linear = mm(value_pair_ref[0, near], jnp.concatenate([grad_high, grad_low], 0))
-        linear_high, linear_low = halves((linear + grad_denom) * sign_ref[0, c])
-        mask = carried.astype(BF16)
-        grad_high, grad_low = grad_high * mask, grad_low * mask
+        grad_denom_ref[0, c] = grad_denom * carried[c]
+        grad_denoms.append(grad_denom)
+        cuts.append(halves(residual * inverse))
+    linear = [
+        mm(value_pair_ref[0, CHUNK * c : CHUNK * c + NEAR], jnp.concatenate(cuts[c], 0))
+        for c in every
+    ]
+    left_high, left_low = [], []
+    for c in every:
+        linear_high, linear_low = halves(
+            signed(kinds(kind_ref, c), linear[c] + grad_denoms[c])
+        )
+        mask = carried[c].astype(BF16)
+        grad_high, grad_low = cuts[c][0] * mask, cuts[c][1] * mask
         right_ref[0, c] = jnp.concatenate([linear_high, linear_low, grad_high, grad_low], 0)
-        denom_high, denom_low = halves(jnp.broadcast_to(grad_denom * carried, (16, LANES)))
-        left_high = jnp.concatenate([linear_high, grad_high, denom_high], 0)
-        left_low = jnp.concatenate([linear_low, grad_low, denom_low], 0)
-        both = mm_nt(jnp.concatenate([left_high, left_low], 0), high)
-        rows = left_high.shape[0]
-        results.append(both[:rows] + both[rows:] + mm_nt(left_high, low))
+        denom_high, denom_low = halves(
+            jnp.broadcast_to(grad_denoms[c] * carried[c], (16, LANES))
+        )
+        left_high.append(jnp.concatenate([linear_high, grad_high, denom_high], 0))
+        left_low.append(jnp.concatenate([linear_low, grad_low, denom_low], 0))
+    both = [
+        mm_nt(jnp.concatenate([left_high[c], left_low[c]], 0), qf_high_ref[0, c]) for c in every
+    ]
+    third = [mm_nt(left_high[c], qf_low_ref[0, c]) for c in every]
+    rows = NEAR + padded
+    results = [both[c][:rows] + both[c][rows:] + third[c] for c in every]
 
     @pl.when(begins)
     def _():
@@ -254,39 +273,53 @@
 
 def query_kernel(
     chunks, core_ref, q0_ref, q1_ref, q2_ref, q3_ref, right_ref, grad_denom_ref, qf_high_ref,
-    qf_low_ref, columns_ref, norm_ref, mine_ref, theirs_ref, diag_ref,
+    qf_low_ref, feat_t_ref, columns_ref, norm_ref, *refs,
 ):
+    mine_ref, theirs_ref, diag_ref, left_ref, spread_ref = refs[-5:]
+
     @pl.when(pl.program_id(0) + pl.program_id(1) == 0)
     def _():
         diag_ref[...] = jnp.zeros_like(diag_ref)
 
+    @pl.when(pl.program_id(1) == 0)
+    def _():
+        for c in range(chunks):
+            feat_high, feat_low = feat_t_ref[0, c, :, :NEAR], feat_t_ref[0, c, :, NEAR:]
+            state_high, state_low = columns_ref[0, c, :, :128], columns_ref[0, c, :, 128:]
+            left_ref[c] = jnp.concatenate(
+                [feat_high, feat_high, state_high, state_high, feat_low, state_low], 1
+            )
+            norm = jnp.broadcast_to(norm_ref[0, c, :1], (128, norm_ref.shape[3]))
+            spread_ref[c] = norm.T
+
     q_refs = (q0_ref, q1_ref, q2_ref, q3_ref)
-    for c in range(chunks):
+    every = range(chunks)
+    for c in every:
         place_diagonal([ref[CHUNK * c : CHUNK * (c + 1)] for ref in q_refs], diag_ref.at[c])
-    total = None
-    for c in range(chunks):
+    feature_grads = []
+    for c in every:
         stack = right_ref[0, c]
         right = jnp.concatenate([stack, stack[:NEAR], stack[2 * NEAR : 2 * NEAR + 128]], 0)
-        norm = jnp.concatenate([norm_ref[0, c]] * (LANES // 128), 1)
-        feature_grad = mm(columns_ref[0, c], right) + norm * grad_denom_ref[0, c]
+        feature_grads.append(mm(left_ref[c], right))
+    cuts = []
+    for c in every:
+        norm = jnp.concatenate([spread_ref[c]] * (LANES // 128), 1)
+        feature_grad = feature_grads[c] + norm * grad_denom_ref[0, c]
         high, low = qf_high_ref[0, c], qf_low_ref[0, c]
         upper = high[:128].astype(F32) + low[:128].astype(F32)
         lower = high[128:].astype(F32) + low[128:].astype(F32)
-        logit_grad = softmax_grads(upper, lower, feature_grad[:128], feature_grad[128:], 0)
-        both = mm(jnp.concatenate(halves(logit_grad), 0), diag_ref[c])
-        query_grad = both[:128] + both[128:]
-        total = query_grad if total is None else total + query_grad
-
-    share = mine_ref.shape[2]
+        cuts.append(
+            halves(softmax_grads(upper, lower, feature_grad[:128], feature_grad[128:], 0))
+        )
+    both = [mm(jnp.concatenate(cuts[c], 0), diag_ref[c]) for c in every]
+    total = sum(x[:128] + x[128:] for x in both)
+
     for core, own in enumerate(((mine_ref, theirs_ref), (theirs_ref, mine_ref))):
 
         @pl.when(core_ref[0] == core)
         def _(own=own):
-            for k in range(mine_ref.shape[0]):
-                for i in range(QUAD):
-                    own[i % 2][k, i // 2] = total[
-                        share * k : share * (k + 1), i * 128 : (i + 1) * 128
-                    ]
+            for i in range(QUAD):
+                own[i % 2][i // 2] = total[:, i * 128 : (i + 1) * 128]
 
 
 def tail_kernel(
@@ -385,14 +418,14 @@
         scalars=1,
     )
 
-    def across(pieces, backward, beside=lambda: ()):
-        received, aside = exchange(pieces, "ctx"), beside()
-        received, aside = lax.optimization_barrier((received, aside))
+    def across(pieces, backward, first, second):
+        received, aside = lax.optimization_barrier((exchange(pieces, "ctx"), first()))
         summed = call(
             functools.partial(scan_kernel, ctx, backward), "scan", 2, (1,), [whole(piece_shape)],
             whole(piece_shape), sds(piece_shape, F32), (received,),
         )
-        return exchange(summed, "ctx"), aside
+        summed, aside = lax.optimization_barrier((summed, aside))
+        return lax.optimization_barrier((exchange(summed, "ctx"), second(aside)))
 
     rim = jnp.concatenate([keys[0, -CHUNK:], values[0, -CHUNK:]], 1)
     rim_seg = jnp.broadcast_to(seg_row[-CHUNK:].astype(BF16)[:, None], (CHUNK, 128))
@@ -405,7 +438,7 @@
     rim_segments = jnp.where(me > 0, rim[:, 2 * width].astype(jnp.int32), -1)
     near_segments = jnp.concatenate([rim_segments, seg_row], 0)
     seg_col = near_segments[:, None]
-    feat_high, feat_low, feat_t, value_t, value_pair, bias, sign = call(
+    feat_high, feat_low, feat_t, value_t, value_pair, kind = call(
         functools.partial(key_kernel, chunks), "keys", 5, (groups,),
         [
             column(near_rows), column(near_rows), group_spec(head_dim, map_width),
@@ -414,15 +447,14 @@
         [
             group_spec(near_rows, features), group_spec(near_rows, features),
             group_spec(chunks, features, 2 * NEAR), group_spec(chunks, head_dim, 2 * NEAR),
-            group_spec(near_rows, 2 * head_dim), group_spec(chunks, NEAR, LANES),
-            group_spec(chunks, NEAR, LANES),
+            group_spec(near_rows, 2 * head_dim), group_spec(chunks, NEAR, 128),
         ],
         [
             sds((groups, near_rows, features), BF16), sds((groups, near_rows, features), BF16),
             sds((groups, chunks, features, 2 * NEAR), BF16),
             sds((groups, chunks, head_dim, 2 * NEAR), BF16),
             sds((groups, near_rows, 2 * head_dim), BF16),
-            sds((groups, chunks, NEAR, LANES), F32), sds((groups, chunks, NEAR, LANES), F32),
+            sds((groups, chunks, NEAR, 128), BF16),
         ],
         (window, near_keys, near_values, key_map, seg_col, seg_rows),
         scalars=1,
@@ -461,7 +493,7 @@
             + [
                 column(near_rows), group_spec(near_rows, features),
                 group_spec(near_rows, features), group_spec(chunks, head_dim, 2 * NEAR),
-                group_spec(chunks, NEAR, LANES), group_spec(chunks, NEAR, LANES),
+                group_spec(chunks, NEAR, 128),
             ]
             + [pl.BlockSpec(memory_space=pl.ANY)] * len(so_far),
             [
@@ -475,14 +507,15 @@
             ],
             (
                 *([query_rows] * QUAD), *([query_feature_projection] * QUAD), near_keys, feat_high,
-                feat_low, value_t, bias, sign, *so_far,
+                feat_low, value_t, kind, *so_far,
             ),
             scratch=[pltpu.VMEM((chunks, LANES, QUAD * head_dim), BF16)],
-            aliases={14 + i: i for i in range(len(so_far))},
-        )
-
-    entering, forward = across(block_pieces, False, lambda: local(0, ()))
-    entering, forward = lax.optimization_barrier((entering, local(1, forward)))
+            aliases={13 + i: i for i in range(len(so_far))},
+        )
+
+    entering, forward = across(
+        block_pieces, False, lambda: local(0, ()), lambda so_far: local(1, so_far)
+    )
 
     every_step = lambda *shape: pl.BlockSpec(
         (1,) + shape, lambda g, h, q, *_: (h * half_steps + spot(g, q),) + (0,) * len(shape)
@@ -500,24 +533,24 @@
             every_step(chunks, head_dim, LANES), every_step(chunks, 1, LANES),
             every_step(chunks, features, LANES), every_step(chunks, features, LANES),
             piece_spec, group_spec(chunks, state_rows, features),
-            group_spec(chunks, features, 2 * NEAR), group_spec(near_rows, 2 * head_dim),
-            group_spec(chunks, NEAR, LANES), whole((chunks, 1, LANES)),
+            group_spec(near_rows, 2 * head_dim), group_spec(chunks, NEAR, 128),
+            whole((chunks, 1, LANES)),
         ],
         [
             every_step(chunks, 4 * NEAR, LANES), every_step(chunks, 1, LANES),
             group_spec(chunks, NEAR, features), group_spec(chunks, state_rows, features),
-            piece_spec, group_spec(chunks, features, 6 * 128), group_spec(chunks, features, 128),
+            piece_spec, group_spec(chunks, features, 2 * head_dim), group_spec(chunks, 8, features),
         ],
         [
             sds((steps, chunks, 4 * NEAR, LANES), BF16), sds((steps, chunks, 1, LANES), F32),
             sds((groups, chunks, NEAR, features), F32),
             sds((groups, chunks, state_rows, features), F32), sds(piece_shape, F32),
-            sds((groups, chunks, features, 6 * 128), BF16),
-            sds((groups, chunks, features, 128), F32),
+            sds((groups, chunks, features, 2 * head_dim), BF16),
+            sds((groups, chunks, 8, features), F32),
         ],
         (
-            near_segments, *([target_rows] * QUAD), *forward, entering, chunk_state, feat_t,
-            value_pair, sign, seg_rows,
+            near_segments, *([target_rows] * QUAD), *forward, entering, chunk_state, value_pair,
+            kind, seg_rows,
         ),
         scalars=1,
         scratch=[pltpu.VMEM((chunks, 2 * (state_rows + 8), features), BF16)],
@@ -526,28 +559,68 @@
     core = lax.rem(me, 2)
     partner = [(i, i ^ 1) for i in range(ctx)]
 
-    def query(half):
-        share = map_width // dp
+    def query(half, right, start, count, so_far=()):
+        part = pl.BlockSpec(
+            (QUAD // 2, map_width, head_dim), lambda g, q, *_: (spot(g + start, q), 0, 0)
+        )
+        shape = sds((head_count // 4, map_width, head_dim), F32)
+        from_start = lambda spec: pl.BlockSpec(
+            spec.block_shape, lambda g, q, *_: spec.index_map(g + start, q)
+        )
         step = functools.partial(step_spec, half)
-        shape = (dp, head_count // 4, share, head_dim)
-        part = pl.BlockSpec((dp, QUAD // 2, share, head_dim), lambda g, q, *_: (0, spot(g, q), 0, 0))
-        mine, theirs = call(
-            functools.partial(query_kernel, chunks), "queries", 15, grid,
-            head_specs(half)
-            + [
-                step(chunks, 4 * NEAR, LANES), step(chunks, 1, LANES),
-                step(chunks, features, LANES), step(chunks, features, LANES),
-                group_spec(chunks, features, 6 * 128), group_spec(chunks, features, 128),
+        specs = head_specs(half) + [
+            step(chunks, 4 * NEAR, LANES), step(chunks, 1, LANES), step(chunks, features, LANES),
+            step(chunks, features, LANES), group_spec(chunks, features, 2 * NEAR),
+            group_spec(chunks, features, 2 * head_dim), group_spec(chunks, 8, features),
+        ]
+        return call(
+            functools.partial(query_kernel, chunks), "queries", 10 * count // groups,
+            (count, quads),
+            [from_start(spec) for spec in specs]
+            + [pl.BlockSpec(memory_space=pl.ANY)] * len(so_far),
+            [part, part], [shape, shape],
+            (
+                core[None], *([query_rows] * QUAD), right, grad_denom, *forward[2:], feat_t,
+                columns, norms, *so_far,
+            ),
+            scalars=1,
+            scratch=[
+                pltpu.VMEM((chunks, LANES, QUAD * head_dim), BF16),
+                pltpu.VMEM((chunks, features, 6 * 128), BF16),
+                pltpu.VMEM((chunks, features, 128), F32),
             ],
-            [part, part], [sds(shape, F32), sds(shape, F32)],
-            (core[None], *([query_rows] * QUAD), right, grad_denom, *forward[2:], columns, norms),
-            scalars=1,
-            scratch=[pltpu.VMEM((chunks, LANES, QUAD * head_dim), BF16)],
-        )
-        return (mine + lax.ppermute(theirs, "ctx", partner)).reshape(-1, share, head_dim)
-
-    later, first = across(grad_pieces, True, lambda: query(0))
-    later, second = lax.optimization_barrier((later, query(1)))
+            aliases={12 + i: i for i in range(len(so_far))},
+        )
+
+    same_core = [[i for i in range(ctx) if i % 2 == k] for k in range(2)]
+
+    def around(axis, value):
+        if axis == "dp":
+            routes = [[(i, (i + s) % dp) for i in range(dp)] for s in range(1, RING)]
+        else:
+            stride = 2 if axis == "z" else 2 * RING
+            at = lambda i, s: i + ((i // stride + s) % RING - i // stride % RING) * stride
+            routes = [[(i, at(i, s)) for i in range(ctx)] for s in range(1, RING)]
+            axis = "ctx"
+        one, two, three = (lax.ppermute(value, axis, route) for route in routes)
+        return (value + two) + (one + three)
+
+    def over_cores(mine, theirs):
+        return mine + lax.ppermute(theirs, "ctx", partner)
+
+    def over_chips(pieces):
+        received = lax.all_to_all(pieces, "ctx", 0, 0, tiled=True, axis_index_groups=same_core)
+        return jnp.sum(received.reshape(ctx // 2, -1, map_width, head_dim), axis=0)
+
+    def second_half(done):
+        first, right = lax.optimization_barrier((over_cores(*done[0]), done[1]))
+        return first, query(1, right, 0, groups)
+
+    later, (first, second) = across(
+        grad_pieces, True, lambda: (query(0, right, 0, groups), right), second_half
+    )
+    second = over_cores(*second)
+    later, first, second = lax.optimization_barrier((later, first, second))
 
     key_grad = call(
         functools.partial(tail_kernel, chunks), "tail", 5, (groups,),
@@ -563,32 +636,17 @@
         scalars=1,
     )
 
-    everyone = ("dp", "ctx")
-    devices = dp * ctx
-    same_core = [[i for i in range(devices) if i % 2 == k] for k in range(2)]
-
-    def summed(pieces):
-        received = lax.all_to_all(
-            pieces, everyone, 0, 0, tiled=True, axis_index_groups=same_core
-        )
-        return jnp.sum(received, axis=0)
-
-    first = summed(first)
     key_halves = key_grad.reshape(2, -1, map_width)
     key_mine = lax.dynamic_index_in_dim(key_halves, core, 0, False)
     key_theirs = lax.dynamic_index_in_dim(key_halves, 1 - core, 0, False)
-    key_mine = key_mine + lax.ppermute(key_theirs, "ctx", partner)
-    rows = second.shape[1]
-    second = summed(
-        jnp.concatenate([second, key_mine.reshape(devices // 2, -1, map_width)], 1)
-    )
-    key_share = second[rows:]
-    full_key = exchange(jnp.broadcast_to(key_share, (devices,) + key_share.shape), everyone)
-    full_key = full_key.reshape(devices // 2, 2, -1, map_width).transpose(1, 0, 2, 3)
-    full_key = full_key.reshape(groups, head_dim, map_width)
-    own = jnp.stack([first, second[:rows]], 0)
-    full_query = lax.all_gather(own, "dp", axis=1, tiled=True)
-    return (full_query.transpose(0, 2, 1), full_key)
+    key_mine = over_cores(key_mine, key_theirs)
+    key_mine = around("dp", around("x", around("z", key_mine)))
+    key_theirs = lax.ppermute(key_mine, "ctx", partner)
+    full_key = jnp.concatenate(
+        [jnp.where(core == 0, key_mine, key_theirs), jnp.where(core == 0, key_theirs, key_mine)], 0
+    )
+    full_query = around("dp", over_chips(jnp.stack([first, second], 1)))
+    return (full_query.transpose(0, 2, 1), full_key.reshape(groups, head_dim, map_width))
 
 
 def solution(mesh):

time: 242 us -> 219 us (0.905)
  Pallas kernels: 116 us -> 101 us
  blocking collectives: 12.4 us -> 0 us
  starting transfers between devices: 51.5 us -> 58.8 us
  waiting for transfers between devices: 43.6 us -> 39.8 us
    ppermute x3 -> x16, waiting for transfers between devices: 1.33 us -> 37.5 us  [the longest x12 33.6 us: around(): one, two, three = (lax.ppermute(value, axis, route) for route in routes)]
    all_to_all x2 -> x1, waiting for transfers between devices: 28.6 us -> 0.01 us  [over_chips(): lax.all_to_all(pieces, 'ctx', 0, 0, tiled=True, axis_index_groups=same_core)]
    ppermute x3 -> x16, starting transfers between devices: 0.81 us -> 20.8 us  [the longest x12 19.3 us: around(): one, two, three = (lax.ppermute(value, axis, route) for route in routes)]
    pallas_call x10, Pallas kernels: 116 us -> 101 us  [call(): pl.pallas_call(kernel, grid_spec=pltpu.PrefetchScalarGridSpec(num_scalar_...]
    all_gather x1 -> x0, blocking collectives: 12.4 us -> none  [on_device(): full_query = lax.all_gather(own, 'dp', axis=1, tiled=True)]
    all_to_all x5 -> x4, waiting for transfers between devices: 13.6 us -> 2.28 us  [exchange(): return lax.all_to_all(pieces, axis, 0, 0, tiled=True)]
    all_to_all x5 -> x4, starting transfers between devices: 37 us -> 30 us  [exchange(): return lax.all_to_all(pieces, axis, 0, 0, tiled=True)]
    all_to_all x2 -> x1, starting transfers between devices: 12.3 us -> 6.69 us  [over_chips(): lax.all_to_all(pieces, 'ctx', 0, 0, tiled=True, axis_index_groups=same_core)]
  transfers between devices with their start and end apart: 11 -> 22, of which waited for: 4 -> 16; matrix products, arithmetic and copies ran while one was open for 4% -> 4% of each run, Pallas kernels for 27% -> 32%
where the time goes in v2:
time: 219 us; the launch traced here: 217 us
  Pallas kernels  101 us (46%)
  starting transfers between devices  58.8 us (27%)
  waiting for transfers between devices  39.8 us (18%)
  local copies, waits for them, and re-layouts  8.91 us (4%)
  other arithmetic  7.21 us (3%)
    pallas_call x10, Pallas kernels, call(): pl.pallas_call(kernel, grid_spec=pltpu.PrefetchScalarGridSpec(num_scalar_...  101 us
    ppermute x12, waiting for transfers between devices, around(): one, two, three = (lax.ppermute(value, axis, route) for route in routes)  33.6 us
    all_to_all x4, starting transfers between devices, exchange(): return lax.all_to_all(pieces, axis, 0, 0, tiled=True)  30 us
    ppermute x12, starting transfers between devices, around(): one, two, three = (lax.ppermute(value, axis, route) for route in routes)  19.3 us
    all_to_all x1, starting transfers between devices, over_chips(): lax.all_to_all(pieces, 'ctx', 0, 0, tiled=True, axis_index_groups=same_core)  6.69 us
  transfers between devices with their start and end apart: 22, of which 16 were waited for; matrix products, arithmetic and copies ran while one was open for 4% of the time, Pallas kernels for 32%

profile of v2, /device:TPU:0, one launch (start us, length us, event | category | flops | bytes accessed | tf_op | source)
XLA Modules:
  0.0 217.0 jit_solution(16118182118635373792)
XLA Ops:
  1.3 0.9 slice_bitcast_fusion
  2.3 1.3 collective-permute-start
  4.1 1.3 reduce.5
  6.2 5.4 %block.1 = (f32[4,3,136,256]{3,2,1,0:T(8,128)}, f32[32,24,256]{2,1,0:T(8,128)}) custom-call(s32[192]{0:T(256)} %bitcast.49, bf16[192,512]{1,0:T(8,128)(2,1)} %bitcast.41, bf16[192,512]{1,0:T(8,128)(2,1)} %bitcast.43, bf16[4,128,128]{2,1,0:T(8,128)(2,1)} %map_ref.5, s32[3,1,256]{2,1,0:T(1,128)} %tile.12.seg_row_ref), custom_call_target="tpu_custom_call" | custom-call | flops 4000000000 | bytes 12000000 | tf_op jit(solution)/shard_map/block/pallas_call | solution.py:363
  11.6 10.2 %all-to-all-start = ((f32[32,24,256]{2,1,0:T(8,128)}), f32[32,24,256]{2,1,0:T(8,128)S(1)}, u32[]{:S(2)}, u32[]{:S(2)}) async-start(f32[32,24,256]{2,1,0:T(8,128)} %get-tuple-element.61), calls=%async_computation | async-start | bytes 1572864 | tf_op jit(solution)/shard_map/all_to_all | solution.py:383
  24.3 5.5 %keys.1 = (bf16[4,256,256]{2,1,0:T(8,128)(2,1)}, bf16[4,256,256]{2,1,0:T(8,128)(2,1)}, bf16[4,3,256,256]{3,2,1,0:T(8,128)(2,1)}, bf16[4,3,128,256]{3,2,1,0:T(8,1...) custom-call(s32[4]{0:T(128)} %window_ref.1, bf16[256,512]{1,0:T(8,128)(2,1)} %pad_maximum_fusion.1.key_ref, ...), custom_call_target="tpu_custom_call" | custom-call | flops 5000000000 | bytes 15000000 | tf_op jit(solution)/shard_map/keys/pallas_call | solution.py:363
  29.8 12.5 %local.2 = (f32[16,3,128,256]{3,2,1,0:T(8,128)}, f32[16,3,1,256]{3,2,1,0:T(1,128)}, bf16[16,3,256,256]{3,2,1,0:T(8,128)(2,1)}, bf16[16,3,256,256]{3,2,1,0:T(8,128)(2,1)}) custom-call(bf16[192,8192]{1,0:T(8,128)(2,1)} %bitcast.23, bf16[192,8192]{1,0:T(8,128)(2,1)} %bitcast.24, bf16[192,8192]{1,0:T(8,128)(2,1)} %bitcast.25, bf16[192,8192]{1,0:T(8,128)(2,1)} %bitcast.26, ...), custom_call_target="tpu_custom_call" | custom-call | flops 15000000512 | bytes 45000000 | tf_op jit(solution)/shard_map/local/pallas_call | solution.py:363
  42.4 0.9 copy-done.1
  43.3 2.1 scan.2
  45.4 7.4 %all-to-all-start.1 = ((f32[32,24,256]{2,1,0:T(8,128)}), f32[32,24,256]{2,1,0:T(8,128)S(1)}, u32[]{:S(2)}, u32[]{:S(2)}) async-start(f32[32,24,256]{2,1,0:T(8,128)} %scan.2), calls=%async_computation.1 | async-start | bytes 1572864 | tf_op jit(solution)/shard_map/all_to_all | solution.py:383
  52.8 12.0 %local.3 = (f32[16,3,128,256]{3,2,1,0:T(8,128)}, f32[16,3,1,256]{3,2,1,0:T(1,128)}, bf16[16,3,256,256]{3,2,1,0:T(8,128)(2,1)}, bf16[16,3,256,256]{3,2,1,0:T(8,128)(2,1)}) custom-call(bf16[192,8192]{1,0:T(8,128)(2,1)} %bitcast.27, bf16[192,8192]{1,0:T(8,128)(2,1)} %bitcast.28, ...), custom_call_target="tpu_custom_call", output_to_operand_aliasing={{0}: (13, {}), {1}: (14, {}), {2}: (15, {}), {3}: (16, {})} | custom-call | flops 15000000512 | bytes 45000000 | tf_op jit(solution)/shard_map/local/pallas_call | solution.py:363
  64.8 1.8 all-to-all-done.1.first_ref
  66.6 0.9 copy-done.2
  67.5 28.5 %outputs.1 = (bf16[16,3,512,256]{3,2,1,0:T(8,128)(2,1)}, f32[16,3,1,256]{3,2,1,0:T(1,128)}, f32[4,3,128,256]{3,2,1,0:T(8,128)}, f32[4,3,136,256]{3,2,1,0:T(8,128...) custom-call(s32[256]{0:T(256)} %copy-done.6, bf16[192,8192]{1,0:T(8,128)(2,1)} %bitcast.51, ...), custom_call_target="tpu_custom_call" | custom-call | flops 44999999488 | bytes 135000000 | tf_op jit(solution)/shard_map/outputs/pallas_call | solution.py:363
  96.0 5.6 %all-to-all-start.2 = ((f32[32,24,256]{2,1,0:T(8,128)}), f32[32,24,256]{2,1,0:T(8,128)S(1)}, u32[]{:S(2)}, u32[]{:S(2)}) async-start(f32[32,24,256]{2,1,0:T(8,128)} %get-tuple-element.91), calls=%async_computation.2 | async-start | bytes 1572864 | tf_op jit(solution)/shard_map/all_to_all | solution.py:383
  101.6 13.5 %queries.2 = (f32[16,128,128]{2,1,0:T(8,128)}, f32[16,128,128]{2,1,0:T(8,128)}) custom-call(s32[1]{0:T(128)} %bitcast.9.core_ref, bf16[192,8192]{1,0:T(8,128)(2,1)} %bitcast.31, bf16[192,8192]{1,0:T(8,128)(2,1)} %bitcast.32, bf16[192,8192]{1,0:T(8,128)(2,1)} %bitcast.33, bf16[192,8192]{1,0:T(8,128)(2,1)} %bitcast.34, ...), custom_call_target="tpu_custom_call" | custom-call | flops 10000000000 | bytes 30000000 | tf_op jit(solution)/shard_map/queries/pallas_call | solution.py:363
  115.5 0.9 copy-done.3
  116.4 2.1 scan.3
  119.1 6.9 %all-to-all-start.3 = ((f32[32,24,256]{2,1,0:T(8,128)}), f32[32,24,256]{2,1,0:T(8,128)}, u32[]{:S(2)}, u32[]{:S(2)}) async-start(f32[32,24,256]{2,1,0:T(8,128)} %scan.3), calls=%async_computation.3 | async-start | bytes 1572864 | tf_op jit(solution)/shard_map/all_to_all | solution.py:383
  126.2 13.5 %queries.3 = (f32[16,128,128]{2,1,0:T(8,128)}, f32[16,128,128]{2,1,0:T(8,128)}) custom-call(s32[1]{0:T(128)} %bitcast.9.core_ref, bf16[192,8192]{1,0:T(8,128)(2,1)} %bitcast.35, bf16[192,8192]{1,0:T(8,128)(2,1)} %bitcast.36, bf16[192,8192]{1,0:T(8,128)(2,1)} %bitcast.37, bf16[192,8192]{1,0:T(8,128)(2,1)} %bitcast.38, ...), custom_call_target="tpu_custom_call" | custom-call | flops 10000000000 | bytes 30000000 | tf_op jit(solution)/shard_map/queries/pallas_call | solution.py:363
  140.5 2.5 %collective-permute-done.2 = f32[16,128,128]{2,1,0:T(8,128)S(1)} collective-permute-done((f32[16,128,128]{2,1,0:T(8,128)}, f32[16,128,128]{2,1,0:T(8,128)S(1)}, u32[]{:S(2)}, u32[]{:S(2)}) %collective-permute-start.2) | collective-permute-done | bytes 1048608 | tf_op jit(solution)/shard_map/ppermute | solution.py:609
  143.0 1.3 add.54
  144.6 1.5 copy.17
  146.1 6.7 %all-to-all-start.4 = ((f32[16,2,128,128]{3,2,1,0:T(8,128)}), f32[16,2,128,128]{3,2,1,0:T(8,128)S(1)}, u32[]{:S(2)}, u32[]{:S(2)}) async-start(f32[16,2,128,128]{3,2,1,0:T(8,128)} %copy.17), calls=%async_computation.4 | async-start | bytes 4194304 | tf_op jit(solution)/shard_map/all_to_all | solution.py:612
  152.8 6.1 %tail.1 = f32[4,128,128]{2,1,0:T(8,128)} custom-call(s32[256]{0:T(256)} %copy-done.6, bf16[256,512]{1,0:T(8,128)(2,1)} %pad_maximum_fusion.1.key_ref, bf16[256,512]{1,0:T(8,128)(2,1)} %pad_maximum_fusion.2.value_ref, bf16[4,128,128]{2,1,0:T(8,128)(2,1)} %map_ref.5, s32[256,1]{1,0:T(8,128)} %copy.16.seg_col_ref, f32[32,24,256]{2,1,0:T(8,128)} %all-to-all-done.3.later_ref, ...), custom_call_target="tpu_custom_call" | custom-call | flops 5000000000 | bytes 15000000 | tf_op jit(solution)/shard_map/tail/pallas_call | solution.py:363
  158.9 0.9 dynamic-slice_bitcast_fusion
  159.9 1.3 collective-permute-done.6
  161.2 0.9 bitcast_add_fusion
  162.2 2.0 collective-permute-start.8
  164.2 1.5 collective-permute-start.9
  165.6 2.1 collective-permute-start.7
  167.7 16.1 %collective-permute-done.8 = f32[256,128]{1,0:T(8,128)S(1)} collective-permute-done((f32[256,128]{1,0:T(8,128)S(1)}, f32[256,128]{1,0:T(8,128)S(1)}, u32[]{:S(2)}, u32[]{:S(2)}) %collective-permute-start.8) | collective-permute-done | bytes 131104 | tf_op jit(solution)/shard_map/ppermute | solution.py:605
  183.8 1.5 collective-permute-done.7
  185.3 1.3 collective-permute-start.11
  186.6 2.0 collective-permute-start.12
  188.6 1.6 collective-permute-start.10
  190.2 1.4 collective-permute-done.11
  191.5 2.4 %collective-permute-done.12 = f32[256,128]{1,0:T(8,128)S(1)} collective-permute-done((f32[256,128]{1,0:T(8,128)S(1)}, f32[256,128]{1,0:T(8,128)S(1)}, u32[]{:S(2)}, u32[]{:S(2)}) %collective-permute-start.12) | collective-permute-done | bytes 131104 | tf_op jit(solution)/shard_map/ppermute | solution.py:605
  193.9 1.6 collective-permute-done.10
  195.5 1.7 collective-permute-start.14
  197.2 1.7 collective-permute-start.15
  198.8 2.0 collective-permute-start.13
  200.8 1.1 collective-permute-done.14
  202.0 1.4 collective-permute-done.15
  203.4 2.4 %collective-permute-done.13 = f32[256,128]{1,0:T(8,128)S(1)} collective-permute-done((f32[256,128]{1,0:T(8,128)S(1)}, f32[256,128]{1,0:T(8,128)S(1)}, u32[]{:S(2)}, u32[]{:S(2)}) %collective-permute-start.13) | collective-permute-done | bytes 131104 | tf_op jit(solution)/shard_map/ppermute | solution.py:605
  206.8 2.6 %collective-permute-start.5 = (f32[2,128,128]{2,1,0:T(8,128)S(1)}, f32[2,128,128]{2,1,0:T(8,128)S(1)}, u32[]{:S(2)}, u32[]{:S(2)}) collective-permute-start(f32[2,128,128]{2,1,0:T(8,128)S(1)} %reduce_sum.9), channel_id=1, source_target_pairs={{0,96},{32,0},{64,32},{96,64},{1,97},{33,1},{65,33},{97,65},{2,98}... | collective-permute-start | bytes 393224 | tf_op jit(solution)/shard_map/ppermute | solution.py:605
  210.4 2.8 %collective-permute-done.4 = f32[2,128,128]{2,1,0:T(8,128)S(1)} collective-permute-done((f32[2,128,128]{2,1,0:T(8,128)S(1)}, f32[2,128,128]{2,1,0:T(8,128)S(1)}, u32[]{:S(2)}, u32[]{:S(2)}) %collective-permute-start.4) | collective-permute-done | bytes 131104 | tf_op jit(solution)/shard_map/ppermute | solution.py:605
  213.2 2.1 collective-permute-done.5
  (51 shorter events, 10.4 us)
Async XLA Ops:
  2.3 19.5 %collective-permute-start = (bf16[64,1152]{1,0:T(8,128)(2,1)S(1)}, bf16[64,1152]{1,0:T(8,128)(2,1)S(1)}, u32[]{:S(2)}, u32[]{:S(2)}) collective-permute-start(bf16[64,1152]{1,0:T(8,128)(2,1)S(1)} %pad_maximum_fusion.4), channel_id=1, source_target_pairs={{0,1},{1,2},{2,3},{3,4},{4,5},{5,6},{6,7},{7,8},{8,9},{9,10},{10,1... | collective-permute-start | bytes 442376 | tf_op jit(solution)/shard_map/ppermute | solution.py:432
  6.2 15.7 %copy-start.7 = (s32[1,192]{1,0:T(1,128)S(1)}, s32[1,192]{1,0:T(1,128)}, u32[]{:S(2)}) copy-start(s32[1,192]{1,0:T(1,128)} %param.12) | copy-start | bytes 2308
  6.2 15.8 %copy-start.4 = (bf16[1,192,512]{2,1,0:T(8,128)(2,1)S(1)}, bf16[1,192,512]{2,1,0:T(8,128)(2,1)}, u32[]{:S(2)}) copy-start(bf16[1,192,512]{2,1,0:T(8,128)(2,1)} %param.9) | copy-start | bytes 589828
  11.6 11.1 %copy-start.5 = (bf16[1,192,512]{2,1,0:T(8,128)(2,1)S(1)}, bf16[1,192,512]{2,1,0:T(8,128)(2,1)}, u32[]{:S(2)}) copy-start(bf16[1,192,512]{2,1,0:T(8,128)(2,1)} %param.10) | copy-start | bytes 589828
  11.6 30.8 %all-to-all-start = ((f32[32,24,256]{2,1,0:T(8,128)}), f32[32,24,256]{2,1,0:T(8,128)S(1)}, u32[]{:S(2)}, u32[]{:S(2)}) async-start(f32[32,24,256]{2,1,0:T(8,128)} %get-tuple-element.61), calls=%async_computation | async-start | bytes 1572864 | tf_op jit(solution)/shard_map/all_to_all | solution.py:383
  22.0 7.8 %copy-start.6 = (s32[256]{0:T(256)}, s32[256]{0:T(256)S(1)}, u32[]{:S(2)}) copy-start(s32[256]{0:T(256)S(1)} %pad_add_fusion.seg_ref) | copy-start | bytes 3076
  42.4 0.9 copy-start.1
  45.4 21.2 %all-to-all-start.1 = ((f32[32,24,256]{2,1,0:T(8,128)}), f32[32,24,256]{2,1,0:T(8,128)S(1)}, u32[]{:S(2)}, u32[]{:S(2)}) async-start(f32[32,24,256]{2,1,0:T(8,128)} %scan.2), calls=%async_computation.1 | async-start | bytes 1572864 | tf_op jit(solution)/shard_map/all_to_all | solution.py:383
  66.6 0.9 copy-start.2
  96.0 19.4 %all-to-all-start.2 = ((f32[32,24,256]{2,1,0:T(8,128)}), f32[32,24,256]{2,1,0:T(8,128)S(1)}, u32[]{:S(2)}, u32[]{:S(2)}) async-start(f32[32,24,256]{2,1,0:T(8,128)} %get-tuple-element.91), calls=%async_computation.2 | async-start | bytes 1572864 | tf_op jit(solution)/shard_map/all_to_all | solution.py:383
  115.5 0.9 copy-start.3
  118.5 7.5 %copy-start = (f32[16,128,128]{2,1,0:T(8,128)S(1)}, f32[16,128,128]{2,1,0:T(8,128)}, u32[]{:S(2)}) copy-start(f32[16,128,128]{2,1,0:T(8,128)} %get-tuple-element.104) | copy-start | bytes 3145732
  118.5 7.5 %collective-permute-start.1 = (f32[16,128,128]{2,1,0:T(8,128)}, f32[16,128,128]{2,1,0:T(8,128)S(1)}, u32[]{:S(2)}, u32[]{:S(2)}) collective-permute-start(f32[16,128,128]{2,1,0:T(8,128)} %get-tuple-element.105), channel_id=1, source_target_pairs={{0,1},{1,0},{2,3},{3,2},{4,5},{5,4},{6,7},{7,6},{8,9},{9,8},{10,11... | collective-permute-start | bytes 3145736 | tf_op jit(solution)/shard_map/ppermute | solution.py:609
  119.1 20.7 %all-to-all-start.3 = ((f32[32,24,256]{2,1,0:T(8,128)}), f32[32,24,256]{2,1,0:T(8,128)}, u32[]{:S(2)}, u32[]{:S(2)}) async-start(f32[32,24,256]{2,1,0:T(8,128)} %scan.3), calls=%async_computation.3 | async-start | bytes 1572864 | tf_op jit(solution)/shard_map/all_to_all | solution.py:383
  139.9 3.2 %collective-permute-start.2 = (f32[16,128,128]{2,1,0:T(8,128)}, f32[16,128,128]{2,1,0:T(8,128)S(1)}, u32[]{:S(2)}, u32[]{:S(2)}) collective-permute-start(f32[16,128,128]{2,1,0:T(8,128)} %get-tuple-element.114), channel_id=1, source_target_pairs={{0,1},{1,0},{2,3},{3,2},{4,5},{5,4},{6,7},{7,6},{8,9},{9,8},{10,11... | collective-permute-start | bytes 3145736 | tf_op jit(solution)/shard_map/ppermute | solution.py:609
  146.1 59.9 %all-to-all-start.4 = ((f32[16,2,128,128]{3,2,1,0:T(8,128)}), f32[16,2,128,128]{3,2,1,0:T(8,128)S(1)}, u32[]{:S(2)}, u32[]{:S(2)}) async-start(f32[16,2,128,128]{3,2,1,0:T(8,128)} %copy.17), calls=%async_computation.4 | async-start | bytes 4194304 | tf_op jit(solution)/shard_map/all_to_all | solution.py:612
  159.8 1.4 collective-permute-start.6
  162.2 21.6 %collective-permute-start.8 = (f32[256,128]{1,0:T(8,128)S(1)}, f32[256,128]{1,0:T(8,128)S(1)}, u32[]{:S(2)}, u32[]{:S(2)}) collective-permute-start(f32[256,128]{1,0:T(8,128)S(1)} %bitcast_add_fusion), channel_id=1, source_target_pairs={{0,2},{1,3},{2,4},{3,5},{4,6},{5,7},{6,0},{7,1},{8,10},{9,11},{10,... | collective-permute-start | bytes 393224 | tf_op jit(solution)/shard_map/ppermute | solution.py:605
  164.2 19.6 %collective-permute-start.9 = (f32[256,128]{1,0:T(8,128)S(1)}, f32[256,128]{1,0:T(8,128)S(1)}, u32[]{:S(2)}, u32[]{:S(2)}) collective-permute-start(f32[256,128]{1,0:T(8,128)S(1)} %bitcast_add_fusion), channel_id=1, source_target_pairs={{0,6},{1,7},{2,0},{3,1},{4,2},{5,3},{6,4},{7,5},{8,14},{9,15},{10,... | collective-permute-start | bytes 393224 | tf_op jit(solution)/shard_map/ppermute | solution.py:605
  165.6 19.6 %collective-permute-start.7 = (f32[256,128]{1,0:T(8,128)S(1)}, f32[256,128]{1,0:T(8,128)S(1)}, u32[]{:S(2)}, u32[]{:S(2)}) collective-permute-start(f32[256,128]{1,0:T(8,128)S(1)} %bitcast_add_fusion), channel_id=1, source_target_pairs={{0,4},{1,5},{2,6},{3,7},{4,0},{5,1},{6,2},{7,3},{8,12},{9,13},{10,... | collective-permute-start | bytes 393224 | tf_op jit(solution)/shard_map/ppermute | solution.py:605
  185.3 6.3 %collective-permute-start.11 = (f32[256,128]{1,0:T(8,128)S(1)}, f32[256,128]{1,0:T(8,128)S(1)}, u32[]{:S(2)}, u32[]{:S(2)}) collective-permute-start(f32[256,128]{1,0:T(8,128)S(1)} %add_add_fusion.2), channel_id=1, source_target_pairs={{0,8},{1,9},{2,10},{3,11},{4,12},{5,13},{6,14},{7,15},{8,16},{9,17... | collective-permute-start | bytes 393224 | tf_op jit(solution)/shard_map/ppermute | solution.py:605
  186.6 7.3 %collective-permute-start.12 = (f32[256,128]{1,0:T(8,128)S(1)}, f32[256,128]{1,0:T(8,128)S(1)}, u32[]{:S(2)}, u32[]{:S(2)}) collective-permute-start(f32[256,128]{1,0:T(8,128)S(1)} %add_add_fusion.2), channel_id=1, source_target_pairs={{0,24},{1,25},{2,26},{3,27},{4,28},{5,29},{6,30},{7,31},{8,0},{9,1... | collective-permute-start | bytes 393224 | tf_op jit(solution)/shard_map/ppermute | solution.py:605
  188.6 6.9 %collective-permute-start.10 = (f32[256,128]{1,0:T(8,128)S(1)}, f32[256,128]{1,0:T(8,128)S(1)}, u32[]{:S(2)}, u32[]{:S(2)}) collective-permute-start(f32[256,128]{1,0:T(8,128)S(1)} %add_add_fusion.2), channel_id=1, source_target_pairs={{0,16},{1,17},{2,18},{3,19},{4,20},{5,21},{6,22},{7,23},{8,24},{9,... | collective-permute-start | bytes 393224 | tf_op jit(solution)/shard_map/ppermute | solution.py:605
  195.5 6.4 %collective-permute-start.14 = (f32[256,128]{1,0:T(8,128)S(1)}, f32[256,128]{1,0:T(8,128)S(1)}, u32[]{:S(2)}, u32[]{:S(2)}) collective-permute-start(f32[256,128]{1,0:T(8,128)S(1)} %add_add_fusion.1), channel_id=1, source_target_pairs={{0,32},{32,64},{64,96},{96,0},{1,33},{33,65},{65,97},{97,1},{2,34}... | collective-permute-start | bytes 393224 | tf_op jit(solution)/shard_map/ppermute | solution.py:605
  197.2 6.2 %collective-permute-start.15 = (f32[256,128]{1,0:T(8,128)S(1)}, f32[256,128]{1,0:T(8,128)S(1)}, u32[]{:S(2)}, u32[]{:S(2)}) collective-permute-start(f32[256,128]{1,0:T(8,128)S(1)} %add_add_fusion.1), channel_id=1, source_target_pairs={{0,96},{32,0},{64,32},{96,64},{1,97},{33,1},{65,33},{97,65},{2,98}... | collective-permute-start | bytes 393224 | tf_op jit(solution)/shard_map/ppermute | solution.py:605
  198.8 7.0 %collective-permute-start.13 = (f32[256,128]{1,0:T(8,128)S(1)}, f32[256,128]{1,0:T(8,128)S(1)}, u32[]{:S(2)}, u32[]{:S(2)}) collective-permute-start(f32[256,128]{1,0:T(8,128)S(1)} %add_add_fusion.1), channel_id=1, source_target_pairs={{0,64},{32,96},{64,0},{96,32},{1,65},{33,97},{65,1},{97,33},{2,66}... | collective-permute-start | bytes 393224 | tf_op jit(solution)/shard_map/ppermute | solution.py:605
  205.8 3.8 %collective-permute-start.16 = (f32[256,128]{1,0:T(8,128)S(1)}, f32[256,128]{1,0:T(8,128)S(1)}, u32[]{:S(2)}, u32[]{:S(2)}) collective-permute-start(f32[256,128]{1,0:T(8,128)S(1)} %add_add_fusion), channel_id=1, source_target_pairs={{0,1},{1,0},{2,3},{3,2},{4,5},{5,4},{6,7},{7,6},{8,9},{9,8},{10,11... | collective-permute-start | bytes 393224 | tf_op jit(solution)/shard_map/ppermute | solution.py:644
  206.1 7.2 %collective-permute-start.4 = (f32[2,128,128]{2,1,0:T(8,128)S(1)}, f32[2,128,128]{2,1,0:T(8,128)S(1)}, u32[]{:S(2)}, u32[]{:S(2)}) collective-permute-start(f32[2,128,128]{2,1,0:T(8,128)S(1)} %reduce_sum.9), channel_id=1, source_target_pairs={{0,32},{32,64},{64,96},{96,0},{1,33},{33,65},{65,97},{97,1},{2,34}... | collective-permute-start | bytes 393224 | tf_op jit(solution)/shard_map/ppermute | solution.py:605
  206.8 8.5 %collective-permute-start.5 = (f32[2,128,128]{2,1,0:T(8,128)S(1)}, f32[2,128,128]{2,1,0:T(8,128)S(1)}, u32[]{:S(2)}, u32[]{:S(2)}) collective-permute-start(f32[2,128,128]{2,1,0:T(8,128)S(1)} %reduce_sum.9), channel_id=1, source_target_pairs={{0,96},{32,0},{64,32},{96,64},{1,97},{33,1},{65,33},{97,65},{2,98}... | collective-permute-start | bytes 393224 | tf_op jit(solution)/shard_map/ppermute | solution.py:605
  209.4 6.8 %collective-permute-start.3 = (f32[2,128,128]{2,1,0:T(8,128)S(1)}, f32[2,128,128]{2,1,0:T(8,128)S(1)}, u32[]{:S(2)}, u32[]{:S(2)}) collective-permute-start(f32[2,128,128]{2,1,0:T(8,128)S(1)} %reduce_sum.9), channel_id=1, source_target_pairs={{0,64},{32,96},{64,0},{96,32},{1,65},{33,97},{65,1},{97,33},{2,66}... | collective-permute-start | bytes 393224 | tf_op jit(solution)/shard_map/ppermute | solution.py:605

commit v3 on v2

--- a/solution.py
+++ b/solution.py
@@ -319,7 +319,7 @@
         @pl.when(core_ref[0] == core)
         def _(own=own):
             for i in range(QUAD):
-                own[i % 2][i // 2] = total[:, i * 128 : (i + 1) * 128]
+                own[i % 2][i // 2, 0] = total[:, i * 128 : (i + 1) * 128]
 
 
 def tail_kernel(
@@ -425,16 +425,20 @@
             whole(piece_shape), sds(piece_shape, F32), (received,),
         )
         summed, aside = lax.optimization_barrier((summed, aside))
-        return lax.optimization_barrier((exchange(summed, "ctx"), second(aside)))
-
-    rim = jnp.concatenate([keys[0, -CHUNK:], values[0, -CHUNK:]], 1)
+        done, free = second(aside)
+        return *lax.optimization_barrier((exchange(summed, "ctx"), done)), free
+
+    block_pieces, row_keys, row_values = lax.optimization_barrier(
+        (block_pieces, keys[0], values[0])
+    )
+    rim = jnp.concatenate([row_keys[-CHUNK:], row_values[-CHUNK:]], 1)
     rim_seg = jnp.broadcast_to(seg_row[-CHUNK:].astype(BF16)[:, None], (CHUNK, 128))
     rim = lax.ppermute(
         jnp.concatenate([rim, rim_seg], 1), "ctx", [(i, i + 1) for i in range(ctx - 1)]
     )
     width = keys.shape[2]
-    near_keys = jnp.concatenate([rim[:, :width], keys[0]], 0)
-    near_values = jnp.concatenate([rim[:, width : 2 * width], values[0]], 0)
+    near_keys = jnp.concatenate([rim[:, :width], row_keys], 0)
+    near_values = jnp.concatenate([rim[:, width : 2 * width], row_values], 0)
     rim_segments = jnp.where(me > 0, rim[:, 2 * width].astype(jnp.int32), -1)
     near_segments = jnp.concatenate([rim_segments, seg_row], 0)
     seg_col = near_segments[:, None]
@@ -513,8 +517,8 @@
             aliases={13 + i: i for i in range(len(so_far))},
         )
 
-    entering, forward = across(
-        block_pieces, False, lambda: local(0, ()), lambda so_far: local(1, so_far)
+    entering, forward, _ = across(
+        block_pieces, False, lambda: local(0, ()), lambda so_far: (local(1, so_far), None)
     )
 
     every_step = lambda *shape: pl.BlockSpec(
@@ -561,9 +565,9 @@
 
     def query(half, right, start, count, so_far=()):
         part = pl.BlockSpec(
-            (QUAD // 2, map_width, head_dim), lambda g, q, *_: (spot(g + start, q), 0, 0)
-        )
-        shape = sds((head_count // 4, map_width, head_dim), F32)
+            (QUAD // 2, 1, map_width, head_dim), lambda g, q, *_: (q, g + start, 0, 0)
+        )
+        shape = sds((RING, RING, map_width, head_dim), F32)
         from_start = lambda spec: pl.BlockSpec(
             spec.block_shape, lambda g, q, *_: spec.index_map(g + start, q)
         )
@@ -592,35 +596,44 @@
             aliases={12 + i: i for i in range(len(so_far))},
         )
 
-    same_core = [[i for i in range(ctx) if i % 2 == k] for k in range(2)]
+    place = {"z": me // 2 % RING, "x": me // (2 * RING)}
+
+    def routes(axis):
+        if axis == "dp":
+            return [[(i, (i + s) % dp) for i in range(dp)] for s in range(1, RING)]
+        stride = 2 if axis == "z" else 2 * RING
+        at = lambda i, s: i + ((i // stride + s) % RING - i // stride % RING) * stride
+        return [[(i, at(i, s)) for i in range(ctx)] for s in range(1, RING)]
+
+    def add_up(own, one, two, three):
+        return (own + two) + (one + three)
 
     def around(axis, value):
-        if axis == "dp":
-            routes = [[(i, (i + s) % dp) for i in range(dp)] for s in range(1, RING)]
-        else:
-            stride = 2 if axis == "z" else 2 * RING
-            at = lambda i, s: i + ((i // stride + s) % RING - i // stride % RING) * stride
-            routes = [[(i, at(i, s)) for i in range(ctx)] for s in range(1, RING)]
-            axis = "ctx"
-        one, two, three = (lax.ppermute(value, axis, route) for route in routes)
-        return (value + two) + (one + three)
-
-    def over_cores(mine, theirs):
-        return mine + lax.ppermute(theirs, "ctx", partner)
-
-    def over_chips(pieces):
-        received = lax.all_to_all(pieces, "ctx", 0, 0, tiled=True, axis_index_groups=same_core)
-        return jnp.sum(received.reshape(ctx // 2, -1, map_width, head_dim), axis=0)
+        name = axis if axis == "dp" else "ctx"
+        return add_up(value, *(lax.ppermute(value, name, route) for route in routes(axis)))
+
+    def slice_around(axis, dim, *values):
+        own, *others = [
+            sum(
+                lax.dynamic_index_in_dim(value, lax.rem(place[axis] + s, RING), dim, False)
+                for value in values
+            )
+            for s in range(RING)
+        ]
+        return add_up(
+            own, *(lax.ppermute(part, "ctx", route) for part, route in zip(others, routes(axis)))
+        )
+
+    def over_chip(mine, theirs):
+        return mine, lax.ppermute(theirs, "ctx", partner)
 
     def second_half(done):
-        first, right = lax.optimization_barrier((over_cores(*done[0]), done[1]))
-        return first, query(1, right, 0, groups)
-
-    later, (first, second) = across(
+        first, right = lax.optimization_barrier((over_chip(*done[0]), done[1]))
+        return query(1, right, 0, groups), slice_around("z", 0, *first)
+
+    later, second, first = across(
         grad_pieces, True, lambda: (query(0, right, 0, groups), right), second_half
     )
-    second = over_cores(*second)
-    later, first, second = lax.optimization_barrier((later, first, second))
 
     key_grad = call(
         functools.partial(tail_kernel, chunks), "tail", 5, (groups,),
@@ -636,17 +649,22 @@
         scalars=1,
     )
 
+    key_grad, first = lax.optimization_barrier((key_grad, first))
     key_halves = key_grad.reshape(2, -1, map_width)
     key_mine = lax.dynamic_index_in_dim(key_halves, core, 0, False)
     key_theirs = lax.dynamic_index_in_dim(key_halves, 1 - core, 0, False)
-    key_mine = over_cores(key_mine, key_theirs)
-    key_mine = around("dp", around("x", around("z", key_mine)))
-    key_theirs = lax.ppermute(key_mine, "ctx", partner)
+    key_mine, key_theirs = over_chip(key_mine, key_theirs)
+    second = over_chip(*second)
+    key_sum, second = lax.optimization_barrier((key_mine + key_theirs, second))
+    key_sum = around("x", around("dp", around("z", key_sum)))
+    second = slice_around("z", 0, slice_around("x", 1, *second))
+    first = slice_around("x", 0, first)
+    both = around("dp", jnp.stack([first, second], 0))
+    key_theirs = lax.ppermute(key_sum, "ctx", partner)
     full_key = jnp.concatenate(
-        [jnp.where(core == 0, key_mine, key_theirs), jnp.where(core == 0, key_theirs, key_mine)], 0
-    )
-    full_query = around("dp", over_chips(jnp.stack([first, second], 1)))
-    return (full_query.transpose(0, 2, 1), full_key.reshape(groups, head_dim, map_width))
+        [jnp.where(core == 0, key_sum, key_theirs), jnp.where(core == 0, key_theirs, key_sum)], 0
+    )
+    return (both.transpose(0, 2, 1), full_key.reshape(groups, head_dim, map_width))
 
 
 def solution(mesh):

time: 219 us -> 206 us (0.941)
  waiting for transfers between devices: 39.8 us -> 10.9 us
  starting transfers between devices: 58.8 us -> 73 us
  other arithmetic: 7.21 us -> 10 us
    ppermute x16 -> x28, waiting for transfers between devices: 37.5 us -> 8.78 us  [the longest x12 4.93 us: around(): lax.ppermute(value, name, route)]
    ppermute x16 -> x28, starting transfers between devices: 20.8 us -> 42.1 us  [the longest x12 21.4 us: around(): lax.ppermute(value, name, route)]
    all_to_all x1 -> x0, starting transfers between devices: 6.69 us -> none  [over_chips(): lax.all_to_all(pieces, 'ctx', 0, 0, tiled=True, axis_index_groups=same_core)]
    add x6 -> x9, other arithmetic: 2.47 us -> 6.19 us  [the longest x3 2.99 us: slice_around(): sum((lax.dynamic_index_in_dim(value, lax.rem(place[axis] + s, RING), dim,...]
    unnamed x18 -> x22, local copies, waits for them, and re-layouts: 3.98 us -> 4.79 us
  transfers between devices with their start and end apart: 22 -> 33, of which waited for: 16 -> 8; matrix products, arithmetic and copies ran while one was open for 4% -> 5% of each run, Pallas kernels for 32% -> 31%
where the time goes in v3:
time: 206 us; the launch traced here: 204 us
  Pallas kernels  102 us (50%)
  starting transfers between devices  73 us (35%)
  waiting for transfers between devices  10.9 us (5%)
  other arithmetic  10 us (5%)
  local copies, waits for them, and re-layouts  7.41 us (4%)
    pallas_call x10, Pallas kernels, call(): pl.pallas_call(kernel, grid_spec=pltpu.PrefetchScalarGridSpec(num_scalar_...  102 us
    all_to_all x4, starting transfers between devices, exchange(): return lax.all_to_all(pieces, axis, 0, 0, tiled=True)  29.7 us
    ppermute x12, starting transfers between devices, around(): lax.ppermute(value, name, route)  21.4 us
    ppermute x12, starting transfers between devices, slice_around(): lax.ppermute(part, 'ctx', route)  19.6 us
    ppermute x12, waiting for transfers between devices, around(): lax.ppermute(value, name, route)  4.93 us
    unnamed x22, local copies, waits for them, and re-layouts  4.79 us
  transfers between devices with their start and end apart: 33, of which 8 were waited for; matrix products, arithmetic and copies ran while one was open for 5% of the time, Pallas kernels for 31%

profile of v3, /device:TPU:0, one launch (start us, length us, event | category | flops | bytes accessed | tf_op | source)
XLA Modules:
  0.0 204.0 jit_solution(8577595513743488868)
XLA Ops:
  1.8 1.3 reduce.5
  3.9 5.4 %block.1 = (f32[4,3,136,256]{3,2,1,0:T(8,128)}, f32[32,24,256]{2,1,0:T(8,128)}) custom-call(s32[192]{0:T(256)} %bitcast.91, bf16[192,512]{1,0:T(8,128)(2,1)} %bitcast.84, bf16[192,512]{1,0:T(8,128)(2,1)} %bitcast.81, bf16[4,128,128]{2,1,0:T(8,128)(2,1)} %map_ref.5, s32[3,1,256]{2,1,0:T(1,128)} %tile.12.seg_row_ref), custom_call_target="tpu_custom_call" | custom-call | flops 4000000000 | bytes 12000000 | tf_op jit(solution)/shard_map/block/pallas_call | solution.py:363
  9.4 1.3 collective-permute-start
  10.7 10.1 %all-to-all-start = ((f32[32,24,256]{2,1,0:T(8,128)}), f32[32,24,256]{2,1,0:T(8,128)S(1)}, u32[]{:S(2)}, u32[]{:S(2)}) async-start(f32[32,24,256]{2,1,0:T(8,128)} %get-tuple-element.69), calls=%async_computation | async-start | bytes 1572864 | tf_op jit(solution)/shard_map/all_to_all | solution.py:383
  22.6 5.5 %keys.1 = (bf16[4,256,256]{2,1,0:T(8,128)(2,1)}, bf16[4,256,256]{2,1,0:T(8,128)(2,1)}, bf16[4,3,256,256]{3,2,1,0:T(8,128)(2,1)}, bf16[4,3,128,256]{3,2,1,0:T(8,1...) custom-call(s32[4]{0:T(128)} %window_ref.1, bf16[256,512]{1,0:T(8,128)(2,1)} %get-tuple-element.147.key_ref, ...), custom_call_target="tpu_custom_call" | custom-call | flops 5000000000 | bytes 15000000 | tf_op jit(solution)/shard_map/keys/pallas_call | solution.py:363
  28.1 12.5 %local.2 = (f32[16,3,128,256]{3,2,1,0:T(8,128)}, f32[16,3,1,256]{3,2,1,0:T(1,128)}, bf16[16,3,256,256]{3,2,1,0:T(8,128)(2,1)}, bf16[16,3,256,256]{3,2,1,0:T(8,128)(2,1)}) custom-call(bf16[192,8192]{1,0:T(8,128)(2,1)} %bitcast.65, bf16[192,8192]{1,0:T(8,128)(2,1)} %bitcast.66, bf16[192,8192]{1,0:T(8,128)(2,1)} %bitcast.67, bf16[192,8192]{1,0:T(8,128)(2,1)} %bitcast.68, ...), custom_call_target="tpu_custom_call" | custom-call | flops 15000000512 | bytes 45000000 | tf_op jit(solution)/shard_map/local/pallas_call | solution.py:363
  40.7 0.9 copy-done.2
  41.6 2.1 %scan.2 = f32[32,24,256]{2,1,0:T(8,128)} custom-call(f32[32,24,256]{2,1,0:T(8,128)} %copy-done.2), custom_call_target="tpu_custom_call" | custom-call | flops 2000000000 | bytes 6000000 | tf_op jit(solution)/shard_map/scan/pallas_call | solution.py:363
  43.7 7.4 %all-to-all-start.1 = ((f32[32,24,256]{2,1,0:T(8,128)}), f32[32,24,256]{2,1,0:T(8,128)S(1)}, u32[]{:S(2)}, u32[]{:S(2)}) async-start(f32[32,24,256]{2,1,0:T(8,128)} %scan.2), calls=%async_computation.1 | async-start | bytes 1572864 | tf_op jit(solution)/shard_map/all_to_all | solution.py:383
  51.1 12.0 %local.3 = (f32[16,3,128,256]{3,2,1,0:T(8,128)}, f32[16,3,1,256]{3,2,1,0:T(1,128)}, bf16[16,3,256,256]{3,2,1,0:T(8,128)(2,1)}, bf16[16,3,256,256]{3,2,1,0:T(8,128)(2,1)}) custom-call(bf16[192,8192]{1,0:T(8,128)(2,1)} %bitcast.69, bf16[192,8192]{1,0:T(8,128)(2,1)} %bitcast.70, ...), custom_call_target="tpu_custom_call", output_to_operand_aliasing={{0}: (13, {}), {1}: (14, {}), {2}: (15, {}), {3}: (16, {})} | custom-call | flops 15000000512 | bytes 45000000 | tf_op jit(solution)/shard_map/local/pallas_call | solution.py:363
  63.1 1.8 all-to-all-done.1.first_ref
  64.9 0.9 copy-done.4
  65.8 28.5 %outputs.1 = (bf16[16,3,512,256]{3,2,1,0:T(8,128)(2,1)}, f32[16,3,1,256]{3,2,1,0:T(1,128)}, f32[4,3,128,256]{3,2,1,0:T(8,128)}, f32[4,3,136,256]{3,2,1,0:T(8,128...) custom-call(s32[256]{0:T(256)} %copy-done.8, bf16[192,8192]{1,0:T(8,128)(2,1)} %bitcast.93, ...), custom_call_target="tpu_custom_call" | custom-call | flops 44999999488 | bytes 135000000 | tf_op jit(solution)/shard_map/outputs/pallas_call | solution.py:363
  94.4 5.6 %all-to-all-start.2 = ((f32[32,24,256]{2,1,0:T(8,128)}), f32[32,24,256]{2,1,0:T(8,128)S(1)}, u32[]{:S(2)}, u32[]{:S(2)}) async-start(f32[32,24,256]{2,1,0:T(8,128)} %get-tuple-element.99), calls=%async_computation.2 | async-start | bytes 1572864 | tf_op jit(solution)/shard_map/all_to_all | solution.py:383
  100.0 13.5 %queries.2 = (f32[4,4,128,128]{3,2,1,0:T(8,128)}, f32[4,4,128,128]{3,2,1,0:T(8,128)}) custom-call(s32[1]{0:T(128)} %bitcast.7.core_ref, bf16[192,8192]{1,0:T(8,128)(2,1)} %bitcast.73, bf16[192,8192]{1,0:T(8,128)(2,1)} %bitcast.74, bf16[192,8192]{1,0:T(8,128)(2,1)} %bitcast.75, bf16[192,8192]{1,0:T(8,128)(2,1)} %bitcast.76, ...), custom_call_target="tpu_custom_call" | custom-call | flops 10000000000 | bytes 30000000 | tf_op jit(solution)/shard_map/queries/pallas_call | solution.py:363
  113.8 0.9 copy-done.5
  114.7 2.2 %scan.3 = f32[32,24,256]{2,1,0:T(8,128)} custom-call(f32[32,24,256]{2,1,0:T(8,128)} %copy-done.5), custom_call_target="tpu_custom_call" | custom-call | flops 2000000000 | bytes 6000000 | tf_op jit(solution)/shard_map/scan/pallas_call | solution.py:363
  117.6 6.7 %all-to-all-start.3 = ((f32[32,24,256]{2,1,0:T(8,128)}), f32[32,24,256]{2,1,0:T(8,128)S(1)}, u32[]{:S(2)}, u32[]{:S(2)}) async-start(f32[32,24,256]{2,1,0:T(8,128)} %scan.3), calls=%async_computation.3 | async-start | bytes 1572864 | tf_op jit(solution)/shard_map/all_to_all | solution.py:383
  124.3 0.9 add_bitcast_fusion.3
  125.2 3.3 %collective-permute-start.2 = (f32[4,128,128]{2,1,0:T(8,128)}, f32[4,128,128]{2,1,0:T(8,128)}, u32[]{:S(2)}, u32[]{:S(2)}) collective-permute-start(f32[4,128,128]{2,1,0:T(8,128)} %get-tuple-element.136), channel_id=1, source_target_pairs={{0,4},{1,5},{2,6},{3,7},{4,0},{5,1},{6,2},{7,3},{8,12},{9,13},{10,... | collective-permute-start | bytes 786440 | tf_op jit(solution)/shard_map/ppermute | solution.py:624
  129.0 2.7 %collective-permute-start.4 = (f32[4,128,128]{2,1,0:T(8,128)S(1)}, f32[4,128,128]{2,1,0:T(8,128)}, u32[]{:S(2)}, u32[]{:S(2)}) collective-permute-start(f32[4,128,128]{2,1,0:T(8,128)S(1)} %get-tuple-element.134), channel_id=1, source_target_pairs={{0,6},{1,7},{2,0},{3,1},{4,2},{5,3},{6,4},{7,5},{8,14},{9,15},{10,... | collective-permute-start | bytes 786440 | tf_op jit(solution)/shard_map/ppermute | solution.py:624
  131.7 13.5 %queries.3 = (f32[4,4,128,128]{3,2,1,0:T(8,128)}, f32[4,4,128,128]{3,2,1,0:T(8,128)}) custom-call(s32[1]{0:T(128)} %bitcast.7.core_ref, bf16[192,8192]{1,0:T(8,128)(2,1)} %bitcast.77, bf16[192,8192]{1,0:T(8,128)(2,1)} %bitcast.78, bf16[192,8192]{1,0:T(8,128)(2,1)} %bitcast.79, bf16[192,8192]{1,0:T(8,128)(2,1)} %bitcast.80, ...), custom_call_target="tpu_custom_call" | custom-call | flops 10000000000 | bytes 30000000 | tf_op jit(solution)/shard_map/queries/pallas_call | solution.py:363
  146.2 6.2 %tail.1 = f32[4,128,128]{2,1,0:T(8,128)} custom-call(s32[256]{0:T(256)} %copy-done.8, bf16[256,512]{1,0:T(8,128)(2,1)} %get-tuple-element.147.key_ref, bf16[256,512]{1,0:T(8,128)(2,1)} %get-tuple-element.148.value_ref, bf16[4,128,128]{2,1,0:T(8,128)(2,1)} %map_ref.5, s32[256,1]{1,0:T(8,128)} %copy.21.seg_col_ref, f32[32,24,256]{2,1,0:T(8,128)} %copy-done.3, ...), custom_call_target="tpu_custom_call" | custom-call | flops 5000000000 | bytes 15000000 | tf_op jit(solution)/shard_map/tail/pallas_call | solution.py:363
  152.4 1.2 fusion.1
  153.6 0.9 dynamic-slice_bitcast_fusion
  154.9 3.1 %collective-permute-start.5 = (f32[128,128]{1,0:T(8,128)S(1)}, f32[128,128]{1,0:T(8,128)S(1)}, u32[]{:S(2)}, u32[]{:S(2)}) collective-permute-start(f32[128,128]{1,0:T(8,128)S(1)} %get-tuple-element.141), channel_id=1, source_target_pairs={{0,16},{1,17},{2,18},{3,19},{4,20},{5,21},{6,22},{7,23},{8,24},{9,... | collective-permute-start | bytes 196616 | tf_op jit(solution)/shard_map/ppermute | solution.py:624
  158.6 2.6 %collective-permute-start.7 = (f32[128,128]{1,0:T(8,128)S(1)}, f32[128,128]{1,0:T(8,128)S(1)}, u32[]{:S(2)}, u32[]{:S(2)}) collective-permute-start(f32[128,128]{1,0:T(8,128)S(1)} %get-tuple-element.139), channel_id=1, source_target_pairs={{0,24},{1,25},{2,26},{3,27},{4,28},{5,29},{6,30},{7,31},{8,0},{9,1... | collective-permute-start | bytes 196616 | tf_op jit(solution)/shard_map/ppermute | solution.py:624
  161.2 0.9 bitcast_add_fusion.2
  162.2 0.8 collective-permute-start.20
  163.1 1.1 add_bitcast_fusion.1
  164.2 1.0 add_bitcast_fusion
  165.2 2.5 %collective-permute-start.21 = (f32[256,128]{1,0:T(8,128)S(1)}, f32[256,128]{1,0:T(8,128)S(1)}, u32[]{:S(2)}, u32[]{:S(2)}) collective-permute-start(f32[256,128]{1,0:T(8,128)S(1)} %bitcast_add_fusion.2), channel_id=1, source_target_pairs={{0,6},{1,7},{2,0},{3,1},{4,2},{5,3},{6,4},{7,5},{8,14},{9,15},{10,... | collective-permute-start | bytes 393224 | tf_op jit(solution)/shard_map/ppermute | solution.py:613
  167.7 1.5 collective-permute-start.10
  169.2 1.0 collective-permute-done.19
  170.2 1.1 collective-permute-done.20
  171.3 3.3 %collective-permute-start.22 = (f32[256,128]{1,0:T(8,128)S(1)}, f32[256,128]{1,0:T(8,128)S(1)}, u32[]{:S(2)}, u32[]{:S(2)}) collective-permute-start(f32[256,128]{1,0:T(8,128)S(1)} %add_add_fusion.2), channel_id=1, source_target_pairs={{0,64},{32,96},{64,0},{96,32},{1,65},{33,97},{65,1},{97,33},{2,66}... | collective-permute-start | bytes 393224 | tf_op jit(solution)/shard_map/ppermute | solution.py:613
  175.3 1.6 collective-permute-done.12
  176.9 3.0 %collective-permute-start.24 = (f32[256,128]{1,0:T(8,128)S(1)}, f32[256,128]{1,0:T(8,128)S(1)}, u32[]{:S(2)}, u32[]{:S(2)}) collective-permute-start(f32[256,128]{1,0:T(8,128)S(1)} %add_add_fusion.2), channel_id=1, source_target_pairs={{0,96},{32,0},{64,32},{96,64},{1,97},{33,1},{65,33},{97,65},{2,98}... | collective-permute-start | bytes 393224 | tf_op jit(solution)/shard_map/ppermute | solution.py:613
  180.0 2.2 %collective-permute-done.11 = f32[4,128,128]{2,1,0:T(8,128)S(1)} collective-permute-done((f32[4,128,128]{2,1,0:T(8,128)S(1)}, f32[4,128,128]{2,1,0:T(8,128)S(1)}, u32[]{:S(2)}, u32[]{:S(2)}) %collective-permute-start.11) | collective-permute-done | bytes 262176 | tf_op jit(solution)/shard_map/ppermute | solution.py:624
  182.2 1.0 fusion
  183.2 2.0 collective-permute-start.13
  185.2 3.2 %collective-permute-start.15 = (f32[128,128]{1,0:T(8,128)S(1)}, f32[128,128]{1,0:T(8,128)S(1)}, u32[]{:S(2)}, u32[]{:S(2)}) collective-permute-start(f32[128,128]{1,0:T(8,128)S(1)} %get-tuple-element.142), channel_id=1, source_target_pairs={{0,6},{1,7},{2,0},{3,1},{4,2},{5,3},{6,4},{7,5},{8,14},{9,15},{10,... | collective-permute-start | bytes 196616 | tf_op jit(solution)/shard_map/ppermute | solution.py:624
  188.5 1.2 collective-permute-start.25
  189.7 0.8 collective-permute-start.26
  190.5 2.4 %collective-permute-start.27 = (f32[256,128]{1,0:T(8,128)S(1)}, f32[256,128]{1,0:T(8,128)S(1)}, u32[]{:S(2)}, u32[]{:S(2)}) collective-permute-start(f32[256,128]{1,0:T(8,128)S(1)} %add_add_fusion.1), channel_id=1, source_target_pairs={{0,24},{1,25},{2,26},{3,27},{4,28},{5,29},{6,30},{7,31},{8,0},{9,1... | collective-permute-start | bytes 393224 | tf_op jit(solution)/shard_map/ppermute | solution.py:613
  193.0 3.3 %collective-permute-start.16 = (f32[2,128,128]{2,1,0:T(8,128)S(1)}, f32[2,128,128]{2,1,0:T(8,128)S(1)}, u32[]{:S(2)}, u32[]{:S(2)}) collective-permute-start(f32[2,128,128]{2,1,0:T(8,128)S(1)} %pad_maximum_fusion.4), channel_id=1, source_target_pairs={{0,64},{32,96},{64,0},{96,32},{1,65},{33,97},{65,1},{97,33},{2,66}... | collective-permute-start | bytes 393224 | tf_op jit(solution)/shard_map/ppermute | solution.py:613
  197.0 2.6 %collective-permute-start.18 = (f32[2,128,128]{2,1,0:T(8,128)S(1)}, f32[2,128,128]{2,1,0:T(8,128)S(1)}, u32[]{:S(2)}, u32[]{:S(2)}) collective-permute-start(f32[2,128,128]{2,1,0:T(8,128)S(1)} %pad_maximum_fusion.4), channel_id=1, source_target_pairs={{0,96},{32,0},{64,32},{96,64},{1,97},{33,1},{65,33},{97,65},{2,98}... | collective-permute-start | bytes 393224 | tf_op jit(solution)/shard_map/ppermute | solution.py:613
  200.3 2.2 %collective-permute-done.17 = f32[2,128,128]{2,1,0:T(8,128)S(1)} collective-permute-done((f32[2,128,128]{2,1,0:T(8,128)S(1)}, f32[2,128,128]{2,1,0:T(8,128)S(1)}, u32[]{:S(2)}, u32[]{:S(2)}) %collective-permute-start.17) | collective-permute-done | bytes 131104 | tf_op jit(solution)/shard_map/ppermute | solution.py:613
  (82 shorter events, 11.1 us)
Async XLA Ops:
  3.9 5.4 %copy-start.7 = (bf16[1,192,512]{2,1,0:T(8,128)(2,1)S(1)}, bf16[1,192,512]{2,1,0:T(8,128)(2,1)}, u32[]{:S(2)}) copy-start(bf16[1,192,512]{2,1,0:T(8,128)(2,1)} %param.9) | copy-start | bytes 589828
  3.9 5.4 %copy-start.6 = (bf16[1,192,512]{2,1,0:T(8,128)(2,1)S(1)}, bf16[1,192,512]{2,1,0:T(8,128)(2,1)}, u32[]{:S(2)}) copy-start(bf16[1,192,512]{2,1,0:T(8,128)(2,1)} %param.10) | copy-start | bytes 589828
  3.9 17.0 %copy-start.9 = (s32[1,192]{1,0:T(1,128)S(1)}, s32[1,192]{1,0:T(1,128)}, u32[]{:S(2)}) copy-start(s32[1,192]{1,0:T(1,128)} %param.12) | copy-start | bytes 2308
  9.4 11.4 %collective-permute-start = (bf16[64,1152]{1,0:T(8,128)(2,1)S(1)}, bf16[64,1152]{1,0:T(8,128)(2,1)S(1)}, u32[]{:S(2)}, u32[]{:S(2)}) collective-permute-start(bf16[64,1152]{1,0:T(8,128)(2,1)S(1)} %pad_maximum_fusion.3), channel_id=1, source_target_pairs={{0,1},{1,2},{2,3},{3,4},{4,5},{5,6},{6,7},{7,8},{8,9},{9,10},{10,1... | collective-permute-start | bytes 442376 | tf_op jit(solution)/shard_map/ppermute | solution.py:436
  10.7 29.9 %all-to-all-start = ((f32[32,24,256]{2,1,0:T(8,128)}), f32[32,24,256]{2,1,0:T(8,128)S(1)}, u32[]{:S(2)}, u32[]{:S(2)}) async-start(f32[32,24,256]{2,1,0:T(8,128)} %get-tuple-element.69), calls=%async_computation | async-start | bytes 1572864 | tf_op jit(solution)/shard_map/all_to_all | solution.py:383
  21.0 7.1 %copy-start.8 = (s32[256]{0:T(256)}, s32[256]{0:T(256)S(1)}, u32[]{:S(2)}) copy-start(s32[256]{0:T(256)S(1)} %pad_add_fusion.seg_ref) | copy-start | bytes 3076
  40.7 0.9 copy-start.2
  43.7 21.2 %all-to-all-start.1 = ((f32[32,24,256]{2,1,0:T(8,128)}), f32[32,24,256]{2,1,0:T(8,128)S(1)}, u32[]{:S(2)}, u32[]{:S(2)}) async-start(f32[32,24,256]{2,1,0:T(8,128)} %scan.2), calls=%async_computation.1 | async-start | bytes 1572864 | tf_op jit(solution)/shard_map/all_to_all | solution.py:383
  64.9 0.9 copy-start.4
  94.4 19.5 %all-to-all-start.2 = ((f32[32,24,256]{2,1,0:T(8,128)}), f32[32,24,256]{2,1,0:T(8,128)S(1)}, u32[]{:S(2)}, u32[]{:S(2)}) async-start(f32[32,24,256]{2,1,0:T(8,128)} %get-tuple-element.99), calls=%async_computation.2 | async-start | bytes 1572864 | tf_op jit(solution)/shard_map/all_to_all | solution.py:383
  113.8 0.9 copy-start.5
  114.7 9.5 %copy-start = (f32[4,4,128,128]{3,2,1,0:T(8,128)S(1)}, f32[4,4,128,128]{3,2,1,0:T(8,128)}, u32[]{:S(2)}) copy-start(f32[4,4,128,128]{3,2,1,0:T(8,128)} %get-tuple-element.121) | copy-start | bytes 3145732
  116.9 7.3 %collective-permute-start.1 = (f32[4,4,128,128]{3,2,1,0:T(8,128)}, f32[4,4,128,128]{3,2,1,0:T(8,128)S(1)}, u32[]{:S(2)}, u32[]{:S(2)}) collective-permute-start(f32[4,4,128,128]{3,2,1,0:T(8,128)} %get-tuple-element.113), channel_id=1, source_target_pairs={{0,1},{1,0},{2,3},{3,2},{4,5},{5,4},{6,7},{7,6},{8,9},{9,8},{10,11... | collective-permute-start | bytes 3145736 | tf_op jit(solution)/shard_map/ppermute | solution.py:628
  117.6 27.7 %all-to-all-start.3 = ((f32[32,24,256]{2,1,0:T(8,128)}), f32[32,24,256]{2,1,0:T(8,128)S(1)}, u32[]{:S(2)}, u32[]{:S(2)}) async-start(f32[32,24,256]{2,1,0:T(8,128)} %scan.3), calls=%async_computation.3 | async-start | bytes 1572864 | tf_op jit(solution)/shard_map/all_to_all | solution.py:383
  125.2 27.2 %collective-permute-start.2 = (f32[4,128,128]{2,1,0:T(8,128)}, f32[4,128,128]{2,1,0:T(8,128)}, u32[]{:S(2)}, u32[]{:S(2)}) collective-permute-start(f32[4,128,128]{2,1,0:T(8,128)} %get-tuple-element.136), channel_id=1, source_target_pairs={{0,4},{1,5},{2,6},{3,7},{4,0},{5,1},{6,2},{7,3},{8,12},{9,13},{10,... | collective-permute-start | bytes 786440 | tf_op jit(solution)/shard_map/ppermute | solution.py:624
  128.5 23.9 %collective-permute-start.3 = (f32[4,128,128]{2,1,0:T(8,128)}, f32[4,128,128]{2,1,0:T(8,128)}, u32[]{:S(2)}, u32[]{:S(2)}) collective-permute-start(f32[4,128,128]{2,1,0:T(8,128)} %get-tuple-element.135), channel_id=1, source_target_pairs={{0,2},{1,3},{2,4},{3,5},{4,6},{5,7},{6,0},{7,1},{8,10},{9,11},{10,... | collective-permute-start | bytes 786440 | tf_op jit(solution)/shard_map/ppermute | solution.py:624
  129.0 23.4 %collective-permute-start.4 = (f32[4,128,128]{2,1,0:T(8,128)S(1)}, f32[4,128,128]{2,1,0:T(8,128)}, u32[]{:S(2)}, u32[]{:S(2)}) collective-permute-start(f32[4,128,128]{2,1,0:T(8,128)S(1)} %get-tuple-element.134), channel_id=1, source_target_pairs={{0,6},{1,7},{2,0},{3,1},{4,2},{5,3},{6,4},{7,5},{8,14},{9,15},{10,... | collective-permute-start | bytes 786440 | tf_op jit(solution)/shard_map/ppermute | solution.py:624
  145.2 0.9 copy-start.3
  145.3 16.9 %collective-permute-start.9 = (f32[4,4,128,128]{3,2,1,0:T(8,128)}, f32[4,4,128,128]{3,2,1,0:T(8,128)}, u32[]{:S(2)}, u32[]{:S(2)}) collective-permute-start(f32[4,4,128,128]{3,2,1,0:T(8,128)} %get-tuple-element.126), channel_id=1, source_target_pairs={{0,1},{1,0},{2,3},{3,2},{4,5},{5,4},{6,7},{7,6},{8,9},{9,8},{10,11... | collective-permute-start | bytes 3145736 | tf_op jit(solution)/shard_map/ppermute | solution.py:628
  146.1 16.9 %copy-start.1 = (f32[4,4,128,128]{3,2,1,0:T(8,128)S(1)}, f32[4,4,128,128]{3,2,1,0:T(8,128)}, u32[]{:S(2)}) copy-start(f32[4,4,128,128]{3,2,1,0:T(8,128)} %get-tuple-element.127) | copy-start | bytes 3145732
  154.5 6.7 %collective-permute-start.8 = (f32[256,128]{1,0:T(8,128)S(1)}, f32[256,128]{1,0:T(8,128)S(1)}, u32[]{:S(2)}, u32[]{:S(2)}) collective-permute-start(f32[256,128]{1,0:T(8,128)S(1)} %dynamic-slice_bitcast_fusion), channel_id=1, source_target_pairs={{0,1},{1,0},{2,3},{3,2},{4,5},{5,4},{6,7},{7,6},{8,9},{9,8},{10,11... | collective-permute-start | bytes 393224 | tf_op jit(solution)/shard_map/ppermute | solution.py:628
  154.9 10.3 %collective-permute-start.5 = (f32[128,128]{1,0:T(8,128)S(1)}, f32[128,128]{1,0:T(8,128)S(1)}, u32[]{:S(2)}, u32[]{:S(2)}) collective-permute-start(f32[128,128]{1,0:T(8,128)S(1)} %get-tuple-element.141), channel_id=1, source_target_pairs={{0,16},{1,17},{2,18},{3,19},{4,20},{5,21},{6,22},{7,23},{8,24},{9,... | collective-permute-start | bytes 196616 | tf_op jit(solution)/shard_map/ppermute | solution.py:624
  158.0 9.7 %collective-permute-start.6 = (f32[128,128]{1,0:T(8,128)S(1)}, f32[128,128]{1,0:T(8,128)S(1)}, u32[]{:S(2)}, u32[]{:S(2)}) collective-permute-start(f32[128,128]{1,0:T(8,128)S(1)} %get-tuple-element.140), channel_id=1, source_target_pairs={{0,8},{1,9},{2,10},{3,11},{4,12},{5,13},{6,14},{7,15},{8,16},{9,17... | collective-permute-start | bytes 196616 | tf_op jit(solution)/shard_map/ppermute | solution.py:624
  158.6 9.1 %collective-permute-start.7 = (f32[128,128]{1,0:T(8,128)S(1)}, f32[128,128]{1,0:T(8,128)S(1)}, u32[]{:S(2)}, u32[]{:S(2)}) collective-permute-start(f32[128,128]{1,0:T(8,128)S(1)} %get-tuple-element.139), channel_id=1, source_target_pairs={{0,24},{1,25},{2,26},{3,27},{4,28},{5,29},{6,30},{7,31},{8,0},{9,1... | collective-permute-start | bytes 196616 | tf_op jit(solution)/shard_map/ppermute | solution.py:624
  162.1 8.0 %collective-permute-start.19 = (f32[256,128]{1,0:T(8,128)S(1)}, f32[256,128]{1,0:T(8,128)S(1)}, u32[]{:S(2)}, u32[]{:S(2)}) collective-permute-start(f32[256,128]{1,0:T(8,128)S(1)} %bitcast_add_fusion.2), channel_id=1, source_target_pairs={{0,4},{1,5},{2,6},{3,7},{4,0},{5,1},{6,2},{7,3},{8,12},{9,13},{10,... | collective-permute-start | bytes 393224 | tf_op jit(solution)/shard_map/ppermute | solution.py:613
  162.2 9.1 %collective-permute-start.20 = (f32[256,128]{1,0:T(8,128)S(1)}, f32[256,128]{1,0:T(8,128)S(1)}, u32[]{:S(2)}, u32[]{:S(2)}) collective-permute-start(f32[256,128]{1,0:T(8,128)S(1)} %bitcast_add_fusion.2), channel_id=1, source_target_pairs={{0,2},{1,3},{2,4},{3,5},{4,6},{5,7},{6,0},{7,1},{8,10},{9,11},{10,... | collective-permute-start | bytes 393224 | tf_op jit(solution)/shard_map/ppermute | solution.py:613
  165.2 6.1 %collective-permute-start.21 = (f32[256,128]{1,0:T(8,128)S(1)}, f32[256,128]{1,0:T(8,128)S(1)}, u32[]{:S(2)}, u32[]{:S(2)}) collective-permute-start(f32[256,128]{1,0:T(8,128)S(1)} %bitcast_add_fusion.2), channel_id=1, source_target_pairs={{0,6},{1,7},{2,0},{3,1},{4,2},{5,3},{6,4},{7,5},{8,14},{9,15},{10,... | collective-permute-start | bytes 393224 | tf_op jit(solution)/shard_map/ppermute | solution.py:613
  167.7 9.2 %collective-permute-start.12 = (f32[4,128,128]{2,1,0:T(8,128)S(1)}, f32[4,128,128]{2,1,0:T(8,128)S(1)}, u32[]{:S(2)}, u32[]{:S(2)}) collective-permute-start(f32[4,128,128]{2,1,0:T(8,128)S(1)} %add_bitcast_fusion), channel_id=1, source_target_pairs={{0,24},{1,25},{2,26},{3,27},{4,28},{5,29},{6,30},{7,31},{8,0},{9,1... | collective-permute-start | bytes 786440 | tf_op jit(solution)/shard_map/ppermute | solution.py:624
  167.7 12.3 %collective-permute-start.10 = (f32[4,128,128]{2,1,0:T(8,128)S(1)}, f32[4,128,128]{2,1,0:T(8,128)S(1)}, u32[]{:S(2)}, u32[]{:S(2)}) collective-permute-start(f32[4,128,128]{2,1,0:T(8,128)S(1)} %get-tuple-element.133), channel_id=1, source_target_pairs={{0,16},{1,17},{2,18},{3,19},{4,20},{5,21},{6,22},{7,23},{8,24},{9,... | collective-permute-start | bytes 786440 | tf_op jit(solution)/shard_map/ppermute | solution.py:624
  170.1 12.0 %collective-permute-start.11 = (f32[4,128,128]{2,1,0:T(8,128)S(1)}, f32[4,128,128]{2,1,0:T(8,128)S(1)}, u32[]{:S(2)}, u32[]{:S(2)}) collective-permute-start(f32[4,128,128]{2,1,0:T(8,128)S(1)} %get-tuple-element.132), channel_id=1, source_target_pairs={{0,8},{1,9},{2,10},{3,11},{4,12},{5,13},{6,14},{7,15},{8,16},{9,17... | collective-permute-start | bytes 786440 | tf_op jit(solution)/shard_map/ppermute | solution.py:624
  171.3 13.9 %collective-permute-start.22 = (f32[256,128]{1,0:T(8,128)S(1)}, f32[256,128]{1,0:T(8,128)S(1)}, u32[]{:S(2)}, u32[]{:S(2)}) collective-permute-start(f32[256,128]{1,0:T(8,128)S(1)} %add_add_fusion.2), channel_id=1, source_target_pairs={{0,64},{32,96},{64,0},{96,32},{1,65},{33,97},{65,1},{97,33},{2,66}... | collective-permute-start | bytes 393224 | tf_op jit(solution)/shard_map/ppermute | solution.py:613
  174.6 13.9 %collective-permute-start.23 = (f32[256,128]{1,0:T(8,128)S(1)}, f32[256,128]{1,0:T(8,128)S(1)}, u32[]{:S(2)}, u32[]{:S(2)}) collective-permute-start(f32[256,128]{1,0:T(8,128)S(1)} %add_add_fusion.2), channel_id=1, source_target_pairs={{0,32},{32,64},{64,96},{96,0},{1,33},{33,65},{65,97},{97,1},{2,34}... | collective-permute-start | bytes 393224 | tf_op jit(solution)/shard_map/ppermute | solution.py:613
  176.9 11.5 %collective-permute-start.24 = (f32[256,128]{1,0:T(8,128)S(1)}, f32[256,128]{1,0:T(8,128)S(1)}, u32[]{:S(2)}, u32[]{:S(2)}) collective-permute-start(f32[256,128]{1,0:T(8,128)S(1)} %add_add_fusion.2), channel_id=1, source_target_pairs={{0,96},{32,0},{64,32},{96,64},{1,97},{33,1},{65,33},{97,65},{2,98}... | collective-permute-start | bytes 393224 | tf_op jit(solution)/shard_map/ppermute | solution.py:613
  183.2 7.3 %collective-permute-start.13 = (f32[128,128]{1,0:T(8,128)S(1)}, f32[128,128]{1,0:T(8,128)S(1)}, u32[]{:S(2)}, u32[]{:S(2)}) collective-permute-start(f32[128,128]{1,0:T(8,128)S(1)} %get-tuple-element.144), channel_id=1, source_target_pairs={{0,4},{1,5},{2,6},{3,7},{4,0},{5,1},{6,2},{7,3},{8,12},{9,13},{10,... | collective-permute-start | bytes 196616 | tf_op jit(solution)/shard_map/ppermute | solution.py:624
  185.2 7.7 %collective-permute-start.14 = (f32[128,128]{1,0:T(8,128)S(1)}, f32[128,128]{1,0:T(8,128)S(1)}, u32[]{:S(2)}, u32[]{:S(2)}) collective-permute-start(f32[128,128]{1,0:T(8,128)S(1)} %get-tuple-element.143), channel_id=1, source_target_pairs={{0,2},{1,3},{2,4},{3,5},{4,6},{5,7},{6,0},{7,1},{8,10},{9,11},{10,... | collective-permute-start | bytes 196616 | tf_op jit(solution)/shard_map/ppermute | solution.py:624
  185.2 7.7 %collective-permute-start.15 = (f32[128,128]{1,0:T(8,128)S(1)}, f32[128,128]{1,0:T(8,128)S(1)}, u32[]{:S(2)}, u32[]{:S(2)}) collective-permute-start(f32[128,128]{1,0:T(8,128)S(1)} %get-tuple-element.142), channel_id=1, source_target_pairs={{0,6},{1,7},{2,0},{3,1},{4,2},{5,3},{6,4},{7,5},{8,14},{9,15},{10,... | collective-permute-start | bytes 196616 | tf_op jit(solution)/shard_map/ppermute | solution.py:624
  188.5 8.4 %collective-permute-start.25 = (f32[256,128]{1,0:T(8,128)S(1)}, f32[256,128]{1,0:T(8,128)S(1)}, u32[]{:S(2)}, u32[]{:S(2)}) collective-permute-start(f32[256,128]{1,0:T(8,128)S(1)} %add_add_fusion.1), channel_id=1, source_target_pairs={{0,16},{1,17},{2,18},{3,19},{4,20},{5,21},{6,22},{7,23},{8,24},{9,... | collective-permute-start | bytes 393224 | tf_op jit(solution)/shard_map/ppermute | solution.py:613
  189.7 9.8 %collective-permute-start.26 = (f32[256,128]{1,0:T(8,128)S(1)}, f32[256,128]{1,0:T(8,128)S(1)}, u32[]{:S(2)}, u32[]{:S(2)}) collective-permute-start(f32[256,128]{1,0:T(8,128)S(1)} %add_add_fusion.1), channel_id=1, source_target_pairs={{0,8},{1,9},{2,10},{3,11},{4,12},{5,13},{6,14},{7,15},{8,16},{9,17... | collective-permute-start | bytes 393224 | tf_op jit(solution)/shard_map/ppermute | solution.py:613
  190.5 9.0 %collective-permute-start.27 = (f32[256,128]{1,0:T(8,128)S(1)}, f32[256,128]{1,0:T(8,128)S(1)}, u32[]{:S(2)}, u32[]{:S(2)}) collective-permute-start(f32[256,128]{1,0:T(8,128)S(1)} %add_add_fusion.1), channel_id=1, source_target_pairs={{0,24},{1,25},{2,26},{3,27},{4,28},{5,29},{6,30},{7,31},{8,0},{9,1... | collective-permute-start | bytes 393224 | tf_op jit(solution)/shard_map/ppermute | solution.py:613
  193.0 7.3 %collective-permute-start.16 = (f32[2,128,128]{2,1,0:T(8,128)S(1)}, f32[2,128,128]{2,1,0:T(8,128)S(1)}, u32[]{:S(2)}, u32[]{:S(2)}) collective-permute-start(f32[2,128,128]{2,1,0:T(8,128)S(1)} %pad_maximum_fusion.4), channel_id=1, source_target_pairs={{0,64},{32,96},{64,0},{96,32},{1,65},{33,97},{65,1},{97,33},{2,66}... | collective-permute-start | bytes 393224 | tf_op jit(solution)/shard_map/ppermute | solution.py:613
  196.3 6.2 %collective-permute-start.17 = (f32[2,128,128]{2,1,0:T(8,128)S(1)}, f32[2,128,128]{2,1,0:T(8,128)S(1)}, u32[]{:S(2)}, u32[]{:S(2)}) collective-permute-start(f32[2,128,128]{2,1,0:T(8,128)S(1)} %pad_maximum_fusion.4), channel_id=1, source_target_pairs={{0,32},{32,64},{64,96},{96,0},{1,33},{33,65},{65,97},{97,1},{2,34}... | collective-permute-start | bytes 393224 | tf_op jit(solution)/shard_map/ppermute | solution.py:613
  197.0 5.5 %collective-permute-start.18 = (f32[2,128,128]{2,1,0:T(8,128)S(1)}, f32[2,128,128]{2,1,0:T(8,128)S(1)}, u32[]{:S(2)}, u32[]{:S(2)}) collective-permute-start(f32[2,128,128]{2,1,0:T(8,128)S(1)} %pad_maximum_fusion.4), channel_id=1, source_target_pairs={{0,96},{32,0},{64,32},{96,64},{1,97},{33,1},{65,33},{97,65},{2,98}... | collective-permute-start | bytes 393224 | tf_op jit(solution)/shard_map/ppermute | solution.py:613
  199.6 3.7 %collective-permute-start.28 = (f32[256,128]{1,0:T(8,128)S(1)}, f32[256,128]{1,0:T(8,128)S(1)}, u32[]{:S(2)}, u32[]{:S(2)}) collective-permute-start(f32[256,128]{1,0:T(8,128)S(1)} %add_add_fusion), channel_id=1, source_target_pairs={{0,1},{1,0},{2,3},{3,2},{4,5},{5,4},{6,7},{7,6},{8,9},{9,8},{10,11... | collective-permute-start | bytes 393224 | tf_op jit(solution)/shard_map/ppermute | solution.py:663

commit v4 on v3

--- a/solution.py
+++ b/solution.py
@@ -629,7 +629,11 @@
 
     def second_half(done):
         first, right = lax.optimization_barrier((over_chip(*done[0]), done[1]))
-        return query(1, right, 0, groups), slice_around("z", 0, *first)
+        some = query(1, right, 0, groups // 2)
+        first, some, right = lax.optimization_barrier(
+            (slice_around("z", 0, *first), some, right)
+        )
+        return query(1, right, groups // 2, groups - groups // 2, some), first
 
     later, second, first = across(
         grad_pieces, True, lambda: (query(0, right, 0, groups), right), second_half
@@ -656,8 +660,8 @@
     key_mine, key_theirs = over_chip(key_mine, key_theirs)
     second = over_chip(*second)
     key_sum, second = lax.optimization_barrier((key_mine + key_theirs, second))
-    key_sum = around("x", around("dp", around("z", key_sum)))
-    second = slice_around("z", 0, slice_around("x", 1, *second))
+    key_sum = around("z", around("dp", around("x", key_sum)))
+    second = slice_around("x", 0, slice_around("z", 0, *second))
     first = slice_around("x", 0, first)
     both = around("dp", jnp.stack([first, second], 0))
     key_theirs = lax.ppermute(key_sum, "ctx", partner)

time: 206 us -> 215 us (1.044)
  waiting for transfers between devices: 10.9 us -> 19.6 us
  other arithmetic: 10 us -> 6.21 us
  starting transfers between devices: 73 us -> 75.2 us
    ppermute x12, waiting for transfers between devices: 3.85 us -> 11 us  [slice_around(): lax.ppermute(part, 'ctx', route)]
    ppermute x12, starting transfers between devices: 19.6 us -> 23.1 us  [slice_around(): lax.ppermute(part, 'ctx', route)]
    add x3 -> x2, other arithmetic: 2.99 us -> 0.17 us  [slice_around(): sum((lax.dynamic_index_in_dim(value, lax.rem(place[axis] + s, RING), dim,...]
    pallas_call x10 -> x11, Pallas kernels: 102 us -> 104 us  [call(): pl.pallas_call(kernel, grid_spec=pltpu.PrefetchScalarGridSpec(num_scalar_...]
  transfers between devices with their start and end apart: 33 -> 33, of which waited for: 8 -> 13; matrix products, arithmetic and copies ran while one was open for 5% -> 3% of each run, Pallas kernels for 31% -> 31%
where the time goes in v4:
time: 215 us; the launch traced here: 213 us
  Pallas kernels  104 us (48%)
  starting transfers between devices  75.2 us (35%)
  waiting for transfers between devices  19.6 us (9%)
  local copies, waits for them, and re-layouts  7.24 us (3%)
  other arithmetic  6.21 us (3%)
    pallas_call x11, Pallas kernels, call(): pl.pallas_call(kernel, grid_spec=pltpu.PrefetchScalarGridSpec(num_scalar_...  104 us
    all_to_all x4, starting transfers between devices, exchange(): return lax.all_to_all(pieces, axis, 0, 0, tiled=True)  29.7 us
    ppermute x12, starting transfers between devices, slice_around(): lax.ppermute(part, 'ctx', route)  23.1 us
    ppermute x12, starting transfers between devices, around(): lax.ppermute(value, name, route)  19.9 us
    ppermute x12, waiting for transfers between devices, slice_around(): lax.ppermute(part, 'ctx', route)  11 us
    ppermute x12, waiting for transfers between devices, around(): lax.ppermute(value, name, route)  6.59 us
    unnamed x22, local copies, waits for them, and re-layouts  4.64 us
  transfers between devices with their start and end apart: 33, of which 13 were waited for; matrix products, arithmetic and copies ran while one was open for 3% of the time, Pallas kernels for 31%

profile of v4, /device:TPU:0, one launch (start us, length us, event | category | flops | bytes accessed | tf_op | source)
XLA Modules:
  0.0 212.8 jit_solution(9717609569400577989)
XLA Ops:
  1.8 1.3 reduce.5
  3.9 5.4 %block.1 = (f32[4,3,136,256]{3,2,1,0:T(8,128)}, f32[32,24,256]{2,1,0:T(8,128)}) custom-call(s32[192]{0:T(256)} %bitcast.95, bf16[192,512]{1,0:T(8,128)(2,1)} %bitcast.88, bf16[192,512]{1,0:T(8,128)(2,1)} %bitcast.85, bf16[4,128,128]{2,1,0:T(8,128)(2,1)} %map_ref.5, s32[3,1,256]{2,1,0:T(1,128)} %tile.12.seg_row_ref), custom_call_target="tpu_custom_call" | custom-call | flops 4000000000 | bytes 12000000 | tf_op jit(solution)/shard_map/block/pallas_call | solution.py:363
  9.4 1.3 collective-permute-start
  10.7 10.0 %all-to-all-start = ((f32[32,24,256]{2,1,0:T(8,128)}), f32[32,24,256]{2,1,0:T(8,128)S(1)}, u32[]{:S(2)}, u32[]{:S(2)}) async-start(f32[32,24,256]{2,1,0:T(8,128)} %get-tuple-element.75), calls=%async_computation | async-start | bytes 1572864 | tf_op jit(solution)/shard_map/all_to_all | solution.py:383
  21.0 0.8 copy.17.seg_col_ref
  21.8 0.8 pad_maximum_fusion
  22.6 5.5 %keys.1 = (bf16[4,256,256]{2,1,0:T(8,128)(2,1)}, bf16[4,256,256]{2,1,0:T(8,128)(2,1)}, bf16[4,3,256,256]{3,2,1,0:T(8,128)(2,1)}, bf16[4,3,128,256]{3,2,1,0:T(8,1...) custom-call(s32[4]{0:T(128)} %window_ref.1, bf16[256,512]{1,0:T(8,128)(2,1)} %get-tuple-element.160.key_ref, ...), custom_call_target="tpu_custom_call" | custom-call | flops 5000000000 | bytes 15000000 | tf_op jit(solution)/shard_map/keys/pallas_call | solution.py:363
  28.1 12.5 %local.2 = (f32[16,3,128,256]{3,2,1,0:T(8,128)}, f32[16,3,1,256]{3,2,1,0:T(1,128)}, bf16[16,3,256,256]{3,2,1,0:T(8,128)(2,1)}, bf16[16,3,256,256]{3,2,1,0:T(8,128)(2,1)}) custom-call(bf16[192,8192]{1,0:T(8,128)(2,1)} %bitcast.65, bf16[192,8192]{1,0:T(8,128)(2,1)} %bitcast.66, bf16[192,8192]{1,0:T(8,128)(2,1)} %bitcast.67, bf16[192,8192]{1,0:T(8,128)(2,1)} %bitcast.68, ...), custom_call_target="tpu_custom_call" | custom-call | flops 15000000512 | bytes 45000000 | tf_op jit(solution)/shard_map/local/pallas_call | solution.py:363
  40.7 0.9 copy-done.3
  41.6 2.1 scan.2
  43.7 7.4 %all-to-all-start.1 = ((f32[32,24,256]{2,1,0:T(8,128)}), f32[32,24,256]{2,1,0:T(8,128)S(1)}, u32[]{:S(2)}, u32[]{:S(2)}) async-start(f32[32,24,256]{2,1,0:T(8,128)} %scan.2), calls=%async_computation.1 | async-start | bytes 1572864 | tf_op jit(solution)/shard_map/all_to_all | solution.py:383
  51.1 12.0 %local.3 = (f32[16,3,128,256]{3,2,1,0:T(8,128)}, f32[16,3,1,256]{3,2,1,0:T(1,128)}, bf16[16,3,256,256]{3,2,1,0:T(8,128)(2,1)}, bf16[16,3,256,256]{3,2,1,0:T(8,128)(2,1)}) custom-call(bf16[192,8192]{1,0:T(8,128)(2,1)} %bitcast.69, bf16[192,8192]{1,0:T(8,128)(2,1)} %bitcast.70, ...), custom_call_target="tpu_custom_call", output_to_operand_aliasing={{0}: (13, {}), {1}: (14, {}), {2}: (15, {}), {3}: (16, {})} | custom-call | flops 15000000512 | bytes 45000000 | tf_op jit(solution)/shard_map/local/pallas_call | solution.py:363
  63.2 1.8 all-to-all-done.1.first_ref
  65.0 0.9 copy-done.4
  65.9 28.6 %outputs.1 = (bf16[16,3,512,256]{3,2,1,0:T(8,128)(2,1)}, f32[16,3,1,256]{3,2,1,0:T(1,128)}, f32[4,3,128,256]{3,2,1,0:T(8,128)}, f32[4,3,136,256]{3,2,1,0:T(8,128...) custom-call(s32[256]{0:T(256)} %copy-done.8, bf16[192,8192]{1,0:T(8,128)(2,1)} %bitcast.97, ...), custom_call_target="tpu_custom_call" | custom-call | flops 44999999488 | bytes 135000000 | tf_op jit(solution)/shard_map/outputs/pallas_call | solution.py:363
  94.4 5.6 %all-to-all-start.2 = ((f32[32,24,256]{2,1,0:T(8,128)}), f32[32,24,256]{2,1,0:T(8,128)S(1)}, u32[]{:S(2)}, u32[]{:S(2)}) async-start(f32[32,24,256]{2,1,0:T(8,128)} %get-tuple-element.105), calls=%async_computation.2 | async-start | bytes 1572864 | tf_op jit(solution)/shard_map/all_to_all | solution.py:383
  100.0 13.6 %queries.3 = (f32[4,4,128,128]{3,2,1,0:T(8,128)}, f32[4,4,128,128]{3,2,1,0:T(8,128)}) custom-call(s32[1]{0:T(128)} %bitcast.7.core_ref, bf16[192,8192]{1,0:T(8,128)(2,1)} %bitcast.73, bf16[192,8192]{1,0:T(8,128)(2,1)} %bitcast.74, bf16[192,8192]{1,0:T(8,128)(2,1)} %bitcast.75, bf16[192,8192]{1,0:T(8,128)(2,1)} %bitcast.76, ...), custom_call_target="tpu_custom_call" | custom-call | flops 10000000000 | bytes 30000000 | tf_op jit(solution)/shard_map/queries/pallas_call | solution.py:363
  113.9 0.9 copy-done.5
  114.8 2.2 %scan.3 = f32[32,24,256]{2,1,0:T(8,128)} custom-call(f32[32,24,256]{2,1,0:T(8,128)} %copy-done.5), custom_call_target="tpu_custom_call" | custom-call | flops 2000000000 | bytes 6000000 | tf_op jit(solution)/shard_map/scan/pallas_call | solution.py:363
  117.7 6.7 %all-to-all-start.3 = ((f32[32,24,256]{2,1,0:T(8,128)}), f32[32,24,256]{2,1,0:T(8,128)S(1)}, u32[]{:S(2)}, u32[]{:S(2)}) async-start(f32[32,24,256]{2,1,0:T(8,128)} %scan.3), calls=%async_computation.3 | async-start | bytes 1572864 | tf_op jit(solution)/shard_map/all_to_all | solution.py:383
  124.5 3.4 %collective-permute-start.2 = (f32[4,128,128]{2,1,0:T(8,128)S(1)}, f32[4,128,128]{2,1,0:T(8,128)S(1)}, u32[]{:S(2)}, u32[]{:S(2)}) collective-permute-start(f32[4,128,128]{2,1,0:T(8,128)S(1)} %get-tuple-element.149), channel_id=1, source_target_pairs={{0,4},{1,5},{2,6},{3,7},{4,0},{5,1},{6,2},{7,3},{8,12},{9,13},{10,... | collective-permute-start | bytes 786440 | tf_op jit(solution)/shard_map/ppermute | solution.py:624
  128.4 2.7 %collective-permute-start.4 = (f32[4,128,128]{2,1,0:T(8,128)S(1)}, f32[4,128,128]{2,1,0:T(8,128)}, u32[]{:S(2)}, u32[]{:S(2)}) collective-permute-start(f32[4,128,128]{2,1,0:T(8,128)S(1)} %get-tuple-element.147), channel_id=1, source_target_pairs={{0,6},{1,7},{2,0},{3,1},{4,2},{5,3},{6,4},{7,5},{8,14},{9,15},{10,... | collective-permute-start | bytes 786440 | tf_op jit(solution)/shard_map/ppermute | solution.py:624
  131.1 7.7 %queries.4 = (f32[4,4,128,128]{3,2,1,0:T(8,128)}, f32[4,4,128,128]{3,2,1,0:T(8,128)}) custom-call(s32[1]{0:T(128)} %bitcast.7.core_ref, bf16[192,8192]{1,0:T(8,128)(2,1)} %bitcast.77, bf16[192,8192]{1,0:T(8,128)(2,1)} %bitcast.78, bf16[192,8192]{1,0:T(8,128)(2,1)} %bitcast.79, bf16[192,8192]{1,0:T(8,128)(2,1)} %bitcast.80, ...), custom_call_target="tpu_custom_call" | custom-call | flops 5000000000 | bytes 15000000 | tf_op jit(solution)/shard_map/queries/pallas_call | solution.py:363
  138.8 4.8 %collective-permute-done.2 = f32[4,128,128]{2,1,0:T(8,128)S(1)} collective-permute-done((f32[4,128,128]{2,1,0:T(8,128)S(1)}, f32[4,128,128]{2,1,0:T(8,128)S(1)}, u32[]{:S(2)}, u32[]{:S(2)}) %collective-permute-start.2) | collective-permute-done | bytes 262176 | tf_op jit(solution)/shard_map/ppermute | solution.py:624
  143.5 4.7 %collective-permute-done.3 = f32[4,128,128]{2,1,0:T(8,128)} collective-permute-done((f32[4,128,128]{2,1,0:T(8,128)S(1)}, f32[4,128,128]{2,1,0:T(8,128)}, u32[]{:S(2)}, u32[]{:S(2)}) %collective-permute-start.3) | collective-permute-done | bytes 262176 | tf_op jit(solution)/shard_map/ppermute | solution.py:624
  148.3 1.1 fusion.1
  149.4 7.7 %queries.5 = (f32[4,4,128,128]{3,2,1,0:T(8,128)}, f32[4,4,128,128]{3,2,1,0:T(8,128)}) custom-call(s32[1]{0:T(128)} %bitcast.7.core_ref, bf16[192,8192]{1,0:T(8,128)(2,1)} %bitcast.81, bf16[192,8192]{1,0:T(8,128)(2,1)} %bitcast.82, bf16[192,8192]{1,0:T(8,128)(2,1)} %bitcast.83, ...), custom_call_target="tpu_custom_call", output_to_operand_aliasing={{0}: (12, {}), {1}: (13, {})} | custom-call | flops 5000000000 | bytes 15000000 | tf_op jit(solution)/shard_map/queries/pallas_call | solution.py:363
  158.0 6.2 %tail.1 = f32[4,128,128]{2,1,0:T(8,128)} custom-call(s32[256]{0:T(256)} %copy-done.8, bf16[256,512]{1,0:T(8,128)(2,1)} %get-tuple-element.160.key_ref, bf16[256,512]{1,0:T(8,128)(2,1)} %get-tuple-element.161.value_ref, bf16[4,128,128]{2,1,0:T(8,128)(2,1)} %map_ref.5, s32[256,1]{1,0:T(8,128)} %copy.17.seg_col_ref, f32[32,24,256]{2,1,0:T(8,128)} %copy-done.2, ...), custom_call_target="tpu_custom_call" | custom-call | flops 5000000000 | bytes 15000000 | tf_op jit(solution)/shard_map/tail/pallas_call | solution.py:363
  164.2 0.9 dynamic-slice_bitcast_fusion
  165.4 3.0 %collective-permute-start.5 = (f32[128,128]{1,0:T(8,128)S(1)}, f32[128,128]{1,0:T(8,128)S(1)}, u32[]{:S(2)}, u32[]{:S(2)}) collective-permute-start(f32[128,128]{1,0:T(8,128)S(1)} %get-tuple-element.154), channel_id=1, source_target_pairs={{0,16},{1,17},{2,18},{3,19},{4,20},{5,21},{6,22},{7,23},{8,24},{9,... | collective-permute-start | bytes 196616 | tf_op jit(solution)/shard_map/ppermute | solution.py:624
  169.0 2.6 %collective-permute-start.7 = (f32[128,128]{1,0:T(8,128)S(1)}, f32[128,128]{1,0:T(8,128)S(1)}, u32[]{:S(2)}, u32[]{:S(2)}) collective-permute-start(f32[128,128]{1,0:T(8,128)S(1)} %get-tuple-element.152), channel_id=1, source_target_pairs={{0,24},{1,25},{2,26},{3,27},{4,28},{5,29},{6,30},{7,31},{8,0},{9,1... | collective-permute-start | bytes 196616 | tf_op jit(solution)/shard_map/ppermute | solution.py:624
  171.6 0.9 bitcast_add_fusion.2
  172.6 3.2 %collective-permute-start.21 = (f32[256,128]{1,0:T(8,128)S(1)}, f32[256,128]{1,0:T(8,128)S(1)}, u32[]{:S(2)}, u32[]{:S(2)}) collective-permute-start(f32[256,128]{1,0:T(8,128)S(1)} %bitcast_add_fusion.2), channel_id=1, source_target_pairs={{0,24},{1,25},{2,26},{3,27},{4,28},{5,29},{6,30},{7,31},{8,0},{9,1... | collective-permute-start | bytes 393224 | tf_op jit(solution)/shard_map/ppermute | solution.py:613
  176.1 1.5 collective-permute-start.10
  177.8 1.0 collective-permute-done.20
  178.8 2.0 collective-permute-start.12
  180.9 1.6 collective-permute-done.19
  182.6 1.6 collective-permute-start.23
  184.2 1.7 collective-permute-start.24
  185.9 1.1 collective-permute-done.10
  186.9 3.2 %collective-permute-start.22 = (f32[256,128]{1,0:T(8,128)S(1)}, f32[256,128]{1,0:T(8,128)S(1)}, u32[]{:S(2)}, u32[]{:S(2)}) collective-permute-start(f32[256,128]{1,0:T(8,128)S(1)} %add_add_fusion.2), channel_id=1, source_target_pairs={{0,64},{32,96},{64,0},{96,32},{1,65},{33,97},{65,1},{97,33},{2,66}... | collective-permute-start | bytes 393224 | tf_op jit(solution)/shard_map/ppermute | solution.py:613
  190.6 3.2 %collective-permute-start.13 = (f32[128,128]{1,0:T(8,128)S(1)}, f32[128,128]{1,0:T(8,128)S(1)}, u32[]{:S(2)}, u32[]{:S(2)}) collective-permute-start(f32[128,128]{1,0:T(8,128)S(1)} %get-tuple-element.157), channel_id=1, source_target_pairs={{0,16},{1,17},{2,18},{3,19},{4,20},{5,21},{6,22},{7,23},{8,24},{9,... | collective-permute-start | bytes 196616 | tf_op jit(solution)/shard_map/ppermute | solution.py:624
  193.9 3.2 %collective-permute-start.15 = (f32[128,128]{1,0:T(8,128)S(1)}, f32[128,128]{1,0:T(8,128)S(1)}, u32[]{:S(2)}, u32[]{:S(2)}) collective-permute-start(f32[128,128]{1,0:T(8,128)S(1)} %get-tuple-element.155), channel_id=1, source_target_pairs={{0,24},{1,25},{2,26},{3,27},{4,28},{5,29},{6,30},{7,31},{8,0},{9,1... | collective-permute-start | bytes 196616 | tf_op jit(solution)/shard_map/ppermute | solution.py:624
  197.4 3.0 %collective-permute-start.27 = (f32[256,128]{1,0:T(8,128)S(1)}, f32[256,128]{1,0:T(8,128)S(1)}, u32[]{:S(2)}, u32[]{:S(2)}) collective-permute-start(f32[256,128]{1,0:T(8,128)S(1)} %add_add_fusion.1), channel_id=1, source_target_pairs={{0,6},{1,7},{2,0},{3,1},{4,2},{5,3},{6,4},{7,5},{8,14},{9,15},{10,... | collective-permute-start | bytes 393224 | tf_op jit(solution)/shard_map/ppermute | solution.py:613
  200.7 1.6 collective-permute-start.17
  202.4 1.7 collective-permute-start.18
  204.8 3.2 %collective-permute-start.16 = (f32[2,128,128]{2,1,0:T(8,128)S(1)}, f32[2,128,128]{2,1,0:T(8,128)S(1)}, u32[]{:S(2)}, u32[]{:S(2)}) collective-permute-start(f32[2,128,128]{2,1,0:T(8,128)S(1)} %pad_maximum_fusion.4), channel_id=1, source_target_pairs={{0,64},{32,96},{64,0},{96,32},{1,65},{33,97},{65,1},{97,33},{2,66}... | collective-permute-start | bytes 393224 | tf_op jit(solution)/shard_map/ppermute | solution.py:613
  208.7 2.6 %collective-permute-done.16 = f32[2,128,128]{2,1,0:T(8,128)S(1)} collective-permute-done((f32[2,128,128]{2,1,0:T(8,128)S(1)}, f32[2,128,128]{2,1,0:T(8,128)S(1)}, u32[]{:S(2)}, u32[]{:S(2)}) %collective-permute-start.16) | collective-permute-done | bytes 131104 | tf_op jit(solution)/shard_map/ppermute | solution.py:613
  (82 shorter events, 10.2 us)
Async XLA Ops:
  3.9 5.4 %copy-start.6 = (bf16[1,192,512]{2,1,0:T(8,128)(2,1)S(1)}, bf16[1,192,512]{2,1,0:T(8,128)(2,1)}, u32[]{:S(2)}) copy-start(bf16[1,192,512]{2,1,0:T(8,128)(2,1)} %param.10) | copy-start | bytes 589828
  3.9 5.4 %copy-start.7 = (bf16[1,192,512]{2,1,0:T(8,128)(2,1)S(1)}, bf16[1,192,512]{2,1,0:T(8,128)(2,1)}, u32[]{:S(2)}) copy-start(bf16[1,192,512]{2,1,0:T(8,128)(2,1)} %param.9) | copy-start | bytes 589828
  3.9 17.0 %copy-start.9 = (s32[1,192]{1,0:T(1,128)S(1)}, s32[1,192]{1,0:T(1,128)}, u32[]{:S(2)}) copy-start(s32[1,192]{1,0:T(1,128)} %param.12) | copy-start | bytes 2308
  9.4 11.4 %collective-permute-start = (bf16[64,1152]{1,0:T(8,128)(2,1)S(1)}, bf16[64,1152]{1,0:T(8,128)(2,1)S(1)}, u32[]{:S(2)}, u32[]{:S(2)}) collective-permute-start(bf16[64,1152]{1,0:T(8,128)(2,1)S(1)} %pad_maximum_fusion.3), channel_id=1, source_target_pairs={{0,1},{1,2},{2,3},{3,4},{4,5},{5,6},{6,7},{7,8},{8,9},{9,10},{10,1... | collective-permute-start | bytes 442376 | tf_op jit(solution)/shard_map/ppermute | solution.py:436
  10.7 29.9 %all-to-all-start = ((f32[32,24,256]{2,1,0:T(8,128)}), f32[32,24,256]{2,1,0:T(8,128)S(1)}, u32[]{:S(2)}, u32[]{:S(2)}) async-start(f32[32,24,256]{2,1,0:T(8,128)} %get-tuple-element.75), calls=%async_computation | async-start | bytes 1572864 | tf_op jit(solution)/shard_map/all_to_all | solution.py:383
  21.0 7.1 %copy-start.8 = (s32[256]{0:T(256)}, s32[256]{0:T(256)S(1)}, u32[]{:S(2)}) copy-start(s32[256]{0:T(256)S(1)} %pad_add_fusion.seg_ref) | copy-start | bytes 3076
  40.7 0.9 copy-start.3
  43.7 21.2 %all-to-all-start.1 = ((f32[32,24,256]{2,1,0:T(8,128)}), f32[32,24,256]{2,1,0:T(8,128)S(1)}, u32[]{:S(2)}, u32[]{:S(2)}) async-start(f32[32,24,256]{2,1,0:T(8,128)} %scan.2), calls=%async_computation.1 | async-start | bytes 1572864 | tf_op jit(solution)/shard_map/all_to_all | solution.py:383
  65.0 0.9 copy-start.4
  94.4 19.4 %all-to-all-start.2 = ((f32[32,24,256]{2,1,0:T(8,128)}), f32[32,24,256]{2,1,0:T(8,128)S(1)}, u32[]{:S(2)}, u32[]{:S(2)}) async-start(f32[32,24,256]{2,1,0:T(8,128)} %get-tuple-element.105), calls=%async_computation.2 | async-start | bytes 1572864 | tf_op jit(solution)/shard_map/all_to_all | solution.py:383
  113.9 0.9 copy-start.5
  114.8 9.6 %copy-start.1 = (f32[4,4,128,128]{3,2,1,0:T(8,128)S(1)}, f32[4,4,128,128]{3,2,1,0:T(8,128)}, u32[]{:S(2)}) copy-start(f32[4,4,128,128]{3,2,1,0:T(8,128)} %get-tuple-element.121) | copy-start | bytes 3145732
  117.0 7.4 %collective-permute-start.1 = (f32[4,4,128,128]{3,2,1,0:T(8,128)}, f32[4,4,128,128]{3,2,1,0:T(8,128)S(1)}, u32[]{:S(2)}, u32[]{:S(2)}) collective-permute-start(f32[4,4,128,128]{3,2,1,0:T(8,128)} %get-tuple-element.119), channel_id=1, source_target_pairs={{0,1},{1,0},{2,3},{3,2},{4,5},{5,4},{6,7},{7,6},{8,9},{9,8},{10,11... | collective-permute-start | bytes 3145736 | tf_op jit(solution)/shard_map/ppermute | solution.py:628
  117.7 39.4 %all-to-all-start.3 = ((f32[32,24,256]{2,1,0:T(8,128)}), f32[32,24,256]{2,1,0:T(8,128)S(1)}, u32[]{:S(2)}, u32[]{:S(2)}) async-start(f32[32,24,256]{2,1,0:T(8,128)} %scan.3), calls=%async_computation.3 | async-start | bytes 1572864 | tf_op jit(solution)/shard_map/all_to_all | solution.py:383
  124.5 19.1 %collective-permute-start.2 = (f32[4,128,128]{2,1,0:T(8,128)S(1)}, f32[4,128,128]{2,1,0:T(8,128)S(1)}, u32[]{:S(2)}, u32[]{:S(2)}) collective-permute-start(f32[4,128,128]{2,1,0:T(8,128)S(1)} %get-tuple-element.149), channel_id=1, source_target_pairs={{0,4},{1,5},{2,6},{3,7},{4,0},{5,1},{6,2},{7,3},{8,12},{9,13},{10,... | collective-permute-start | bytes 786440 | tf_op jit(solution)/shard_map/ppermute | solution.py:624
  127.9 20.4 %collective-permute-start.3 = (f32[4,128,128]{2,1,0:T(8,128)S(1)}, f32[4,128,128]{2,1,0:T(8,128)}, u32[]{:S(2)}, u32[]{:S(2)}) collective-permute-start(f32[4,128,128]{2,1,0:T(8,128)S(1)} %get-tuple-element.148), channel_id=1, source_target_pairs={{0,2},{1,3},{2,4},{3,5},{4,6},{5,7},{6,0},{7,1},{8,10},{9,11},{10,... | collective-permute-start | bytes 786440 | tf_op jit(solution)/shard_map/ppermute | solution.py:624
  128.4 19.8 %collective-permute-start.4 = (f32[4,128,128]{2,1,0:T(8,128)S(1)}, f32[4,128,128]{2,1,0:T(8,128)}, u32[]{:S(2)}, u32[]{:S(2)}) collective-permute-start(f32[4,128,128]{2,1,0:T(8,128)S(1)} %get-tuple-element.147), channel_id=1, source_target_pairs={{0,6},{1,7},{2,0},{3,1},{4,2},{5,3},{6,4},{7,5},{8,14},{9,15},{10,... | collective-permute-start | bytes 786440 | tf_op jit(solution)/shard_map/ppermute | solution.py:624
  157.1 0.9 copy-start.2
  157.1 15.5 %collective-permute-start.9 = (f32[4,4,128,128]{3,2,1,0:T(8,128)}, f32[4,4,128,128]{3,2,1,0:T(8,128)S(1)}, u32[]{:S(2)}, u32[]{:S(2)}) collective-permute-start(f32[4,4,128,128]{3,2,1,0:T(8,128)} %get-tuple-element.138), channel_id=1, source_target_pairs={{0,1},{1,0},{2,3},{3,2},{4,5},{5,4},{6,7},{7,6},{8,9},{9,8},{10,11... | collective-permute-start | bytes 3145736 | tf_op jit(solution)/shard_map/ppermute | solution.py:628
  158.0 17.9 %copy-start = (f32[4,4,128,128]{3,2,1,0:T(8,128)S(1)}, f32[4,4,128,128]{3,2,1,0:T(8,128)}, u32[]{:S(2)}) copy-start(f32[4,4,128,128]{3,2,1,0:T(8,128)} %get-tuple-element.139) | copy-start | bytes 3145732
  165.1 6.5 %collective-permute-start.8 = (f32[256,128]{1,0:T(8,128)S(1)}, f32[256,128]{1,0:T(8,128)S(1)}, u32[]{:S(2)}, u32[]{:S(2)}) collective-permute-start(f32[256,128]{1,0:T(8,128)S(1)} %dynamic-slice_bitcast_fusion), channel_id=1, source_target_pairs={{0,1},{1,0},{2,3},{3,2},{4,5},{5,4},{6,7},{7,6},{8,9},{9,8},{10,11... | collective-permute-start | bytes 393224 | tf_op jit(solution)/shard_map/ppermute | solution.py:628
  165.4 10.6 %collective-permute-start.5 = (f32[128,128]{1,0:T(8,128)S(1)}, f32[128,128]{1,0:T(8,128)S(1)}, u32[]{:S(2)}, u32[]{:S(2)}) collective-permute-start(f32[128,128]{1,0:T(8,128)S(1)} %get-tuple-element.154), channel_id=1, source_target_pairs={{0,16},{1,17},{2,18},{3,19},{4,20},{5,21},{6,22},{7,23},{8,24},{9,... | collective-permute-start | bytes 196616 | tf_op jit(solution)/shard_map/ppermute | solution.py:624
  168.4 7.7 %collective-permute-start.6 = (f32[128,128]{1,0:T(8,128)S(1)}, f32[128,128]{1,0:T(8,128)S(1)}, u32[]{:S(2)}, u32[]{:S(2)}) collective-permute-start(f32[128,128]{1,0:T(8,128)S(1)} %get-tuple-element.153), channel_id=1, source_target_pairs={{0,8},{1,9},{2,10},{3,11},{4,12},{5,13},{6,14},{7,15},{8,16},{9,17... | collective-permute-start | bytes 196616 | tf_op jit(solution)/shard_map/ppermute | solution.py:624
  169.0 8.6 %collective-permute-start.7 = (f32[128,128]{1,0:T(8,128)S(1)}, f32[128,128]{1,0:T(8,128)S(1)}, u32[]{:S(2)}, u32[]{:S(2)}) collective-permute-start(f32[128,128]{1,0:T(8,128)S(1)} %get-tuple-element.152), channel_id=1, source_target_pairs={{0,24},{1,25},{2,26},{3,27},{4,28},{5,29},{6,30},{7,31},{8,0},{9,1... | collective-permute-start | bytes 196616 | tf_op jit(solution)/shard_map/ppermute | solution.py:624
  172.6 6.3 %collective-permute-start.20 = (f32[256,128]{1,0:T(8,128)S(1)}, f32[256,128]{1,0:T(8,128)S(1)}, u32[]{:S(2)}, u32[]{:S(2)}) collective-permute-start(f32[256,128]{1,0:T(8,128)S(1)} %bitcast_add_fusion.2), channel_id=1, source_target_pairs={{0,8},{1,9},{2,10},{3,11},{4,12},{5,13},{6,14},{7,15},{8,16},{9,17... | collective-permute-start | bytes 393224 | tf_op jit(solution)/shard_map/ppermute | solution.py:613
  172.6 8.3 %collective-permute-start.21 = (f32[256,128]{1,0:T(8,128)S(1)}, f32[256,128]{1,0:T(8,128)S(1)}, u32[]{:S(2)}, u32[]{:S(2)}) collective-permute-start(f32[256,128]{1,0:T(8,128)S(1)} %bitcast_add_fusion.2), channel_id=1, source_target_pairs={{0,24},{1,25},{2,26},{3,27},{4,28},{5,29},{6,30},{7,31},{8,0},{9,1... | collective-permute-start | bytes 393224 | tf_op jit(solution)/shard_map/ppermute | solution.py:613
  176.0 6.6 %collective-permute-start.19 = (f32[256,128]{1,0:T(8,128)S(1)}, f32[256,128]{1,0:T(8,128)S(1)}, u32[]{:S(2)}, u32[]{:S(2)}) collective-permute-start(f32[256,128]{1,0:T(8,128)S(1)} %bitcast_add_fusion.2), channel_id=1, source_target_pairs={{0,16},{1,17},{2,18},{3,19},{4,20},{5,21},{6,22},{7,23},{8,24},{9,... | collective-permute-start | bytes 393224 | tf_op jit(solution)/shard_map/ppermute | solution.py:613
  176.1 10.9 %collective-permute-start.10 = (f32[4,128,128]{2,1,0:T(8,128)S(1)}, f32[4,128,128]{2,1,0:T(8,128)S(1)}, u32[]{:S(2)}, u32[]{:S(2)}) collective-permute-start(f32[4,128,128]{2,1,0:T(8,128)S(1)} %get-tuple-element.146), channel_id=1, source_target_pairs={{0,4},{1,5},{2,6},{3,7},{4,0},{5,1},{6,2},{7,3},{8,12},{9,13},{10,... | collective-permute-start | bytes 786440 | tf_op jit(solution)/shard_map/ppermute | solution.py:624
  177.6 12.9 %collective-permute-start.11 = (f32[4,128,128]{2,1,0:T(8,128)S(1)}, f32[4,128,128]{2,1,0:T(8,128)S(1)}, u32[]{:S(2)}, u32[]{:S(2)}) collective-permute-start(f32[4,128,128]{2,1,0:T(8,128)S(1)} %get-tuple-element.145), channel_id=1, source_target_pairs={{0,2},{1,3},{2,4},{3,5},{4,6},{5,7},{6,0},{7,1},{8,10},{9,11},{10,... | collective-permute-start | bytes 786440 | tf_op jit(solution)/shard_map/ppermute | solution.py:624
  178.8 11.7 %collective-permute-start.12 = (f32[4,128,128]{2,1,0:T(8,128)S(1)}, f32[4,128,128]{2,1,0:T(8,128)S(1)}, u32[]{:S(2)}, u32[]{:S(2)}) collective-permute-start(f32[4,128,128]{2,1,0:T(8,128)S(1)} %get-tuple-element.144), channel_id=1, source_target_pairs={{0,6},{1,7},{2,0},{3,1},{4,2},{5,3},{6,4},{7,5},{8,14},{9,15},{10,... | collective-permute-start | bytes 786440 | tf_op jit(solution)/shard_map/ppermute | solution.py:624
  182.6 11.3 %collective-permute-start.23 = (f32[256,128]{1,0:T(8,128)S(1)}, f32[256,128]{1,0:T(8,128)S(1)}, u32[]{:S(2)}, u32[]{:S(2)}) collective-permute-start(f32[256,128]{1,0:T(8,128)S(1)} %add_add_fusion.2), channel_id=1, source_target_pairs={{0,32},{32,64},{64,96},{96,0},{1,33},{33,65},{65,97},{97,1},{2,34}... | collective-permute-start | bytes 393224 | tf_op jit(solution)/shard_map/ppermute | solution.py:613
  184.2 12.9 %collective-permute-start.24 = (f32[256,128]{1,0:T(8,128)S(1)}, f32[256,128]{1,0:T(8,128)S(1)}, u32[]{:S(2)}, u32[]{:S(2)}) collective-permute-start(f32[256,128]{1,0:T(8,128)S(1)} %add_add_fusion.2), channel_id=1, source_target_pairs={{0,96},{32,0},{64,32},{96,64},{1,97},{33,1},{65,33},{97,65},{2,98}... | collective-permute-start | bytes 393224 | tf_op jit(solution)/shard_map/ppermute | solution.py:613
  186.9 10.2 %collective-permute-start.22 = (f32[256,128]{1,0:T(8,128)S(1)}, f32[256,128]{1,0:T(8,128)S(1)}, u32[]{:S(2)}, u32[]{:S(2)}) collective-permute-start(f32[256,128]{1,0:T(8,128)S(1)} %add_add_fusion.2), channel_id=1, source_target_pairs={{0,64},{32,96},{64,0},{96,32},{1,65},{33,97},{65,1},{97,33},{2,66}... | collective-permute-start | bytes 393224 | tf_op jit(solution)/shard_map/ppermute | solution.py:613
  190.6 9.8 %collective-permute-start.13 = (f32[128,128]{1,0:T(8,128)S(1)}, f32[128,128]{1,0:T(8,128)S(1)}, u32[]{:S(2)}, u32[]{:S(2)}) collective-permute-start(f32[128,128]{1,0:T(8,128)S(1)} %get-tuple-element.157), channel_id=1, source_target_pairs={{0,16},{1,17},{2,18},{3,19},{4,20},{5,21},{6,22},{7,23},{8,24},{9,... | collective-permute-start | bytes 196616 | tf_op jit(solution)/shard_map/ppermute | solution.py:624
  193.9 6.8 %collective-permute-start.14 = (f32[128,128]{1,0:T(8,128)S(1)}, f32[128,128]{1,0:T(8,128)S(1)}, u32[]{:S(2)}, u32[]{:S(2)}) collective-permute-start(f32[128,128]{1,0:T(8,128)S(1)} %get-tuple-element.156), channel_id=1, source_target_pairs={{0,8},{1,9},{2,10},{3,11},{4,12},{5,13},{6,14},{7,15},{8,16},{9,17... | collective-permute-start | bytes 196616 | tf_op jit(solution)/shard_map/ppermute | solution.py:624
  193.9 6.8 %collective-permute-start.15 = (f32[128,128]{1,0:T(8,128)S(1)}, f32[128,128]{1,0:T(8,128)S(1)}, u32[]{:S(2)}, u32[]{:S(2)}) collective-permute-start(f32[128,128]{1,0:T(8,128)S(1)} %get-tuple-element.155), channel_id=1, source_target_pairs={{0,24},{1,25},{2,26},{3,27},{4,28},{5,29},{6,30},{7,31},{8,0},{9,1... | collective-permute-start | bytes 196616 | tf_op jit(solution)/shard_map/ppermute | solution.py:624
  197.2 7.7 %collective-permute-start.26 = (f32[256,128]{1,0:T(8,128)S(1)}, f32[256,128]{1,0:T(8,128)S(1)}, u32[]{:S(2)}, u32[]{:S(2)}) collective-permute-start(f32[256,128]{1,0:T(8,128)S(1)} %add_add_fusion.1), channel_id=1, source_target_pairs={{0,2},{1,3},{2,4},{3,5},{4,6},{5,7},{6,0},{7,1},{8,10},{9,11},{10,... | collective-permute-start | bytes 393224 | tf_op jit(solution)/shard_map/ppermute | solution.py:613
  197.4 10.6 %collective-permute-start.27 = (f32[256,128]{1,0:T(8,128)S(1)}, f32[256,128]{1,0:T(8,128)S(1)}, u32[]{:S(2)}, u32[]{:S(2)}) collective-permute-start(f32[256,128]{1,0:T(8,128)S(1)} %add_add_fusion.1), channel_id=1, source_target_pairs={{0,6},{1,7},{2,0},{3,1},{4,2},{5,3},{6,4},{7,5},{8,14},{9,15},{10,... | collective-permute-start | bytes 393224 | tf_op jit(solution)/shard_map/ppermute | solution.py:613
  200.5 7.5 %collective-permute-start.25 = (f32[256,128]{1,0:T(8,128)S(1)}, f32[256,128]{1,0:T(8,128)S(1)}, u32[]{:S(2)}, u32[]{:S(2)}) collective-permute-start(f32[256,128]{1,0:T(8,128)S(1)} %add_add_fusion.1), channel_id=1, source_target_pairs={{0,4},{1,5},{2,6},{3,7},{4,0},{5,1},{6,2},{7,3},{8,12},{9,13},{10,... | collective-permute-start | bytes 393224 | tf_op jit(solution)/shard_map/ppermute | solution.py:613
  200.7 7.7 %collective-permute-start.17 = (f32[2,128,128]{2,1,0:T(8,128)S(1)}, f32[2,128,128]{2,1,0:T(8,128)S(1)}, u32[]{:S(2)}, u32[]{:S(2)}) collective-permute-start(f32[2,128,128]{2,1,0:T(8,128)S(1)} %pad_maximum_fusion.4), channel_id=1, source_target_pairs={{0,32},{32,64},{64,96},{96,0},{1,33},{33,65},{65,97},{97,1},{2,34}... | collective-permute-start | bytes 393224 | tf_op jit(solution)/shard_map/ppermute | solution.py:613
  202.4 6.3 %collective-permute-start.18 = (f32[2,128,128]{2,1,0:T(8,128)S(1)}, f32[2,128,128]{2,1,0:T(8,128)S(1)}, u32[]{:S(2)}, u32[]{:S(2)}) collective-permute-start(f32[2,128,128]{2,1,0:T(8,128)S(1)} %pad_maximum_fusion.4), channel_id=1, source_target_pairs={{0,96},{32,0},{64,32},{96,64},{1,97},{33,1},{65,33},{97,65},{2,98}... | collective-permute-start | bytes 393224 | tf_op jit(solution)/shard_map/ppermute | solution.py:613
  204.8 6.5 %collective-permute-start.16 = (f32[2,128,128]{2,1,0:T(8,128)S(1)}, f32[2,128,128]{2,1,0:T(8,128)S(1)}, u32[]{:S(2)}, u32[]{:S(2)}) collective-permute-start(f32[2,128,128]{2,1,0:T(8,128)S(1)} %pad_maximum_fusion.4), channel_id=1, source_target_pairs={{0,64},{32,96},{64,0},{96,32},{1,65},{33,97},{65,1},{97,33},{2,66}... | collective-permute-start | bytes 393224 | tf_op jit(solution)/shard_map/ppermute | solution.py:613
  208.0 4.0 %collective-permute-start.28 = (f32[256,128]{1,0:T(8,128)S(1)}, f32[256,128]{1,0:T(8,128)S(1)}, u32[]{:S(2)}, u32[]{:S(2)}) collective-permute-start(f32[256,128]{1,0:T(8,128)S(1)} %add_add_fusion), channel_id=1, source_target_pairs={{0,1},{1,0},{2,3},{3,2},{4,5},{5,4},{6,7},{7,6},{8,9},{9,8},{10,11... | collective-permute-start | bytes 393224 | tf_op jit(solution)/shard_map/ppermute | solution.py:667

commit v5 on v3

--- a/solution.py
+++ b/solution.py
@@ -656,8 +656,8 @@
     key_mine, key_theirs = over_chip(key_mine, key_theirs)
     second = over_chip(*second)
     key_sum, second = lax.optimization_barrier((key_mine + key_theirs, second))
-    key_sum = around("x", around("dp", around("z", key_sum)))
-    second = slice_around("z", 0, slice_around("x", 1, *second))
+    key_sum = around("z", around("dp", around("x", key_sum)))
+    second = slice_around("x", 0, slice_around("z", 0, *second))
     first = slice_around("x", 0, first)
     both = around("dp", jnp.stack([first, second], 0))
     key_theirs = lax.ppermute(key_sum, "ctx", partner)

time: 206 us -> 207 us (level)
  other arithmetic: 10 us -> 6.37 us
  starting transfers between devices: 73 us -> 76.5 us
    ppermute x12, starting transfers between devices: 19.6 us -> 24.8 us  [slice_around(): lax.ppermute(part, 'ctx', route)]
    add x3 -> x2, other arithmetic: 2.99 us -> 0.17 us  [slice_around(): sum((lax.dynamic_index_in_dim(value, lax.rem(place[axis] + s, RING), dim,...]
    unnamed x22 -> x24, local copies, waits for them, and re-layouts: 4.79 us -> 3.98 us
  transfers between devices with their start and end apart: 33 -> 33, of which waited for: 8 -> 9; matrix products, arithmetic and copies ran while one was open for 5% -> 3% of each run, Pallas kernels for 31% -> 31%
where the time goes in v5:
time: 207 us; the launch traced here: 204 us
  Pallas kernels  102 us (49%)
  starting transfers between devices  76.5 us (37%)
  waiting for transfers between devices  12 us (6%)
  local copies, waits for them, and re-layouts  6.6 us (3%)
  other arithmetic  6.37 us (3%)
    pallas_call x10, Pallas kernels, call(): pl.pallas_call(kernel, grid_spec=pltpu.PrefetchScalarGridSpec(num_scalar_...  102 us
    all_to_all x4, starting transfers between devices, exchange(): return lax.all_to_all(pieces, axis, 0, 0, tiled=True)  29.7 us
    ppermute x12, starting transfers between devices, slice_around(): lax.ppermute(part, 'ctx', route)  24.8 us
    ppermute x12, starting transfers between devices, around(): lax.ppermute(value, name, route)  19.7 us
    ppermute x12, waiting for transfers between devices, around(): lax.ppermute(value, name, route)  5.04 us
    ppermute x12, waiting for transfers between devices, slice_around(): lax.ppermute(part, 'ctx', route)  4.85 us
  transfers between devices with their start and end apart: 33, of which 9 were waited for; matrix products, arithmetic and copies ran while one was open for 3% of the time, Pallas kernels for 31%

profile of v5, /device:TPU:0, one launch (start us, length us, event | category | flops | bytes accessed | tf_op | source)
XLA Modules:
  0.0 204.5 jit_solution(9438421220873093159)
XLA Ops:
  1.8 1.3 reduce.5
  3.9 5.4 %block.1 = (f32[4,3,136,256]{3,2,1,0:T(8,128)}, f32[32,24,256]{2,1,0:T(8,128)}) custom-call(s32[192]{0:T(256)} %bitcast.91, bf16[192,512]{1,0:T(8,128)(2,1)} %bitcast.84, bf16[192,512]{1,0:T(8,128)(2,1)} %bitcast.81, bf16[4,128,128]{2,1,0:T(8,128)(2,1)} %map_ref.5, s32[3,1,256]{2,1,0:T(1,128)} %tile.12.seg_row_ref), custom_call_target="tpu_custom_call" | custom-call | flops 4000000000 | bytes 12000000 | tf_op jit(solution)/shard_map/block/pallas_call | solution.py:363
  9.4 1.3 collective-permute-start
  10.7 10.0 %all-to-all-start = ((f32[32,24,256]{2,1,0:T(8,128)}), f32[32,24,256]{2,1,0:T(8,128)S(1)}, u32[]{:S(2)}, u32[]{:S(2)}) async-start(f32[32,24,256]{2,1,0:T(8,128)} %get-tuple-element.69), calls=%async_computation | async-start | bytes 1572864 | tf_op jit(solution)/shard_map/all_to_all | solution.py:383
  21.8 0.8 pad_maximum_fusion
  22.6 5.5 %keys.1 = (bf16[4,256,256]{2,1,0:T(8,128)(2,1)}, bf16[4,256,256]{2,1,0:T(8,128)(2,1)}, bf16[4,3,256,256]{3,2,1,0:T(8,128)(2,1)}, bf16[4,3,128,256]{3,2,1,0:T(8,1...) custom-call(s32[4]{0:T(128)} %window_ref.1, bf16[256,512]{1,0:T(8,128)(2,1)} %get-tuple-element.148.key_ref, ...), custom_call_target="tpu_custom_call" | custom-call | flops 5000000000 | bytes 15000000 | tf_op jit(solution)/shard_map/keys/pallas_call | solution.py:363
  28.1 12.5 %local.2 = (f32[16,3,128,256]{3,2,1,0:T(8,128)}, f32[16,3,1,256]{3,2,1,0:T(1,128)}, bf16[16,3,256,256]{3,2,1,0:T(8,128)(2,1)}, bf16[16,3,256,256]{3,2,1,0:T(8,128)(2,1)}) custom-call(bf16[192,8192]{1,0:T(8,128)(2,1)} %bitcast.65, bf16[192,8192]{1,0:T(8,128)(2,1)} %bitcast.66, bf16[192,8192]{1,0:T(8,128)(2,1)} %bitcast.67, bf16[192,8192]{1,0:T(8,128)(2,1)} %bitcast.68, ...), custom_call_target="tpu_custom_call" | custom-call | flops 15000000512 | bytes 45000000 | tf_op jit(solution)/shard_map/local/pallas_call | solution.py:363
  40.7 0.9 copy-done.3
  41.6 2.1 %scan.2 = f32[32,24,256]{2,1,0:T(8,128)} custom-call(f32[32,24,256]{2,1,0:T(8,128)} %copy-done.3), custom_call_target="tpu_custom_call" | custom-call | flops 2000000000 | bytes 6000000 | tf_op jit(solution)/shard_map/scan/pallas_call | solution.py:363
  43.7 7.4 %all-to-all-start.1 = ((f32[32,24,256]{2,1,0:T(8,128)}), f32[32,24,256]{2,1,0:T(8,128)S(1)}, u32[]{:S(2)}, u32[]{:S(2)}) async-start(f32[32,24,256]{2,1,0:T(8,128)} %scan.2), calls=%async_computation.1 | async-start | bytes 1572864 | tf_op jit(solution)/shard_map/all_to_all | solution.py:383
  51.1 12.0 %local.3 = (f32[16,3,128,256]{3,2,1,0:T(8,128)}, f32[16,3,1,256]{3,2,1,0:T(1,128)}, bf16[16,3,256,256]{3,2,1,0:T(8,128)(2,1)}, bf16[16,3,256,256]{3,2,1,0:T(8,128)(2,1)}) custom-call(bf16[192,8192]{1,0:T(8,128)(2,1)} %bitcast.69, bf16[192,8192]{1,0:T(8,128)(2,1)} %bitcast.70, ...), custom_call_target="tpu_custom_call", output_to_operand_aliasing={{0}: (13, {}), {1}: (14, {}), {2}: (15, {}), {3}: (16, {})} | custom-call | flops 15000000512 | bytes 45000000 | tf_op jit(solution)/shard_map/local/pallas_call | solution.py:363
  63.2 1.8 all-to-all-done.1.first_ref
  65.0 0.9 copy-done.5
  65.9 28.6 %outputs.1 = (bf16[16,3,512,256]{3,2,1,0:T(8,128)(2,1)}, f32[16,3,1,256]{3,2,1,0:T(1,128)}, f32[4,3,128,256]{3,2,1,0:T(8,128)}, f32[4,3,136,256]{3,2,1,0:T(8,128...) custom-call(s32[256]{0:T(256)} %copy-done.9, bf16[192,8192]{1,0:T(8,128)(2,1)} %bitcast.93, ...), custom_call_target="tpu_custom_call" | custom-call | flops 44999999488 | bytes 135000000 | tf_op jit(solution)/shard_map/outputs/pallas_call | solution.py:363
  94.4 5.6 %all-to-all-start.2 = ((f32[32,24,256]{2,1,0:T(8,128)}), f32[32,24,256]{2,1,0:T(8,128)S(1)}, u32[]{:S(2)}, u32[]{:S(2)}) async-start(f32[32,24,256]{2,1,0:T(8,128)} %get-tuple-element.99), calls=%async_computation.2 | async-start | bytes 1572864 | tf_op jit(solution)/shard_map/all_to_all | solution.py:383
  100.0 13.6 %queries.2 = (f32[4,4,128,128]{3,2,1,0:T(8,128)}, f32[4,4,128,128]{3,2,1,0:T(8,128)}) custom-call(s32[1]{0:T(128)} %bitcast.7.core_ref, bf16[192,8192]{1,0:T(8,128)(2,1)} %bitcast.73, bf16[192,8192]{1,0:T(8,128)(2,1)} %bitcast.74, bf16[192,8192]{1,0:T(8,128)(2,1)} %bitcast.75, bf16[192,8192]{1,0:T(8,128)(2,1)} %bitcast.76, ...), custom_call_target="tpu_custom_call" | custom-call | flops 10000000000 | bytes 30000000 | tf_op jit(solution)/shard_map/queries/pallas_call | solution.py:363
  113.9 0.9 copy-done.6
  114.8 2.1 %scan.3 = f32[32,24,256]{2,1,0:T(8,128)} custom-call(f32[32,24,256]{2,1,0:T(8,128)} %copy-done.6), custom_call_target="tpu_custom_call" | custom-call | flops 2000000000 | bytes 6000000 | tf_op jit(solution)/shard_map/scan/pallas_call | solution.py:363
  117.5 6.7 %all-to-all-start.3 = ((f32[32,24,256]{2,1,0:T(8,128)}), f32[32,24,256]{2,1,0:T(8,128)S(1)}, u32[]{:S(2)}, u32[]{:S(2)}) async-start(f32[32,24,256]{2,1,0:T(8,128)} %scan.3), calls=%async_computation.3 | async-start | bytes 1572864 | tf_op jit(solution)/shard_map/all_to_all | solution.py:383
  124.3 14.0 %queries.3 = (f32[4,4,128,128]{3,2,1,0:T(8,128)}, f32[4,4,128,128]{3,2,1,0:T(8,128)}) custom-call(s32[1]{0:T(128)} %bitcast.7.core_ref, bf16[192,8192]{1,0:T(8,128)(2,1)} %bitcast.77, bf16[192,8192]{1,0:T(8,128)(2,1)} %bitcast.78, bf16[192,8192]{1,0:T(8,128)(2,1)} %bitcast.79, bf16[192,8192]{1,0:T(8,128)(2,1)} %bitcast.80, ...), custom_call_target="tpu_custom_call" | custom-call | flops 10000000000 | bytes 30000000 | tf_op jit(solution)/shard_map/queries/pallas_call | solution.py:363
  138.4 3.4 %collective-permute-start.2 = (f32[4,128,128]{2,1,0:T(8,128)S(1)}, f32[4,128,128]{2,1,0:T(8,128)}, u32[]{:S(2)}, u32[]{:S(2)}) collective-permute-start(f32[4,128,128]{2,1,0:T(8,128)S(1)} %get-tuple-element.137), channel_id=1, source_target_pairs={{0,4},{1,5},{2,6},{3,7},{4,0},{5,1},{6,2},{7,3},{8,12},{9,13},{10,... | collective-permute-start | bytes 786440 | tf_op jit(solution)/shard_map/ppermute | solution.py:624
  142.3 2.7 %collective-permute-start.4 = (f32[4,128,128]{2,1,0:T(8,128)S(1)}, f32[4,128,128]{2,1,0:T(8,128)}, u32[]{:S(2)}, u32[]{:S(2)}) collective-permute-start(f32[4,128,128]{2,1,0:T(8,128)S(1)} %get-tuple-element.135), channel_id=1, source_target_pairs={{0,6},{1,7},{2,0},{3,1},{4,2},{5,3},{6,4},{7,5},{8,14},{9,15},{10,... | collective-permute-start | bytes 786440 | tf_op jit(solution)/shard_map/ppermute | solution.py:624
  145.0 6.1 %tail.1 = f32[4,128,128]{2,1,0:T(8,128)} custom-call(s32[256]{0:T(256)} %copy-done.9, bf16[256,512]{1,0:T(8,128)(2,1)} %get-tuple-element.148.key_ref, bf16[256,512]{1,0:T(8,128)(2,1)} %get-tuple-element.149.value_ref, bf16[4,128,128]{2,1,0:T(8,128)(2,1)} %map_ref.5, s32[256,1]{1,0:T(8,128)} %copy.15.seg_col_ref, f32[32,24,256]{2,1,0:T(8,128)} %copy-done.4, ...), custom_call_target="tpu_custom_call" | custom-call | flops 5000000000 | bytes 15000000 | tf_op jit(solution)/shard_map/tail/pallas_call | solution.py:363
  151.1 3.2 %collective-permute-done.3 = f32[4,128,128]{2,1,0:T(8,128)} collective-permute-done((f32[4,128,128]{2,1,0:T(8,128)S(1)}, f32[4,128,128]{2,1,0:T(8,128)}, u32[]{:S(2)}, u32[]{:S(2)}) %collective-permute-start.3) | collective-permute-done | bytes 262176 | tf_op jit(solution)/shard_map/ppermute | solution.py:624
  154.5 1.3 fusion.1
  155.8 0.9 dynamic-slice_bitcast_fusion
  157.1 3.1 %collective-permute-start.5 = (f32[128,128]{1,0:T(8,128)S(1)}, f32[128,128]{1,0:T(8,128)S(1)}, u32[]{:S(2)}, u32[]{:S(2)}) collective-permute-start(f32[128,128]{1,0:T(8,128)S(1)} %get-tuple-element.142), channel_id=1, source_target_pairs={{0,16},{1,17},{2,18},{3,19},{4,20},{5,21},{6,22},{7,23},{8,24},{9,... | collective-permute-start | bytes 196616 | tf_op jit(solution)/shard_map/ppermute | solution.py:624
  160.8 2.6 %collective-permute-start.7 = (f32[128,128]{1,0:T(8,128)S(1)}, f32[128,128]{1,0:T(8,128)S(1)}, u32[]{:S(2)}, u32[]{:S(2)}) collective-permute-start(f32[128,128]{1,0:T(8,128)S(1)} %get-tuple-element.140), channel_id=1, source_target_pairs={{0,24},{1,25},{2,26},{3,27},{4,28},{5,29},{6,30},{7,31},{8,0},{9,1... | collective-permute-start | bytes 196616 | tf_op jit(solution)/shard_map/ppermute | solution.py:624
  163.4 0.9 bitcast_add_fusion.2
  164.4 3.2 %collective-permute-start.21 = (f32[256,128]{1,0:T(8,128)S(1)}, f32[256,128]{1,0:T(8,128)S(1)}, u32[]{:S(2)}, u32[]{:S(2)}) collective-permute-start(f32[256,128]{1,0:T(8,128)S(1)} %bitcast_add_fusion.2), channel_id=1, source_target_pairs={{0,24},{1,25},{2,26},{3,27},{4,28},{5,29},{6,30},{7,31},{8,0},{9,1... | collective-permute-start | bytes 393224 | tf_op jit(solution)/shard_map/ppermute | solution.py:613
  167.8 2.1 %collective-permute-start.10 = (f32[4,128,128]{2,1,0:T(8,128)S(1)}, f32[4,128,128]{2,1,0:T(8,128)S(1)}, u32[]{:S(2)}, u32[]{:S(2)}) collective-permute-start(f32[4,128,128]{2,1,0:T(8,128)S(1)} %get-tuple-element.134), channel_id=1, source_target_pairs={{0,4},{1,5},{2,6},{3,7},{4,0},{5,1},{6,2},{7,3},{8,12},{9,13},{10,... | collective-permute-start | bytes 786440 | tf_op jit(solution)/shard_map/ppermute | solution.py:624
  170.0 1.4 collective-permute-start.11
  171.4 1.8 collective-permute-start.12
  173.2 1.0 collective-permute-done.19
  174.3 1.6 collective-permute-start.23
  175.9 1.7 collective-permute-start.24
  177.6 1.1 collective-permute-done.10
  178.7 3.2 %collective-permute-start.22 = (f32[256,128]{1,0:T(8,128)S(1)}, f32[256,128]{1,0:T(8,128)S(1)}, u32[]{:S(2)}, u32[]{:S(2)}) collective-permute-start(f32[256,128]{1,0:T(8,128)S(1)} %add_add_fusion.2), channel_id=1, source_target_pairs={{0,64},{32,96},{64,0},{96,32},{1,65},{33,97},{65,1},{97,33},{2,66}... | collective-permute-start | bytes 393224 | tf_op jit(solution)/shard_map/ppermute | solution.py:613
  182.4 3.2 %collective-permute-start.13 = (f32[128,128]{1,0:T(8,128)S(1)}, f32[128,128]{1,0:T(8,128)S(1)}, u32[]{:S(2)}, u32[]{:S(2)}) collective-permute-start(f32[128,128]{1,0:T(8,128)S(1)} %get-tuple-element.145), channel_id=1, source_target_pairs={{0,16},{1,17},{2,18},{3,19},{4,20},{5,21},{6,22},{7,23},{8,24},{9,... | collective-permute-start | bytes 196616 | tf_op jit(solution)/shard_map/ppermute | solution.py:624
  185.6 3.2 %collective-permute-start.15 = (f32[128,128]{1,0:T(8,128)S(1)}, f32[128,128]{1,0:T(8,128)S(1)}, u32[]{:S(2)}, u32[]{:S(2)}) collective-permute-start(f32[128,128]{1,0:T(8,128)S(1)} %get-tuple-element.143), channel_id=1, source_target_pairs={{0,24},{1,25},{2,26},{3,27},{4,28},{5,29},{6,30},{7,31},{8,0},{9,1... | collective-permute-start | bytes 196616 | tf_op jit(solution)/shard_map/ppermute | solution.py:624
  188.9 1.5 collective-permute-start.26
  190.4 1.8 collective-permute-start.27
  192.2 0.9 collective-permute-start.25
  193.1 1.6 collective-permute-start.17
  194.8 1.7 collective-permute-start.18
  196.5 2.4 %collective-permute-start.16 = (f32[2,128,128]{2,1,0:T(8,128)S(1)}, f32[2,128,128]{2,1,0:T(8,128)S(1)}, u32[]{:S(2)}, u32[]{:S(2)}) collective-permute-start(f32[2,128,128]{2,1,0:T(8,128)S(1)} %pad_maximum_fusion.4), channel_id=1, source_target_pairs={{0,64},{32,96},{64,0},{96,32},{1,65},{33,97},{65,1},{97,33},{2,66}... | collective-permute-start | bytes 393224 | tf_op jit(solution)/shard_map/ppermute | solution.py:613
  198.9 1.9 collective-permute-done.17
  200.8 2.1 %collective-permute-done.16 = f32[2,128,128]{2,1,0:T(8,128)S(1)} collective-permute-done((f32[2,128,128]{2,1,0:T(8,128)S(1)}, f32[2,128,128]{2,1,0:T(8,128)S(1)}, u32[]{:S(2)}, u32[]{:S(2)}) %collective-permute-start.16) | collective-permute-done | bytes 131104 | tf_op jit(solution)/shard_map/ppermute | solution.py:613
  (83 shorter events, 8.2 us)
Async XLA Ops:
  3.9 5.4 %copy-start.7 = (bf16[1,192,512]{2,1,0:T(8,128)(2,1)S(1)}, bf16[1,192,512]{2,1,0:T(8,128)(2,1)}, u32[]{:S(2)}) copy-start(bf16[1,192,512]{2,1,0:T(8,128)(2,1)} %param.10) | copy-start | bytes 589828
  3.9 5.4 %copy-start.8 = (bf16[1,192,512]{2,1,0:T(8,128)(2,1)S(1)}, bf16[1,192,512]{2,1,0:T(8,128)(2,1)}, u32[]{:S(2)}) copy-start(bf16[1,192,512]{2,1,0:T(8,128)(2,1)} %param.9) | copy-start | bytes 589828
  3.9 17.0 %copy-start.10 = (s32[1,192]{1,0:T(1,128)S(1)}, s32[1,192]{1,0:T(1,128)}, u32[]{:S(2)}) copy-start(s32[1,192]{1,0:T(1,128)} %param.12) | copy-start | bytes 2308
  9.4 11.4 %collective-permute-start = (bf16[64,1152]{1,0:T(8,128)(2,1)S(1)}, bf16[64,1152]{1,0:T(8,128)(2,1)S(1)}, u32[]{:S(2)}, u32[]{:S(2)}) collective-permute-start(bf16[64,1152]{1,0:T(8,128)(2,1)S(1)} %pad_maximum_fusion.3), channel_id=1, source_target_pairs={{0,1},{1,2},{2,3},{3,4},{4,5},{5,6},{6,7},{7,8},{8,9},{9,10},{10,1... | collective-permute-start | bytes 442376 | tf_op jit(solution)/shard_map/ppermute | solution.py:436
  10.7 29.9 %all-to-all-start = ((f32[32,24,256]{2,1,0:T(8,128)}), f32[32,24,256]{2,1,0:T(8,128)S(1)}, u32[]{:S(2)}, u32[]{:S(2)}) async-start(f32[32,24,256]{2,1,0:T(8,128)} %get-tuple-element.69), calls=%async_computation | async-start | bytes 1572864 | tf_op jit(solution)/shard_map/all_to_all | solution.py:383
  21.0 7.1 %copy-start.9 = (s32[256]{0:T(256)}, s32[256]{0:T(256)S(1)}, u32[]{:S(2)}) copy-start(s32[256]{0:T(256)S(1)} %pad_add_fusion.seg_ref) | copy-start | bytes 3076
  40.7 0.9 copy-start.3
  43.7 21.2 %all-to-all-start.1 = ((f32[32,24,256]{2,1,0:T(8,128)}), f32[32,24,256]{2,1,0:T(8,128)S(1)}, u32[]{:S(2)}, u32[]{:S(2)}) async-start(f32[32,24,256]{2,1,0:T(8,128)} %scan.2), calls=%async_computation.1 | async-start | bytes 1572864 | tf_op jit(solution)/shard_map/all_to_all | solution.py:383
  65.0 0.9 copy-start.5
  94.4 19.4 %all-to-all-start.2 = ((f32[32,24,256]{2,1,0:T(8,128)}), f32[32,24,256]{2,1,0:T(8,128)S(1)}, u32[]{:S(2)}, u32[]{:S(2)}) async-start(f32[32,24,256]{2,1,0:T(8,128)} %get-tuple-element.99), calls=%async_computation.2 | async-start | bytes 1572864 | tf_op jit(solution)/shard_map/all_to_all | solution.py:383
  113.9 0.9 copy-start.6
  116.9 7.4 %collective-permute-start.1 = (f32[4,4,128,128]{3,2,1,0:T(8,128)}, f32[4,4,128,128]{3,2,1,0:T(8,128)S(1)}, u32[]{:S(2)}, u32[]{:S(2)}) collective-permute-start(f32[4,4,128,128]{3,2,1,0:T(8,128)} %get-tuple-element.113), channel_id=1, source_target_pairs={{0,1},{1,0},{2,3},{3,2},{4,5},{5,4},{6,7},{7,6},{8,9},{9,8},{10,11... | collective-permute-start | bytes 3145736 | tf_op jit(solution)/shard_map/ppermute | solution.py:628
  117.5 20.7 %all-to-all-start.3 = ((f32[32,24,256]{2,1,0:T(8,128)}), f32[32,24,256]{2,1,0:T(8,128)S(1)}, u32[]{:S(2)}, u32[]{:S(2)}) async-start(f32[32,24,256]{2,1,0:T(8,128)} %scan.3), calls=%async_computation.3 | async-start | bytes 1572864 | tf_op jit(solution)/shard_map/all_to_all | solution.py:383
  124.2 14.1 %copy-start.1 = (f32[4,4,128,128]{3,2,1,0:T(8,128)S(1)}, f32[4,4,128,128]{3,2,1,0:T(8,128)}, u32[]{:S(2)}) copy-start(f32[4,4,128,128]{3,2,1,0:T(8,128)} %get-tuple-element.121) | copy-start | bytes 3145732
  124.2 14.0 %copy-start.2 = (f32[4,4,128,128]{3,2,1,0:T(8,128)}, f32[4,4,128,128]{3,2,1,0:T(8,128)S(1)}, u32[]{:S(2)}) copy-start(f32[4,4,128,128]{3,2,1,0:T(8,128)S(1)} %collective-permute-done.1) | copy-start | bytes 3145732
  138.3 6.7 %copy-start.4 = (f32[32,24,256]{2,1,0:T(8,128)}, f32[32,24,256]{2,1,0:T(8,128)S(1)}, u32[]{:S(2)}) copy-start(f32[32,24,256]{2,1,0:T(8,128)S(1)} %all-to-all-done.3.later_ref) | copy-start | bytes 2359300
  138.4 12.7 %collective-permute-start.2 = (f32[4,128,128]{2,1,0:T(8,128)S(1)}, f32[4,128,128]{2,1,0:T(8,128)}, u32[]{:S(2)}, u32[]{:S(2)}) collective-permute-start(f32[4,128,128]{2,1,0:T(8,128)S(1)} %get-tuple-element.137), channel_id=1, source_target_pairs={{0,4},{1,5},{2,6},{3,7},{4,0},{5,1},{6,2},{7,3},{8,12},{9,13},{10,... | collective-permute-start | bytes 786440 | tf_op jit(solution)/shard_map/ppermute | solution.py:624
  141.8 12.6 %collective-permute-start.3 = (f32[4,128,128]{2,1,0:T(8,128)S(1)}, f32[4,128,128]{2,1,0:T(8,128)}, u32[]{:S(2)}, u32[]{:S(2)}) collective-permute-start(f32[4,128,128]{2,1,0:T(8,128)S(1)} %get-tuple-element.136), channel_id=1, source_target_pairs={{0,2},{1,3},{2,4},{3,5},{4,6},{5,7},{6,0},{7,1},{8,10},{9,11},{10,... | collective-permute-start | bytes 786440 | tf_op jit(solution)/shard_map/ppermute | solution.py:624
  142.3 12.2 %collective-permute-start.4 = (f32[4,128,128]{2,1,0:T(8,128)S(1)}, f32[4,128,128]{2,1,0:T(8,128)}, u32[]{:S(2)}, u32[]{:S(2)}) collective-permute-start(f32[4,128,128]{2,1,0:T(8,128)S(1)} %get-tuple-element.135), channel_id=1, source_target_pairs={{0,6},{1,7},{2,0},{3,1},{4,2},{5,3},{6,4},{7,5},{8,14},{9,15},{10,... | collective-permute-start | bytes 786440 | tf_op jit(solution)/shard_map/ppermute | solution.py:624
  145.0 19.3 %collective-permute-start.9 = (f32[4,4,128,128]{3,2,1,0:T(8,128)}, f32[4,4,128,128]{3,2,1,0:T(8,128)S(1)}, u32[]{:S(2)}, u32[]{:S(2)}) collective-permute-start(f32[4,4,128,128]{3,2,1,0:T(8,128)} %get-tuple-element.126), channel_id=1, source_target_pairs={{0,1},{1,0},{2,3},{3,2},{4,5},{5,4},{6,7},{7,6},{8,9},{9,8},{10,11... | collective-permute-start | bytes 3145736 | tf_op jit(solution)/shard_map/ppermute | solution.py:628
  151.1 16.5 %copy-start = (f32[4,4,128,128]{3,2,1,0:T(8,128)S(1)}, f32[4,4,128,128]{3,2,1,0:T(8,128)}, u32[]{:S(2)}) copy-start(f32[4,4,128,128]{3,2,1,0:T(8,128)} %get-tuple-element.127) | copy-start | bytes 3145732
  156.7 6.7 %collective-permute-start.8 = (f32[256,128]{1,0:T(8,128)S(1)}, f32[256,128]{1,0:T(8,128)S(1)}, u32[]{:S(2)}, u32[]{:S(2)}) collective-permute-start(f32[256,128]{1,0:T(8,128)S(1)} %dynamic-slice_bitcast_fusion), channel_id=1, source_target_pairs={{0,1},{1,0},{2,3},{3,2},{4,5},{5,4},{6,7},{7,6},{8,9},{9,8},{10,11... | collective-permute-start | bytes 393224 | tf_op jit(solution)/shard_map/ppermute | solution.py:628
  157.1 10.6 %collective-permute-start.5 = (f32[128,128]{1,0:T(8,128)S(1)}, f32[128,128]{1,0:T(8,128)S(1)}, u32[]{:S(2)}, u32[]{:S(2)}) collective-permute-start(f32[128,128]{1,0:T(8,128)S(1)} %get-tuple-element.142), channel_id=1, source_target_pairs={{0,16},{1,17},{2,18},{3,19},{4,20},{5,21},{6,22},{7,23},{8,24},{9,... | collective-permute-start | bytes 196616 | tf_op jit(solution)/shard_map/ppermute | solution.py:624
  160.1 7.7 %collective-permute-start.6 = (f32[128,128]{1,0:T(8,128)S(1)}, f32[128,128]{1,0:T(8,128)S(1)}, u32[]{:S(2)}, u32[]{:S(2)}) collective-permute-start(f32[128,128]{1,0:T(8,128)S(1)} %get-tuple-element.141), channel_id=1, source_target_pairs={{0,8},{1,9},{2,10},{3,11},{4,12},{5,13},{6,14},{7,15},{8,16},{9,17... | collective-permute-start | bytes 196616 | tf_op jit(solution)/shard_map/ppermute | solution.py:624
  160.8 9.2 %collective-permute-start.7 = (f32[128,128]{1,0:T(8,128)S(1)}, f32[128,128]{1,0:T(8,128)S(1)}, u32[]{:S(2)}, u32[]{:S(2)}) collective-permute-start(f32[128,128]{1,0:T(8,128)S(1)} %get-tuple-element.140), channel_id=1, source_target_pairs={{0,24},{1,25},{2,26},{3,27},{4,28},{5,29},{6,30},{7,31},{8,0},{9,1... | collective-permute-start | bytes 196616 | tf_op jit(solution)/shard_map/ppermute | solution.py:624
  164.3 7.1 %collective-permute-start.20 = (f32[256,128]{1,0:T(8,128)S(1)}, f32[256,128]{1,0:T(8,128)S(1)}, u32[]{:S(2)}, u32[]{:S(2)}) collective-permute-start(f32[256,128]{1,0:T(8,128)S(1)} %bitcast_add_fusion.2), channel_id=1, source_target_pairs={{0,8},{1,9},{2,10},{3,11},{4,12},{5,13},{6,14},{7,15},{8,16},{9,17... | collective-permute-start | bytes 393224 | tf_op jit(solution)/shard_map/ppermute | solution.py:613
  164.4 8.8 %collective-permute-start.21 = (f32[256,128]{1,0:T(8,128)S(1)}, f32[256,128]{1,0:T(8,128)S(1)}, u32[]{:S(2)}, u32[]{:S(2)}) collective-permute-start(f32[256,128]{1,0:T(8,128)S(1)} %bitcast_add_fusion.2), channel_id=1, source_target_pairs={{0,24},{1,25},{2,26},{3,27},{4,28},{5,29},{6,30},{7,31},{8,0},{9,1... | collective-permute-start | bytes 393224 | tf_op jit(solution)/shard_map/ppermute | solution.py:613
  167.7 6.6 %collective-permute-start.19 = (f32[256,128]{1,0:T(8,128)S(1)}, f32[256,128]{1,0:T(8,128)S(1)}, u32[]{:S(2)}, u32[]{:S(2)}) collective-permute-start(f32[256,128]{1,0:T(8,128)S(1)} %bitcast_add_fusion.2), channel_id=1, source_target_pairs={{0,16},{1,17},{2,18},{3,19},{4,20},{5,21},{6,22},{7,23},{8,24},{9,... | collective-permute-start | bytes 393224 | tf_op jit(solution)/shard_map/ppermute | solution.py:613
  167.8 10.9 %collective-permute-start.10 = (f32[4,128,128]{2,1,0:T(8,128)S(1)}, f32[4,128,128]{2,1,0:T(8,128)S(1)}, u32[]{:S(2)}, u32[]{:S(2)}) collective-permute-start(f32[4,128,128]{2,1,0:T(8,128)S(1)} %get-tuple-element.134), channel_id=1, source_target_pairs={{0,4},{1,5},{2,6},{3,7},{4,0},{5,1},{6,2},{7,3},{8,12},{9,13},{10,... | collective-permute-start | bytes 786440 | tf_op jit(solution)/shard_map/ppermute | solution.py:624
  170.0 12.3 %collective-permute-start.11 = (f32[4,128,128]{2,1,0:T(8,128)S(1)}, f32[4,128,128]{2,1,0:T(8,128)S(1)}, u32[]{:S(2)}, u32[]{:S(2)}) collective-permute-start(f32[4,128,128]{2,1,0:T(8,128)S(1)} %get-tuple-element.133), channel_id=1, source_target_pairs={{0,2},{1,3},{2,4},{3,5},{4,6},{5,7},{6,0},{7,1},{8,10},{9,11},{10,... | collective-permute-start | bytes 786440 | tf_op jit(solution)/shard_map/ppermute | solution.py:624
  171.4 10.9 %collective-permute-start.12 = (f32[4,128,128]{2,1,0:T(8,128)S(1)}, f32[4,128,128]{2,1,0:T(8,128)S(1)}, u32[]{:S(2)}, u32[]{:S(2)}) collective-permute-start(f32[4,128,128]{2,1,0:T(8,128)S(1)} %get-tuple-element.132), channel_id=1, source_target_pairs={{0,6},{1,7},{2,0},{3,1},{4,2},{5,3},{6,4},{7,5},{8,14},{9,15},{10,... | collective-permute-start | bytes 786440 | tf_op jit(solution)/shard_map/ppermute | solution.py:624
  174.3 11.3 %collective-permute-start.23 = (f32[256,128]{1,0:T(8,128)S(1)}, f32[256,128]{1,0:T(8,128)S(1)}, u32[]{:S(2)}, u32[]{:S(2)}) collective-permute-start(f32[256,128]{1,0:T(8,128)S(1)} %add_add_fusion.2), channel_id=1, source_target_pairs={{0,32},{32,64},{64,96},{96,0},{1,33},{33,65},{65,97},{97,1},{2,34}... | collective-permute-start | bytes 393224 | tf_op jit(solution)/shard_map/ppermute | solution.py:613
  175.9 12.9 %collective-permute-start.24 = (f32[256,128]{1,0:T(8,128)S(1)}, f32[256,128]{1,0:T(8,128)S(1)}, u32[]{:S(2)}, u32[]{:S(2)}) collective-permute-start(f32[256,128]{1,0:T(8,128)S(1)} %add_add_fusion.2), channel_id=1, source_target_pairs={{0,96},{32,0},{64,32},{96,64},{1,97},{33,1},{65,33},{97,65},{2,98}... | collective-permute-start | bytes 393224 | tf_op jit(solution)/shard_map/ppermute | solution.py:613
  178.7 10.2 %collective-permute-start.22 = (f32[256,128]{1,0:T(8,128)S(1)}, f32[256,128]{1,0:T(8,128)S(1)}, u32[]{:S(2)}, u32[]{:S(2)}) collective-permute-start(f32[256,128]{1,0:T(8,128)S(1)} %add_add_fusion.2), channel_id=1, source_target_pairs={{0,64},{32,96},{64,0},{96,32},{1,65},{33,97},{65,1},{97,33},{2,66}... | collective-permute-start | bytes 393224 | tf_op jit(solution)/shard_map/ppermute | solution.py:613
  182.4 9.8 %collective-permute-start.13 = (f32[128,128]{1,0:T(8,128)S(1)}, f32[128,128]{1,0:T(8,128)S(1)}, u32[]{:S(2)}, u32[]{:S(2)}) collective-permute-start(f32[128,128]{1,0:T(8,128)S(1)} %get-tuple-element.145), channel_id=1, source_target_pairs={{0,16},{1,17},{2,18},{3,19},{4,20},{5,21},{6,22},{7,23},{8,24},{9,... | collective-permute-start | bytes 196616 | tf_op jit(solution)/shard_map/ppermute | solution.py:624
  185.6 7.5 %collective-permute-start.14 = (f32[128,128]{1,0:T(8,128)S(1)}, f32[128,128]{1,0:T(8,128)S(1)}, u32[]{:S(2)}, u32[]{:S(2)}) collective-permute-start(f32[128,128]{1,0:T(8,128)S(1)} %get-tuple-element.144), channel_id=1, source_target_pairs={{0,8},{1,9},{2,10},{3,11},{4,12},{5,13},{6,14},{7,15},{8,16},{9,17... | collective-permute-start | bytes 196616 | tf_op jit(solution)/shard_map/ppermute | solution.py:624
  185.6 7.5 %collective-permute-start.15 = (f32[128,128]{1,0:T(8,128)S(1)}, f32[128,128]{1,0:T(8,128)S(1)}, u32[]{:S(2)}, u32[]{:S(2)}) collective-permute-start(f32[128,128]{1,0:T(8,128)S(1)} %get-tuple-element.143), channel_id=1, source_target_pairs={{0,24},{1,25},{2,26},{3,27},{4,28},{5,29},{6,30},{7,31},{8,0},{9,1... | collective-permute-start | bytes 196616 | tf_op jit(solution)/shard_map/ppermute | solution.py:624
  188.9 7.6 %collective-permute-start.26 = (f32[256,128]{1,0:T(8,128)S(1)}, f32[256,128]{1,0:T(8,128)S(1)}, u32[]{:S(2)}, u32[]{:S(2)}) collective-permute-start(f32[256,128]{1,0:T(8,128)S(1)} %add_add_fusion.1), channel_id=1, source_target_pairs={{0,2},{1,3},{2,4},{3,5},{4,6},{5,7},{6,0},{7,1},{8,10},{9,11},{10,... | collective-permute-start | bytes 393224 | tf_op jit(solution)/shard_map/ppermute | solution.py:613
  190.4 8.4 %collective-permute-start.27 = (f32[256,128]{1,0:T(8,128)S(1)}, f32[256,128]{1,0:T(8,128)S(1)}, u32[]{:S(2)}, u32[]{:S(2)}) collective-permute-start(f32[256,128]{1,0:T(8,128)S(1)} %add_add_fusion.1), channel_id=1, source_target_pairs={{0,6},{1,7},{2,0},{3,1},{4,2},{5,3},{6,4},{7,5},{8,14},{9,15},{10,... | collective-permute-start | bytes 393224 | tf_op jit(solution)/shard_map/ppermute | solution.py:613
  192.2 6.6 %collective-permute-start.25 = (f32[256,128]{1,0:T(8,128)S(1)}, f32[256,128]{1,0:T(8,128)S(1)}, u32[]{:S(2)}, u32[]{:S(2)}) collective-permute-start(f32[256,128]{1,0:T(8,128)S(1)} %add_add_fusion.1), channel_id=1, source_target_pairs={{0,4},{1,5},{2,6},{3,7},{4,0},{5,1},{6,2},{7,3},{8,12},{9,13},{10,... | collective-permute-start | bytes 393224 | tf_op jit(solution)/shard_map/ppermute | solution.py:613
  193.1 7.7 %collective-permute-start.17 = (f32[2,128,128]{2,1,0:T(8,128)S(1)}, f32[2,128,128]{2,1,0:T(8,128)S(1)}, u32[]{:S(2)}, u32[]{:S(2)}) collective-permute-start(f32[2,128,128]{2,1,0:T(8,128)S(1)} %pad_maximum_fusion.4), channel_id=1, source_target_pairs={{0,32},{32,64},{64,96},{96,0},{1,33},{33,65},{65,97},{97,1},{2,34}... | collective-permute-start | bytes 393224 | tf_op jit(solution)/shard_map/ppermute | solution.py:613
  194.8 6.0 %collective-permute-start.18 = (f32[2,128,128]{2,1,0:T(8,128)S(1)}, f32[2,128,128]{2,1,0:T(8,128)S(1)}, u32[]{:S(2)}, u32[]{:S(2)}) collective-permute-start(f32[2,128,128]{2,1,0:T(8,128)S(1)} %pad_maximum_fusion.4), channel_id=1, source_target_pairs={{0,96},{32,0},{64,32},{96,64},{1,97},{33,1},{65,33},{97,65},{2,98}... | collective-permute-start | bytes 393224 | tf_op jit(solution)/shard_map/ppermute | solution.py:613
  196.5 6.5 %collective-permute-start.16 = (f32[2,128,128]{2,1,0:T(8,128)S(1)}, f32[2,128,128]{2,1,0:T(8,128)S(1)}, u32[]{:S(2)}, u32[]{:S(2)}) collective-permute-start(f32[2,128,128]{2,1,0:T(8,128)S(1)} %pad_maximum_fusion.4), channel_id=1, source_target_pairs={{0,64},{32,96},{64,0},{96,32},{1,65},{33,97},{65,1},{97,33},{2,66}... | collective-permute-start | bytes 393224 | tf_op jit(solution)/shard_map/ppermute | solution.py:613
  198.8 4.9 %collective-permute-start.28 = (f32[256,128]{1,0:T(8,128)S(1)}, f32[256,128]{1,0:T(8,128)S(1)}, u32[]{:S(2)}, u32[]{:S(2)}) collective-permute-start(f32[256,128]{1,0:T(8,128)S(1)} %add_add_fusion), channel_id=1, source_target_pairs={{0,1},{1,0},{2,3},{3,2},{4,5},{5,4},{6,7},{7,6},{8,9},{9,8},{10,11... | collective-permute-start | bytes 393224 | tf_op jit(solution)/shard_map/ppermute | solution.py:663
